TPU v7x, 32 devices: a whole 2x2x4 slice. The times are simulated.
32 devices in a mesh: shard: 2 (over x), context: 4 (over z), tensor: 4 (over y, core).
Axes of the slice: x: 2, y: 2, z: 4, core: 2. Of those that a mesh axis runs over, the one named last changes fastest.
Arguments:
- tokens: bfloat16 [10240, 1088], P(('shard', 'context', 'tensor')), may hold values from -6 to 6
- cotangent: bfloat16 [10240, 1088], P(('shard', 'context', 'tensor')), may hold values from -6 to 6
- segment_of: int32 [10240], P('shard'), may hold values from 0 to 51, as said below
- position_of: int32 [10240], P('shard'), may hold values from 0 to 1279, as said below
- parent: int32 [52], replicated, may hold values from -1 to 51, as said below
- ln1_gain: bfloat16 [1088], P('shard'), may hold values from 0.099609375 to 1.8984375
- ln1_bias: bfloat16 [1088], P('shard'), may hold values from -4 to 4
- w_qkv: bfloat16 [1088, 3264], P('shard'), may hold values from -0.25 to 0.25
- b_query: bfloat16 [1088], P('shard'), may hold values from -4 to 4
- b_value: bfloat16 [1088], P('shard'), may hold values from -4 to 4
- w_out: bfloat16 [1088, 1088], P('shard'), may hold values from -3 to 3
- b_out: bfloat16 [1088], P('shard'), may hold values from -4 to 4
- ln2_gain: bfloat16 [1088], P('shard'), may hold values from 0.099609375 to 1.8984375
- ln2_bias: bfloat16 [1088], P('shard'), may hold values from -4 to 4
- w_fc: bfloat16 [1088, 4352], P('shard', 'tensor'), may hold values from -0.1875 to 0.1875
- b_fc: bfloat16 [4352], P('tensor'), may hold values from -4 to 4
- w_proj: bfloat16 [4352, 1088], P('tensor', 'shard'), may hold values from -0.09375 to 0.09375
- b_proj: bfloat16 [1088], P('shard'), may hold values from -4 to 4
Outputs:
- out: bfloat16 [10240, 1088], P(('shard', 'context', 'tensor'))
- d_tokens: float32 [10240, 1088], P(('shard', 'context', 'tensor'))
- grad_ln1_gain: float32 [1088], P('shard')
- grad_ln1_bias: float32 [1088], P('shard')
- grad_w_qkv: float32 [1088, 3264], P('shard')
- grad_b_query: float32 [1088], P('shard')
- grad_b_value: float32 [1088], P('shard')
- grad_w_out: float32 [1088, 1088], P('shard')
- grad_b_out: float32 [1088], P('shard')
- grad_ln2_gain: float32 [1088], P('shard')
- grad_ln2_bias: float32 [1088], P('shard')
- grad_w_fc: float32 [1088, 4352], P('shard', 'tensor')
- grad_b_fc: float32 [4352], P('tensor')
- grad_w_proj: float32 [4352, 1088], P('tensor', 'shard')
- grad_b_proj: float32 [1088], P('shard')
Inputs may be any that keep to these rules, and one draw needn't show every extreme that they name: Tree i holds rows i * 2560 to (i + 1) * 2560 - 1 and segments of its own: a trunk of 1024 tokens (parent -1), 4 branches whose parent is the trunk, and 2 leaves on each branch; branches and leaves have 128 tokens. Segment numbers are a permutation within each tree's block of 13 consecutive numbers, and the trunk has the block's last number. `segment_of`: A tree's rows are its 20 pieces of 128 aligned rows (the trunk's 8 pieces and one piece for every other segment) in any order. `position_of`: trunk tokens have positions 0 to 1023, a branch's continue from 1024, a leaf's from (9) * 128; within a piece positions rise by one.
All inputs are finite; a program needn't handle non-finite values.
Results may differ from a plain program's by a relative error of at most 0.012.
The roundings to bfloat16 on the way count: a program that leaves them out, or rounds other values in their place, can miss the bound.
Values may be sent and summed in bfloat16 or wider, within the bound.
A program may use at most 192 MiB of HBM per device.

v0:
```python
import jax
import jax.numpy as jnp
from jax import lax
from jax.sharding import PartitionSpec as P

HEAD_DIM = 64


EPSILON = 1e-05
NEGATIVE = -1e30


def partner(value, axis, stride):
    return lax.ppermute(value, axis, [(i, i ^ 1 << stride) for i in range(lax.axis_size(axis))])


def layer_norm(inputs, gain, shift):
    average = jnp.mean(inputs, axis=-1, keepdims=True)
    centered = inputs - average
    spread = jnp.mean(centered * centered, axis=-1, keepdims=True)
    return centered * lax.rsqrt(spread + EPSILON) * gain + shift


def contract(left, right, left_dim, right_dim):
    return lax.dot_general(
        left, right, (((left_dim,), (right_dim,)), ((), ())), preferred_element_type=jnp.float32
    )


def parent_lookup(identities, shifted_table):
    labels = jnp.arange(shifted_table.shape[0], dtype=jnp.int32)
    matches = identities[:, None] == labels[None, :]
    return jnp.sum(jnp.where(matches, shifted_table[None, :], 0), axis=1) - 1


def gelu_exact(inputs):
    return jax.nn.gelu(inputs, approximate=False)


def local(
    tokens,
    cotangent,
    segment_of,
    position_of,
    parent,
    ln1_gain,
    ln1_bias,
    w_qkv,
    b_query,
    b_value,
    w_out,
    b_out,
    ln2_gain,
    ln2_bias,
    w_fc,
    b_fc,
    w_proj,
    b_proj,
):
    row_count = tokens.shape[0]
    feature_dim = tokens.shape[1]
    group_size = lax.axis_size("tensor")
    half_rows = group_size * row_count
    tree_rows = 2 * half_rows
    head_count = feature_dim // HEAD_DIM
    score_scale = HEAD_DIM ** (-0.5)
    gathered = (
        lax.all_gather(ln1_gain, "shard", axis=0, tiled=True),
        lax.all_gather(ln1_bias, "shard", axis=0, tiled=True),
        lax.all_gather(w_qkv, "shard", axis=0, tiled=True),
        lax.all_gather(b_query, "shard", axis=0, tiled=True),
        lax.all_gather(b_value, "shard", axis=0, tiled=True),
        lax.all_gather(w_out, "shard", axis=0, tiled=True),
        lax.all_gather(b_out, "shard", axis=0, tiled=True),
        lax.all_gather(ln2_gain, "shard", axis=0, tiled=True),
        lax.all_gather(ln2_bias, "shard", axis=0, tiled=True),
        lax.all_gather(w_fc, "shard", axis=0, tiled=True),
        lax.all_gather(w_proj, "shard", axis=1, tiled=True),
        lax.all_gather(b_proj, "shard", axis=0, tiled=True),
    )
    (
        gain_one,
        shift_one,
        mixer,
        bias_query,
        bias_value,
        out_weight,
        bias_out,
        gain_two,
        shift_two,
        fc_weight,
        proj_weight,
        bias_proj,
    ) = gathered
    gain_one = gain_one.astype(jnp.float32)
    shift_one = shift_one.astype(jnp.float32)
    bias_query = bias_query.astype(jnp.float32)
    bias_value = bias_value.astype(jnp.float32)
    bias_out = bias_out.astype(jnp.float32)
    gain_two = gain_two.astype(jnp.float32)
    shift_two = shift_two.astype(jnp.float32)
    bias_proj = bias_proj.astype(jnp.float32)
    bias_fc = b_fc.astype(jnp.float32)
    context_id = lax.axis_index("context")
    tensor_id = lax.axis_index("tensor")
    partner_id = context_id + 1 - 2 * (context_id % 2)
    own_start = context_id * half_rows
    partner_start = partner_id * half_rows
    query_start = own_start + tensor_id * row_count
    query_segments = lax.dynamic_slice_in_dim(segment_of, query_start, row_count)
    query_places = lax.dynamic_slice_in_dim(position_of, query_start, row_count)
    key_segments = jnp.concatenate(
        [
            lax.dynamic_slice_in_dim(segment_of, own_start, half_rows),
            lax.dynamic_slice_in_dim(segment_of, partner_start, half_rows),
        ]
    )
    key_places = jnp.concatenate(
        [
            lax.dynamic_slice_in_dim(position_of, own_start, half_rows),
            lax.dynamic_slice_in_dim(position_of, partner_start, half_rows),
        ]
    )
    shifted_table = parent + 1
    first_up = parent_lookup(query_segments, shifted_table)
    second_up = parent_lookup(first_up, shifted_table)
    related = (
        (key_segments[None, :] == query_segments[:, None])
        | (key_segments[None, :] == first_up[:, None])
        | (key_segments[None, :] == second_up[:, None])
    )
    allowed = related & (key_places[None, :] <= query_places[:, None])
    inputs = tokens.astype(jnp.float32)
    normed_f, norm_one_pull = jax.vjp(layer_norm, inputs, gain_one, shift_one)
    normed = normed_f.astype(jnp.bfloat16)
    mixed = contract(mixer, normed, 0, 1)
    query_t = ((mixed[:feature_dim] + bias_query[:, None]) * score_scale).astype(jnp.bfloat16)
    kv_bias = jnp.concatenate([jnp.zeros((feature_dim,), jnp.float32), bias_value])
    kv_t = (mixed[feature_dim:] + kv_bias[:, None]).astype(jnp.bfloat16)
    group_kv = lax.all_gather(kv_t, "tensor", axis=1, tiled=True)
    partner_kv = partner(group_kv, "context", 0)
    tree_kv = jnp.concatenate([group_kv, partner_kv], axis=1)
    key_heads = tree_kv[:feature_dim].reshape(head_count, HEAD_DIM, tree_rows)
    value_heads = tree_kv[feature_dim:].reshape(head_count, HEAD_DIM, tree_rows)
    query_heads = query_t.reshape(head_count, HEAD_DIM, row_count)

    def forward_head(carry, operands):
        head_query, head_keys, head_values = operands
        scores = jnp.where(allowed, contract(head_query, head_keys, 0, 0), NEGATIVE)
        largest = jnp.max(scores, axis=1, keepdims=True)
        raised = jnp.exp(scores - largest)
        totals = jnp.sum(raised, axis=1, keepdims=True)
        weights = (raised / totals).astype(jnp.bfloat16)
        head_out = contract(head_values, weights, 1, 1)
        return (carry, (head_out, largest[:, 0], totals[:, 0]))

    _, (out_heads, largest_all, totals_all) = lax.scan(
        forward_head, 0, (query_heads, key_heads, value_heads)
    )
    attended_t = out_heads.reshape(feature_dim, row_count).astype(jnp.bfloat16)
    middle = inputs + contract(attended_t, out_weight, 0, 0) + bias_out
    normed_two_f, norm_two_pull = jax.vjp(layer_norm, middle, gain_two, shift_two)
    normed_two = normed_two_f.astype(jnp.bfloat16)
    group_rows = lax.all_gather(normed_two, "tensor", axis=0, tiled=True)
    before = jnp.dot(group_rows, fc_weight, preferred_element_type=jnp.float32) + bias_fc
    hidden_f, gelu_pull = jax.vjp(gelu_exact, before)
    hidden = hidden_f.astype(jnp.bfloat16)
    piece = hidden
    mlp_out = lax.psum_scatter(
        jnp.dot(piece, proj_weight, preferred_element_type=jnp.float32).astype(jnp.bfloat16),
        "tensor",
        scatter_dimension=0,
        tiled=True,
    ).astype(jnp.float32)
    output = (middle + mlp_out + bias_proj).astype(jnp.bfloat16)
    grad_rows_all = lax.all_gather(cotangent, "tensor", axis=0, tiled=True)
    d_hidden = contract(grad_rows_all, proj_weight, 1, 1)
    d_before = gelu_pull(d_hidden)[0].astype(jnp.bfloat16)
    grad_proj = contract(hidden, grad_rows_all, 0, 0)
    grad_fc = contract(group_rows, d_before, 0, 0)
    grad_bias_fc = jnp.sum(d_before, axis=0, dtype=jnp.float32)
    piece = d_before
    d_normed_two = lax.psum_scatter(
        contract(piece, fc_weight, 1, 1), "tensor", scatter_dimension=0, tiled=True
    )
    d_middle, grad_gain_two, grad_shift_two = norm_two_pull(d_normed_two)
    d_middle = d_middle + cotangent.astype(jnp.float32)
    grad_bias_proj = jnp.sum(cotangent, axis=0, dtype=jnp.float32)
    d_attn = d_middle.astype(jnp.bfloat16)
    grad_bias_out = jnp.sum(d_attn, axis=0, dtype=jnp.float32)
    grad_out = contract(attended_t, d_attn, 1, 0)
    d_attended_t = contract(out_weight, d_attn, 1, 1).astype(jnp.bfloat16)
    d_out_heads = d_attended_t.reshape(head_count, HEAD_DIM, row_count)

    def backward_head(carry, operands):
        head_query, head_keys, head_values, head_grad, largest, totals = operands
        scores = jnp.where(allowed, contract(head_query, head_keys, 0, 0), NEGATIVE)
        probs = jnp.exp(scores - largest[:, None]) / totals[:, None]
        weights = probs.astype(jnp.bfloat16)
        d_probs = contract(head_grad, head_values, 0, 0)
        delta = jnp.sum(probs * d_probs, axis=1, keepdims=True)
        d_scores = (probs * (d_probs - delta)).astype(jnp.bfloat16)
        d_values = contract(head_grad, weights, 1, 0)
        d_keys = contract(head_query, d_scores, 1, 0)
        d_query = contract(head_keys, d_scores, 1, 1)
        return (carry, (d_query, d_keys, d_values))

    _, (d_query_all, d_keys_all, d_values_all) = lax.scan(
        backward_head,
        0,
        (query_heads, key_heads, value_heads, d_out_heads, largest_all, totals_all),
    )
    d_query_t = (d_query_all.reshape(feature_dim, row_count) * score_scale).astype(jnp.bfloat16)
    d_tree_kv = jnp.concatenate(
        [d_keys_all.reshape(feature_dim, tree_rows), d_values_all.reshape(feature_dim, tree_rows)],
        axis=0,
    )
    returned = partner(d_tree_kv[:, half_rows:].astype(jnp.bfloat16), "context", 0).astype(
        jnp.float32
    )
    group_sum = d_tree_kv[:, :half_rows] + returned
    d_kv_own = lax.psum_scatter(group_sum, "tensor", scatter_dimension=1, tiled=True)
    d_kv_low = d_kv_own.astype(jnp.bfloat16)
    d_mixed_t = jnp.concatenate([d_query_t, d_kv_low], axis=0)
    grad_mixer = contract(normed, d_mixed_t, 0, 1)
    grad_bias_query = jnp.sum(d_query_t, axis=1, dtype=jnp.float32)
    grad_bias_value = jnp.sum(d_kv_low[feature_dim:], axis=1, dtype=jnp.float32)
    d_normed = contract(d_mixed_t, mixer, 0, 1)
    d_inputs, grad_gain_one, grad_shift_one = norm_one_pull(d_normed)
    d_inputs = d_inputs + d_middle
    owned = (
        lax.psum_scatter(grad_gain_one, "shard", scatter_dimension=0, tiled=True),
        lax.psum_scatter(grad_shift_one, "shard", scatter_dimension=0, tiled=True),
        lax.psum_scatter(grad_mixer, "shard", scatter_dimension=0, tiled=True),
        lax.psum_scatter(grad_bias_query, "shard", scatter_dimension=0, tiled=True),
        lax.psum_scatter(grad_bias_value, "shard", scatter_dimension=0, tiled=True),
        lax.psum_scatter(grad_out, "shard", scatter_dimension=0, tiled=True),
        lax.psum_scatter(grad_bias_out, "shard", scatter_dimension=0, tiled=True),
        lax.psum_scatter(grad_gain_two, "shard", scatter_dimension=0, tiled=True),
        lax.psum_scatter(grad_shift_two, "shard", scatter_dimension=0, tiled=True),
        lax.psum_scatter(grad_bias_proj, "shard", scatter_dimension=0, tiled=True),
    )
    summed = lax.psum(
        (
            owned[0],
            owned[1],
            owned[2],
            owned[3],
            owned[4],
            owned[5],
            owned[6],
            owned[7],
            owned[8],
            owned[9],
        ),
        ("context", "tensor"),
    )
    (
        sum_gain_one,
        sum_shift_one,
        sum_mixer,
        sum_bias_query,
        sum_bias_value,
        sum_out,
        sum_bias_out,
        sum_gain_two,
        sum_shift_two,
        sum_bias_proj,
    ) = summed
    mlp_total = lax.psum((grad_fc, grad_proj, grad_bias_fc), ("shard", "context"))
    shard_id = lax.axis_index("shard")
    owner_rows = feature_dim // lax.axis_size("shard")
    owner_start = shard_id * owner_rows
    own_fc = lax.dynamic_slice_in_dim(mlp_total[0], owner_start, owner_rows, 0)
    own_proj = lax.dynamic_slice_in_dim(mlp_total[1], owner_start, owner_rows, 1)
    return (
        output,
        d_inputs,
        sum_gain_one,
        sum_shift_one,
        sum_mixer,
        sum_bias_query,
        sum_bias_value,
        sum_out,
        sum_bias_out,
        sum_gain_two,
        sum_shift_two,
        own_fc,
        mlp_total[2],
        own_proj,
        sum_bias_proj,
    )


def solution(mesh):
    return jax.shard_map(
        local,
        mesh=mesh,
        in_specs=(
            P(("shard", "context", "tensor"), None),
            P(("shard", "context", "tensor"), None),
            P("shard"),
            P("shard"),
            P(),
            P("shard"),
            P("shard"),
            P("shard", None),
            P("shard"),
            P("shard"),
            P("shard", None),
            P("shard"),
            P("shard"),
            P("shard"),
            P("shard", "tensor"),
            P("tensor"),
            P("tensor", "shard"),
            P("shard"),
        ),
        out_specs=(
            P(("shard", "context", "tensor"), None),
            P(("shard", "context", "tensor"), None),
            P("shard"),
            P("shard"),
            P("shard", None),
            P("shard"),
            P("shard"),
            P("shard", None),
            P("shard"),
            P("shard"),
            P("shard"),
            P("shard", "tensor"),
            P("tensor"),
            P("tensor", "shard"),
            P("shard"),
        ),
        check_vma=False,
    )
```

profile of v0, /device:TPU:0, one launch (start us, length us, event | category | flops | bytes accessed | tf_op | source)
XLA Modules:
  0.0 1795.3 jit_solution(7301513870068671859)
XLA Ops:
  11.3 10.0 all-reduce.21
  22.6 80.9 %all-gather.8.cloned.1.call-done = bf16[1088,3264]{1,0:T(8,128)(2,1)} async-done(((bf16[544,3264]{1,0:T(8,128)(2,1)}), bf16[1088,3264]{1,0:T(8,128)(2,1)}) %all-gather.8.cloned.1.call-update) | async-done | bytes 7102480 | tf_op jit(solution)/shard_map/all_gather | solution.py:70
  103.5 5.7 convolution_bitcast_fusion.3
  113.2 42.4 %all-gather.10.cloned.1.call-done = bf16[2176,1280]{0,1:T(8,128)(2,1)} async-done(((bf16[2176,320]{0,1:T(8,128)(2,1)}), bf16[2176,1280]{0,1:T(8,128)(2,1)}) %all-gather.10.cloned.1.call-update) | async-done | bytes 5570576 | tf_op jit(solution)/shard_map/all_gather | solution.py:140
  161.4 3.3 constant_dynamic-update-slice_fusion.1
  164.8 113.4 %collective-permute-done = bf16[2176,1280]{0,1:T(8,128)(2,1)} collective-permute-done((bf16[2176,1280]{0,1:T(8,128)(2,1)}, bf16[2176,1280]{0,1:T(8,128)(2,1)}, u32[]{:S(2)}, u32[]{:S(2)}) %collective-permute-start) | collective-permute-done | bytes 5570592 | tf_op jit(solution)/shard_map/ppermute | solution.py:14
  278.1 3.4 constant_dynamic-update-slice_fusion
  281.5 5.8 fusion.85
  287.3 8.8 copy.48
  296.1 8.8 copy.50
  304.9 82.0 %while.32 = (s32[]{:T(128)}, bf16[17,64,320]{2,1,0:T(8,128)(2,1)S(1)}, f32[17,320]{1,0:T(8,128)S(1)}, f32[17,320]{1,0:T(8,128)S(1)}, bf16[17,64,2560]{2,1,0:T(8,...) while((s32[]{:T(128)}, ...), condition=%wide.region_7.8_spmd.clone.clone, body=%wide.region_4.7_spmd.clone.sunk.clone | while | flops 221183360 | bytes 10679173 | solution.py:157
  314.5 2.3 fusion.151
  319.4 2.3 fusion.151
  386.9 3.4 fusion.89
  393.8 25.6 %all-gather.14.cloned.1.call-done = bf16[1280,1088]{1,0:T(8,128)(2,1)} async-done(((bf16[320,1088]{1,0:T(8,128)(2,1)}), bf16[1280,1088]{1,0:T(8,128)(2,1)}) %all-gather.14.cloned.1.call-update) | async-done | bytes 2785296 | tf_op jit(solution)/shard_map/all_gather | solution.py:164
  419.5 9.0 convolution_add_fusion
  428.4 30.2 %all-gather.18.cloned.1.call-done = bf16[1088,1088]{0,1:T(8,128)(2,1)} async-done(((bf16[1088,544]{0,1:T(8,128)(2,1)}), bf16[1088,1088]{0,1:T(8,128)(2,1)}) %all-gather.18.cloned.1.call-update) | async-done | bytes 2367504 | tf_op jit(solution)/shard_map/all_gather | solution.py:78
  458.6 29.0 %all-gather.20.cloned.1.call-done = bf16[1280,1088]{1,0:T(8,128)(2,1)} async-done(((bf16[320,1088]{1,0:T(8,128)(2,1)}), bf16[1280,1088]{1,0:T(8,128)(2,1)}) %all-gather.20.cloned.1.call-update) | async-done | bytes 2785296 | tf_op jit(solution)/shard_map/all_gather | solution.py:176
  487.6 21.5 %convert_reduce_fusion = (f32[1088]{0:T(1024)S(1)}, bf16[1280,1088]{0,1:T(8,128)(2,1)S(1)}, f32[1280,1088]{0,1:T(8,128)}) fusion(f32[1280,1088]{0,1:T(8,128)} %convolution_add_fusion, bf16[1280,1088]{1,0:T(8,128)(2,1)} %all-gather.20.cloned.1.call-done, bf16[1088,1088]{0,1:T(8,128)(2,1)} %all-gather.18.cloned.1.call-done), kind=kOutput, calls=%fused_computation.65 | convolution fusion | flops 3133438976 | bytes 19083520 | tf_op jit(solution)/shard_map/dot_general | solution.py:25
  510.8 6.3 fusion.90
  517.4 5.1 multiply_convert_fusion.1
  524.0 5.9 convolution_convert_fusion
  530.0 43.1 %reduce-scatter.10.cloned.1.call-done = f32[320,1088]{1,0:T(8,128)} async-done(((f32[1280,1088]{1,0:T(8,128)}), f32[320,1088]{1,0:T(8,128)}) %reduce-scatter.10.cloned.1.call-update) | async-done | bytes 1392656 | tf_op jit(solution)/shard_map/reduce_scatter | solution.py:183
  575.0 37.5 %reduce-scatter.8.cloned.1.call-done = bf16[320,1088]{1,0:T(8,128)(2,1)} async-done(((bf16[1280,1088]{1,0:T(8,128)(2,1)}), bf16[320,1088]{1,0:T(8,128)(2,1)}) %reduce-scatter.8.cloned.1.call-update) | async-done | bytes 696336 | tf_op jit(solution)/shard_map/reduce_scatter | solution.py:169
  612.5 3.1 fusion.83
  618.8 175.3 %while.33 = (s32[]{:T(128)}, f32[17,64,320]{2,1,0:T(8,128)}, f32[17,64,2560]{2,1,0:T(8,128)}, f32[17,64,2560]{2,1,0:T(8,128)}, bf16[17,64,2560]{2,1,0:T(8,128)(2...) while((s32[]{:T(128)}, f32[17,64,320]{2,1,0:T(8,128)}, ...), condition=%wide.region_16.17_spmd.clone.clone, body=%wide.region_14.16_spmd.clone.sunk.clone | while | flops 537394880 | bytes 27205784 | solution.py:208
  620.4 2.7 multiply_reduce_fusion.6
  630.7 2.7 multiply_reduce_fusion.6
  641.0 2.7 multiply_reduce_fusion.6
  651.3 2.7 multiply_reduce_fusion.6
  661.7 2.7 multiply_reduce_fusion.6
  672.0 2.7 multiply_reduce_fusion.6
  682.3 2.7 multiply_reduce_fusion.6
  692.6 2.7 multiply_reduce_fusion.6
  702.9 2.7 multiply_reduce_fusion.6
  713.2 2.7 multiply_reduce_fusion.6
  723.6 2.7 multiply_reduce_fusion.6
  733.9 2.7 multiply_reduce_fusion.6
  744.2 2.7 multiply_reduce_fusion.6
  754.5 2.7 multiply_reduce_fusion.6
  764.8 2.7 multiply_reduce_fusion.6
  775.2 2.7 multiply_reduce_fusion.6
  785.4 2.7 multiply_reduce_fusion.6
  794.1 7.2 fusion.47
  802.9 120.5 %collective-permute-done.1 = bf16[2176,1280]{1,0:T(8,128)(2,1)S(1)} collective-permute-done((bf16[2176,1280]{1,0:T(8,128)(2,1)}, bf16[2176,1280]{1,0:T(8,128)(2,1)S(1)}, u32[]{:S(2)}, u32[]{:S(2)}) %collective-permute-start.1) | collective-permute-done | bytes 5570592 | tf_op jit(solution)/shard_map/ppermute | solution.py:14
  923.4 7.5 fusion.46
  930.9 12.7 copy.52
  944.7 3.8 fusion.91
  948.7 3.0 convert_reduce_fusion.4
  951.6 81.7 %reduce-scatter.16.cloned.1.call-done = f32[320,2176]{1,0:T(8,128)} async-done(((f32[1280,2176]{1,0:T(8,128)}), f32[320,2176]{1,0:T(8,128)}) %reduce-scatter.16.cloned.1.call-update) | async-done | bytes 2785296
  1033.3 3.5 copy.53
  1036.9 10.6 fusion.63
  1047.8 9.0 fusion.92
  1056.8 6.2 fusion.93
  1063.1 36.4 %reduce-scatter.14.cloned.1.call-done = f32[544,1088]{1,0:T(8,128)} async-done(((f32[1088,1088]{1,0:T(8,128)}), f32[544,1088]{1,0:T(8,128)}) %reduce-scatter.14.cloned.1.call-update) | async-done | bytes 2367504 | tf_op jit(solution)/shard_map/reduce_scatter | solution.py:237
  1099.5 167.3 %reduce-scatter.12.cloned.1.call-done = f32[544,3264]{1,0:T(8,128)} async-done(((f32[1088,3264]{1,0:T(8,128)}), f32[544,3264]{1,0:T(8,128)}) %reduce-scatter.12.cloned.1.call-update) | async-done | bytes 7102480 | tf_op jit(solution)/shard_map/reduce_scatter | solution.py:234
  1267.4 22.6 %psum.101 = f32[1088]{0:T(1024)} all-reduce(f32[1088]{0:T(1024)S(1)} %get-tuple-element.320), channel_id=1, replica_groups=mesh['shard'=2,'context'=4,'tensor'=4] {'shard','context'}, use_global_device_ids=true, to_apply=%region_47.48 | all-reduce | flops 1088 | bytes 8704 | tf_op jit(solution)/shard_map/psum | solution.py:270
  1289.9 296.1 %all-reduce.27.cloned.1.call-done = (f32[1088,1088]{1,0:T(8,128)}, f32[1088,1088]{0,1:T(8,128)}) async-done(((f32[1088,1088]{1,0:T(8,128)}, f32[1088,1088]{0,1:T(8,128)}), (f32[1088,1088]{1,0:T(8,128)}, f32[1088,1088]{0,1:T(8,128)})) %all-reduce.27.cloned.1.call-update) | async-done | bytes 9469968 | tf_op jit(solution)/shard_map/psum | solution.py:270
  1586.0 3.5 constant_dynamic-slice_fusion.2
  1591.7 8.1 fusion.80
  1602.3 8.5 all-reduce.20
  1611.4 61.6 %all-reduce.17 = (f32[544]{0:T(1024)}, f32[544]{0:T(1024)}, f32[544]{0:T(1024)}, f32[544]{0:T(1024)}, f32[544]{0:T(1024)}, /*index=5*/f32[544]{0:T(1024)}, f32[544]{0:T(1024)}, f32[544]{0:T(1024)}) all-reduce(f32[544]{0:T(1024)S(1)} %dynamic-slice.9, ...), channel_id=1, replica_groups=mesh['shard'=2,'context'=4,'tensor'=4] {'context','tensor'}, use_global_device_ids=true, to_apply=%region_22.23 | all-reduce | flops 4352 | bytes 34816 | tf_op jit(solution)/shard_map/psum | solution.py:243
  1673.0 107.2 %all-reduce.25.cloned.1.call-done = (f32[544,3264]{1,0:T(8,128)}, f32[544,1088]{1,0:T(8,128)}) async-done(((f32[544,3264]{1,0:T(8,128)}, f32[544,1088]{1,0:T(8,128)}), (f32[544,3264]{1,0:T(8,128)}, f32[544,1088]{1,0:T(8,128)})) %all-reduce.25.cloned.1.call-update) | async-done | bytes 9469968 | tf_op jit(solution)/shard_map/psum | solution.py:243
  1780.1 6.7 copy.97
  (406 shorter events, 241.2 us)
Async XLA Ops:
  7.2 0.9 copy-start.26
  7.2 2.2 copy-start.27
  7.2 2.4 copy-start.28
  7.2 2.6 copy-start.29
  7.2 2.9 copy-start.30
  7.2 3.1 copy-start.31
  7.2 3.3 copy-start.32
  7.3 3.6 copy-start.33
  7.3 3.8 copy-start.34
  7.3 14.1 copy-start
  7.3 96.2 %all-gather.8.cloned.1.call-start = ((), (), s32[]{:S(2)}) async-start(), calls=%async_computation.5 | async-start | bytes 10862592 | tf_op jit(solution)/shard_map/all_gather | solution.py:70
  8.0 147.6 %all-gather.10.cloned.1.call-start = ((), (), s32[]{:S(2)}) async-start(), calls=%async_computation.6 | async-start | bytes 6963200 | tf_op jit(solution)/shard_map/all_gather | solution.py:140
  21.3 87.9 %copy-start.13 = (f32[1088]{0:T(1024)}, f32[1088]{0:T(1024)S(1)}, u32[]{:S(2)}) copy-start(f32[1088]{0:T(1024)S(1)} %convert_element_type.111) | copy-start | bytes 13060
  21.3 87.9 %copy-start.15 = (f32[1088]{0:T(1024)}, f32[1088]{0:T(1024)S(1)}, u32[]{:S(2)}) copy-start(f32[1088]{0:T(1024)S(1)} %convert_element_type.112) | copy-start | bytes 13060
  21.6 87.6 %copy-start.17 = (f32[320]{0:T(512)}, f32[320]{0:T(512)S(1)}, u32[]{:S(2)}) copy-start(f32[320]{0:T(512)S(1)} %broadcast_multiply_fusion.1) | copy-start | bytes 3844
  22.0 0.6 copy-start.21
  22.6 86.6 %copy-start.19 = (f32[320]{0:T(512)}, f32[320]{0:T(512)S(1)}, u32[]{:S(2)}) copy-start(f32[320]{0:T(512)S(1)} %fusion.73) | copy-start | bytes 3844
  109.2 2.0 copy-start.7
  111.2 46.8 %copy-start.23 = (s32[5120]{0:T(1024)S(1)}, s32[5120]{0:T(1024)}, u32[]{:S(2)}) copy-start(s32[5120]{0:T(1024)} %param.24) | copy-start | bytes 61444
  111.2 46.9 %copy-start.24 = (s32[5120]{0:T(1024)S(1)}, s32[5120]{0:T(1024)}, u32[]{:S(2)}) copy-start(s32[5120]{0:T(1024)} %param.25) | copy-start | bytes 61444
  111.2 47.1 %copy-start.38 = (s32[52]{0:T(128)S(1)}, s32[52]{0:T(128)}, u32[]{:S(2)}) copy-start(s32[52]{0:T(128)} %param.26) | copy-start | bytes 628
  113.2 273.8 %all-gather.12.cloned.1.call-start = ((), (), s32[]{:S(2)}) async-start(), calls=%async_computation.7 | async-start | bytes 3760128 | tf_op jit(solution)/shard_map/all_gather | solution.py:73
  155.6 122.5 %collective-permute-start = (bf16[2176,1280]{0,1:T(8,128)(2,1)}, bf16[2176,1280]{0,1:T(8,128)(2,1)}, u32[]{:S(2)}, u32[]{:S(2)}) collective-permute-start(bf16[2176,1280]{0,1:T(8,128)(2,1)} %all-gather.10.cloned.1.call-done), channel_id=1, source_target_pairs={{0,4},{4,0},{8,12},{12,8},{1,5},{5,1},{9,13},{13,9},{2,6},{6,2},{1... | collective-permute-start | bytes 16711688 | tf_op jit(solution)/shard_map/ppermute | solution.py:14
  157.1 236.7 %all-gather.16.cloned.1.call-start = ((), (), s32[]{:S(2)}) async-start(), calls=%async_computation.9 | async-start | bytes 3760128 | tf_op jit(solution)/shard_map/all_gather | solution.py:77
  157.7 261.8 %all-gather.14.cloned.1.call-start = ((), (), s32[]{:S(2)}) async-start(), calls=%async_computation.8 | async-start | bytes 3686400 | tf_op jit(solution)/shard_map/all_gather | solution.py:164
  386.9 3.7 copy-start.4
  390.3 3.5 copy-start.25
  391.9 66.7 %all-gather.18.cloned.1.call-start = ((), (), s32[]{:S(2)}) async-start(), calls=%async_computation.10 | async-start | bytes 3760128 | tf_op jit(solution)/shard_map/all_gather | solution.py:78
  392.5 95.2 %all-gather.20.cloned.1.call-start = ((), (), s32[]{:S(2)}) async-start(), calls=%async_computation.12 | async-start | bytes 3686400 | tf_op jit(solution)/shard_map/all_gather | solution.py:176
  393.2 179.8 %reduce-scatter.10.cloned.1.call-start = ((), (), s32[]{:S(2)}) async-start(), calls=%async_computation.13 | async-start | bytes 7372800 | tf_op jit(solution)/shard_map/reduce_scatter | solution.py:183
  487.6 23.1 %copy-start.36 = (bf16[1088,1088]{1,0:T(8,128)(2,1)S(1)}, bf16[1088,1088]{1,0:T(8,128)(2,1)}, u32[]{:S(2)}) copy-start(bf16[1088,1088]{1,0:T(8,128)(2,1)} %all-gather.16.cloned.1.call-done) | copy-start | bytes 7102468
  509.2 1.6 copy-start.39
  517.1 95.4 %reduce-scatter.8.cloned.1.call-start = ((), (), s32[]{:S(2)}) async-start(), calls=%async_computation.11 | async-start | bytes 3686400 | tf_op jit(solution)/shard_map/reduce_scatter | solution.py:169
  517.3 6.7 copy-start.37
  522.5 1.5 copy-start.8
  529.9 503.5 %reduce-scatter.16.cloned.1.call-start = ((), (), s32[]{:S(2)}) async-start(), calls=%async_computation.16 | async-start | bytes 13926400
  575.0 41.8 %copy-start.6 = (bf16[320,1088]{1,0:T(8,128)(2,1)S(1)}, bf16[320,1088]{1,0:T(8,128)(2,1)}, u32[]{:S(2)}) copy-start(bf16[320,1088]{1,0:T(8,128)(2,1)} %param.23) | copy-start | bytes 2088964
  612.5 4.6 copy-start.11
  615.7 1.1 copy-start.2
  801.4 122.0 %collective-permute-start.1 = (bf16[2176,1280]{1,0:T(8,128)(2,1)}, bf16[2176,1280]{1,0:T(8,128)(2,1)S(1)}, u32[]{:S(2)}, u32[]{:S(2)}) collective-permute-start(bf16[2176,1280]{1,0:T(8,128)(2,1)} %fusion.47), channel_id=1, source_target_pairs={{0,4},{4,0},{8,12},{12,8},{1,5},{5,1},{9,13},{13,9},{2,6},{6,2},{1... | collective-permute-start | bytes 16711688 | tf_op jit(solution)/shard_map/ppermute | solution.py:14
  943.6 1.1 copy-start.5
  943.6 155.9 %reduce-scatter.14.cloned.1.call-start = ((), (), s32[]{:S(2)}) async-start(), calls=%async_computation.15 | async-start | bytes 7520256 | tf_op jit(solution)/shard_map/reduce_scatter | solution.py:237
  948.6 318.2 %reduce-scatter.12.cloned.1.call-start = ((), (), s32[]{:S(2)}) async-start(), calls=%async_computation.14 | async-start | bytes 21725184 | tf_op jit(solution)/shard_map/reduce_scatter | solution.py:234
  948.6 88.2 %copy-start.1 = (bf16[320,1088]{1,0:T(8,128)(2,1)S(1)}, bf16[320,1088]{1,0:T(8,128)(2,1)}, u32[]{:S(2)}) copy-start(bf16[320,1088]{1,0:T(8,128)(2,1)} %param.22) | copy-start | bytes 2088964
  948.6 88.2 %copy-start.14 = (f32[1088]{0:T(1024)S(1)}, f32[1088]{0:T(1024)}, u32[]{:S(2)}) copy-start(f32[1088]{0:T(1024)} %copy-done.13) | copy-start | bytes 13060
  948.6 88.2 %copy-start.16 = (f32[1088]{0:T(1024)S(1)}, f32[1088]{0:T(1024)}, u32[]{:S(2)}) copy-start(f32[1088]{0:T(1024)} %copy-done.15) | copy-start | bytes 13060
  948.6 88.2 %copy-start.18 = (f32[320]{0:T(512)S(1)}, f32[320]{0:T(512)}, u32[]{:S(2)}) copy-start(f32[320]{0:T(512)} %copy-done.17) | copy-start | bytes 3844
  948.6 88.2 %copy-start.20 = (f32[320]{0:T(512)S(1)}, f32[320]{0:T(512)}, u32[]{:S(2)}) copy-start(f32[320]{0:T(512)} %copy-done.19) | copy-start | bytes 3844
  1047.4 538.6 %all-reduce.27.cloned.1.call-start = ((), (), s32[]{:S(2)}) async-start(), calls=%async_computation.18 | async-start | bytes 20054016 | tf_op jit(solution)/shard_map/psum | solution.py:270
  1047.7 9.1 copy-start.9
  1047.8 9.1 copy-start.35
  1063.0 717.1 %all-reduce.25.cloned.1.call-start = ((), (), s32[]{:S(2)}) async-start(), calls=%async_computation.17 | async-start | bytes 19496960 | tf_op jit(solution)/shard_map/psum | solution.py:243
  1586.0 3.7 copy-start.12
  1591.6 8.1 copy-start.22
  1591.6 8.8 copy-start.3
  1780.1 6.7 copy-start.10
Sparse Core Ops, SparseCore 0:
  9.7 93.7 all-gather.7
  113.3 42.2 all-gather.9
  157.2 37.6 all-gather.11
  196.3 37.7 all-gather.15
  392.0 27.4 all-gather.13
  420.9 37.7 all-gather.17
  460.2 27.4 all-gather.19
  517.2 55.7 reduce-scatter.9
  575.8 36.7 reduce-scatter.7
  943.7 89.5 reduce-scatter.15
  1036.2 63.1 reduce-scatter.13
  1101.7 164.9 reduce-scatter.11
  1270.8 315.1 all-reduce.26
  1589.7 190.3 all-reduce.24
where the time goes:
time: 1800 us
  waiting for transfers between devices  1210 us (67%)
  matrix products  328 us (18%)
  blocking collectives  103 us (6%)
  local copies, waits for them, and re-layouts  74.9 us (4%)
  other arithmetic  53.3 us (3%)
    dot_general x129, matrix products, contract(): lax.dot_general(left, right, (((left_dim,), (right_dim,)), ((), ())), pre...  313 us
    psum x1, waiting for transfers between devices, local(): lax.psum((grad_fc, grad_proj, grad_bias_fc), ('shard', 'context'))  296 us
    ppermute x2, waiting for transfers between devices, partner(): lax.ppermute(value, axis, [(i, i ^ 1 << stride) for i in range(lax.axis_s...  234 us
    reduce_scatter x1, waiting for transfers between devices, local(): lax.psum_scatter(grad_mixer, 'shard', scatter_dimension=0, tiled=True)  167 us
    psum x1, waiting for transfers between devices, local(): lax.psum((owned[0], owned[1], owned[2], owned[3], owned[4], owned[5], own...  107 us
    unnamed x15, waiting for transfers between devices  84.3 us
    all_gather x1, waiting for transfers between devices, local(): lax.all_gather(w_qkv, 'shard', axis=0, tiled=True)  80.9 us
    psum x1, blocking collectives, local(): lax.psum((owned[0], owned[1], owned[2], owned[3], owned[4], owned[5], own...  61.6 us
  transfers between devices with their start and end apart: 16, of which 14 were waited for; matrix products, arithmetic and copies ran while one was open for 11% of the time, Pallas kernels for 0%

commit v1 on v0

v1 whole, which is shorter than its diff:
```python
import functools

import jax
import jax.numpy as jnp
from jax import lax
from jax.experimental import pallas as pl
from jax.experimental.pallas import tpu as pltpu
from jax.sharding import PartitionSpec as P

HEAD_DIM = 64
PAIR = 2 * HEAD_DIM
PIECE = 128
TRUNK = 8 * PIECE
BRANCH = 3 * PIECE
EPSILON = 1e-05
NEGATIVE = -1e30
F32 = jnp.float32
BF16 = jnp.bfloat16
VMEM = pl.BlockSpec(memory_space=pltpu.VMEM)
SMEM = pl.BlockSpec(memory_space=pltpu.SMEM)
ANY = pl.BlockSpec(memory_space=pl.ANY)
MESH = pl.DeviceIdType.MESH


def contract(left, right, left_dim, right_dim):
    return lax.dot_general(
        left, right, (((left_dim,), (right_dim,)), ((), ())), preferred_element_type=F32
    )


def layer_norm(inputs, gain, shift):
    average = jnp.mean(inputs, axis=-1, keepdims=True)
    centered = inputs - average
    spread = jnp.mean(centered * centered, axis=-1, keepdims=True)
    return centered * lax.rsqrt(spread + EPSILON) * gain + shift


def gelu_exact(inputs):
    return jax.nn.gelu(inputs, approximate=False)


def flip(value, bit):
    low = 1 << bit
    return value + low - 2 * low * lax.rem(lax.div(value, low), 2)


def place():
    tensor, context = lax.axis_index("tensor"), lax.axis_index("context")
    return tensor, context, lax.rem(context, 2) * lax.axis_size("tensor") + tensor


def member(mask):
    tensor, context, _ = place()
    size = lax.axis_size("tensor")
    bits = size.bit_length() - 1
    for bit in range(bits):
        if mask >> bit & 1:
            tensor = flip(tensor, bit)
    if mask >> bits & 1:
        context = flip(context, 0)
    return {"context": context, "tensor": tensor}, lax.rem(context, 2) * size + tensor


def greet(masks):
    barrier = pltpu.get_barrier_semaphore()
    for mask in masks:
        pl.semaphore_signal(barrier, inc=1, device_id=member(mask)[0], device_id_type=MESH)
    pl.semaphore_wait(barrier, len(masks))


def swap(value, axis, bit):
    size = lax.axis_size(axis)
    return lax.ppermute(value, axis, [(i, i ^ 1 << bit) for i in range(size)])


def group_gather_kernel(masks, natural, x, out, own_sem, send, recv):
    rows = x.shape[0]
    far = [m for m in masks if m & 1 == 0]
    greet(far + [1])

    def copy(source, target, owner):
        seen = owner ^ target
        index = member(owner)[1] if natural else seen
        return pltpu.make_async_remote_copy(
            src_ref=source,
            dst_ref=out.at[pl.ds(pl.multiple_of(index * rows, rows), rows)],
            send_sem=send.at[seen],
            recv_sem=recv.at[seen],
            device_id=member(target)[0],
            device_id_type=MESH,
        )

    def held(owner):
        index = member(owner)[1] if natural else owner
        return out.at[pl.ds(pl.multiple_of(index * rows, rows), rows)]

    first = [copy(x, m, 0) for m in far]
    for c in first:
        c.start()
    near = copy(x, 1, 0)
    near.start()
    own = pltpu.make_async_copy(x, held(0), own_sem)
    own.start()
    passed = []
    for m, c in zip(far, first):
        c.wait_recv()
        on = copy(held(m), 1, m)
        on.start()
        passed.append(on)
    own.wait()
    near.wait_recv()
    for on in passed:
        on.wait_recv()
    for c in first + [near] + passed:
        c.wait_send()


def semaphores(size):
    return [
        pltpu.SemaphoreType.DMA,
        pltpu.SemaphoreType.DMA((size,)),
        pltpu.SemaphoreType.DMA((size,)),
    ]


def group_gather(x, whole_tree, natural, collective_id, name):
    size = lax.axis_size("tensor") * (2 if whole_tree else 1)
    return pl.pallas_call(
        functools.partial(group_gather_kernel, list(range(1, size)), natural),
        in_specs=[ANY],
        out_specs=ANY,
        out_shape=jax.ShapeDtypeStruct((size * x.shape[0], x.shape[1]), x.dtype),
        scratch_shapes=semaphores(size),
        compiler_params=pltpu.CompilerParams(collective_id=collective_id, has_side_effects=True),
        name=name,
    )(x)


def exchange_kernel(masks, to_rows, x, out, own_sem, send, recv):
    greet(masks)
    tall, wide = (x, out) if to_rows else (out, x)
    rows, columns = wide.shape[0], tall.shape[1]

    def below(ref, index):
        return ref.at[pl.ds(pl.multiple_of(index * rows, rows), rows), :]

    def beside(ref, index):
        return ref.at[:, pl.ds(pl.multiple_of(index * columns, columns), columns)]

    source, target = (below, beside) if to_rows else (beside, below)
    me = member(0)[1]
    copies = []
    for mask in masks:
        device, index = member(mask)
        copies.append(
            pltpu.make_async_remote_copy(
                src_ref=source(x, index),
                dst_ref=target(out, me),
                send_sem=send.at[mask],
                recv_sem=recv.at[mask],
                device_id=device,
                device_id_type=MESH,
            )
        )
        copies[-1].start()
    own = pltpu.make_async_copy(source(x, me), target(out, me), own_sem)
    own.start()
    own.wait()
    for copy in copies:
        copy.wait_recv()
    for copy in copies:
        copy.wait_send()


def exchange(x, to_rows, collective_id, name):
    size = 2 * lax.axis_size("tensor")
    rows, columns = x.shape
    shape = (rows // size, columns * size) if to_rows else (rows * size, columns // size)
    return pl.pallas_call(
        functools.partial(exchange_kernel, list(range(1, size)), to_rows),
        in_specs=[ANY],
        out_specs=ANY,
        out_shape=jax.ShapeDtypeStruct(shape, x.dtype),
        scratch_shapes=semaphores(size),
        compiler_params=pltpu.CompilerParams(collective_id=collective_id, has_side_effects=True),
        name=name,
    )(x)


def sum_scatter_kernel(x, out, near, far, send, recv):
    rows = out.shape[0]
    greet([1, 2])

    def block(mask):
        return x.at[mask * rows : (mask + 1) * rows, :]

    def copy(source, target, mask, index):
        return pltpu.make_async_remote_copy(
            src_ref=source,
            dst_ref=target,
            send_sem=send.at[index],
            recv_sem=recv.at[index],
            device_id=member(mask)[0],
            device_id_type=MESH,
        )

    onward = copy(block(3), near.at[1], 1, 0)
    onward.start()
    mine = copy(block(1), near.at[0], 1, 1)
    mine.start()
    onward.wait_recv()
    far[0] = (block(2)[...].astype(F32) + near[1].astype(F32)).astype(BF16)
    across = copy(far.at[0], far.at[1], 2, 2)
    across.start()
    mine.wait_recv()
    out[...] = block(0)[...].astype(F32) + near[0].astype(F32)
    across.wait_recv()
    out[...] += far[1].astype(F32)
    for c in (onward, mine, across):
        c.wait_send()


def sum_scatter(x, collective_id, name):
    rows, columns = x.shape[0] // lax.axis_size("tensor"), x.shape[1]
    return pl.pallas_call(
        sum_scatter_kernel,
        in_specs=[VMEM],
        out_specs=VMEM,
        out_shape=jax.ShapeDtypeStruct((rows, columns), F32),
        scratch_shapes=[
            pltpu.VMEM((2, rows, columns), BF16),
            pltpu.VMEM((2, rows, columns), BF16),
            pltpu.SemaphoreType.DMA((3,)),
            pltpu.SemaphoreType.DMA((3,)),
        ],
        compiler_params=pltpu.CompilerParams(
            collective_id=collective_id, has_side_effects=True, vmem_limit_bytes=24 << 20
        ),
        name=name,
    )(x)


def tri(n):
    r=lax.broadcasted_iota(jnp.int32,(n,n),0); c=lax.broadcasted_iota(jnp.int32,(n,n),1)
    return c<=r

def branch_mask():
    r=lax.broadcasted_iota(jnp.int32,(BRANCH,BRANCH),0); c=lax.broadcasted_iota(jnp.int32,(BRANCH,BRANCH),1)
    return (c<=r)&((c<PIECE)|(c//PIECE==r//PIECE))

def split_heads(x):
    lane=lax.broadcasted_iota(jnp.int32,(1,2*64),1)<64
    z=jnp.zeros_like(x)
    return jnp.concatenate([jnp.where(lane,x,z),jnp.where(lane,z,x)],axis=0)

def join_heads(x):
    n=x.shape[0]//2
    lane=lax.broadcasted_iota(jnp.int32,(1,2*64),1)<64
    return jnp.where(lane,x[:n],x[n:])

def fwd_kernel(order, qkv, q16, qinfo, kinfo, att, att16, canon, of, lse, of16, lse16):
    n_p=qkv.shape[0]//PIECE
    for i in range(n_p):
        src=pl.ds(pl.multiple_of(order[i]*PIECE,PIECE),PIECE)
        canon[i*PIECE:(i+1)*PIECE,:]=qkv[src,0:384]
    def rows(start,size,parts):
        qh=split_heads(canon[pl.ds(start,size),0:128])
        ss=[]
        for ks,kn,mask in parts:
            s=contract(qh,canon[pl.ds(ks,kn),128:256],1,1)
            if mask is not None:
                m2=jnp.concatenate([mask,mask],axis=0)
                s=jnp.where(m2,s,NEGATIVE)
            ss.append(s)
        top=functools.reduce(jnp.maximum,[jnp.max(s,axis=1,keepdims=True) for s in ss])
        tot=0.; o=0.
        for (ks,kn,_),s in zip(parts,ss):
            e=jnp.exp(s-top)
            tot=tot+jnp.sum(e,axis=1,keepdims=True)
            o=o+contract(e.astype(BF16),canon[pl.ds(ks,kn),256:384],1,0)
        o=join_heads(o*(1.0/tot))
        of[pl.ds(start,size),:]=o
        l=top+jnp.log(tot)
        lse[pl.ds(start,size),:]=join_heads(jnp.broadcast_to(l,(2*size,128)))
    t=tri(256)
    for b in range(4):
        parts=[(b*256,256,t)]
        if b: parts.insert(0,(0,b*256,None))
        rows(b*256,256,parts)
    bm=branch_mask()
    def branch(b,_):
        st=pl.multiple_of(TRUNK+b*BRANCH,PIECE)
        rows(st,BRANCH,[(0,TRUNK,None),(st,BRANCH,bm)])
        return 0
    lax.fori_loop(0,4,branch,0)
    for i in range(n_p):
        dst=pl.ds(pl.multiple_of(order[i]*PIECE,PIECE),PIECE)
        att[dst,:]=of[i*PIECE:(i+1)*PIECE,:].astype(BF16)
    s=contract(q16[...],qkv[:,384:512],1,1)
    s=jnp.where(allowed_mask(qinfo,kinfo),s,NEGATIVE)
    top=jnp.max(s,axis=1,keepdims=True)
    e=jnp.exp(s-top)
    tot=jnp.sum(e,axis=1,keepdims=True)
    o=contract(e.astype(BF16),qkv[:,384:512],1,0)*(1.0/tot)
    of16[...]=o
    att16[...]=o.astype(BF16)
    lse16[...]=jnp.broadcast_to(top+jnp.log(tot),o.shape)

def allowed_mask(qinfo,kinfo):
    ks=kinfo[0:1,:]; kp=kinfo[1:2,:]
    return ((ks==qinfo[:,0:1])|(ks==qinfo[:,1:2])|(ks==qinfo[:,2:3]))&(kp<=qinfo[:,3:4])

def attention_forward(order,qkv,q16,qinfo,kinfo):
    n=qkv.shape[0]; r=q16.shape[0]
    sd=jax.ShapeDtypeStruct
    V=pl.BlockSpec(memory_space=pltpu.VMEM)
    return pl.pallas_call(fwd_kernel,
        in_specs=[pl.BlockSpec(memory_space=pltpu.SMEM)]+[V]*4,
        out_specs=[V]*7,
        out_shape=[sd((n,128),BF16),sd((r,128),BF16),sd((n,384),BF16),sd((n,128),F32),sd((n,128),F32),sd((r,128),F32),sd((r,128),F32)],
        compiler_params=pltpu.CompilerParams(vmem_limit_bytes=50<<20),
        cost_estimate=pl.CostEstimate(flops=20_000_000_000,bytes_accessed=8_000_000,transcendentals=7_000_000),
        name="tree_attention_forward",
    )(order,qkv,q16,qinfo,kinfo)

def bwd_kernel(order, canon, of, lse, datt, kv16, q16, of16, lse16, datt16, qinfo, kinfo, dqkv, dq16, dc, dacc):
    n_p=canon.shape[0]//PIECE
    for i in range(n_p):
        src=pl.ds(pl.multiple_of(order[i]*PIECE,PIECE),PIECE)
        dc[i*PIECE:(i+1)*PIECE,:]=datt[src,:]
    def rows(start,size,parts):
        r=pl.ds(start,size)
        qh=split_heads(canon[r,0:128])
        d=dc[r,:]
        dh=split_heads(d)
        prod=d.astype(F32)*of[r,:]
        delta=jnp.concatenate([jnp.sum(prod[:,0:64],axis=1,keepdims=True),jnp.sum(prod[:,64:128],axis=1,keepdims=True)],axis=0)
        l=jnp.concatenate([lse[r,0:1],lse[r,64:65]],axis=0)
        dq=0.
        for ks,kn,mask,first in parts:
            kk=canon[pl.ds(ks,kn),128:256]
            s=contract(qh,kk,1,1)
            if mask is not None:
                s=jnp.where(jnp.concatenate([mask,mask],axis=0),s,NEGATIVE)
            p=jnp.exp(s-l)
            dp=contract(dh,canon[pl.ds(ks,kn),256:384],1,1)
            ds=(p*(dp-delta)).astype(BF16)
            dv=contract(p.astype(BF16),dh,0,0)
            dk=contract(ds,qh,0,0)
            dq=dq+contract(ds,kk,1,0)
            if first:
                dacc[pl.ds(ks,kn),128:256]=dk
                dacc[pl.ds(ks,kn),256:384]=dv
            else:
                dacc[pl.ds(ks,kn),128:256]+=dk
                dacc[pl.ds(ks,kn),256:384]+=dv
        dacc[r,0:128]=join_heads(dq)
    t=tri(256)
    for b in range(4):
        parts=[(b*256,256,t,True)]
        if b: parts.insert(0,(0,b*256,None,False))
        rows(b*256,256,parts)
    bm=branch_mask()
    def branch(b,_):
        st=pl.multiple_of(TRUNK+b*BRANCH,PIECE)
        rows(st,BRANCH,[(0,TRUNK,None,False),(st,BRANCH,bm,True)])
        return 0
    lax.fori_loop(0,4,branch,0)
    for i in range(n_p):
        dst=pl.ds(pl.multiple_of(order[i]*PIECE,PIECE),PIECE)
        x=dacc[i*PIECE:(i+1)*PIECE,:]
        dqkv[dst,0:128]=(x[:,0:128]*0.125).astype(BF16)
        dqkv[dst,128:384]=x[:,128:384].astype(BF16)
    k16=kv16[:,384:512]
    s=contract(q16[...],k16,1,1)
    s=jnp.where(allowed_mask(qinfo,kinfo),s,NEGATIVE)
    p=jnp.exp(s-lse16[:,0:1])
    dp=contract(datt16[...],k16,1,1)
    delta=jnp.sum(datt16[...].astype(F32)*of16[...],axis=1,keepdims=True)
    ds=(p*(dp-delta)).astype(BF16)
    dqkv[:,384:512]=(contract(ds,q16[...],0,0)+contract(p.astype(BF16),datt16[...],0,0)).astype(BF16)
    dq16[...]=(contract(ds,k16,1,0)*0.125).astype(BF16)

def attention_backward(order,canon,of,lse,datt,qkv,q16,of16,lse16,datt16,qinfo,kinfo):
    n=canon.shape[0]; r=q16.shape[0]
    sd=jax.ShapeDtypeStruct
    V=pl.BlockSpec(memory_space=pltpu.VMEM)
    return pl.pallas_call(bwd_kernel,
        in_specs=[pl.BlockSpec(memory_space=pltpu.SMEM)]+[V]*11,
        out_specs=[V]*2,
        out_shape=[sd((n,512),BF16),sd((r,128),BF16)],
        scratch_shapes=[pltpu.VMEM((n,128),BF16),pltpu.VMEM((n,384),F32)],
        compiler_params=pltpu.CompilerParams(vmem_limit_bytes=60<<20),
        cost_estimate=pl.CostEstimate(flops=50_000_000_000,bytes_accessed=15_000_000,transcendentals=7_000_000),
        name="tree_attention_backward",
    )(order,canon,of,lse,datt,qkv,q16,of16,lse16,datt16,qinfo,kinfo)


def parent_lookup(identities, shifted_table):
    labels = jnp.arange(shifted_table.shape[0], dtype=jnp.int32)
    matches = identities[:, None] == labels[None, :]
    return jnp.sum(jnp.where(matches, shifted_table[None, :], 0), axis=1) - 1


def tree_order(segments, places, parent):
    own = segments.reshape(-1, PIECE)[:, 0]
    start = places.reshape(-1, PIECE)[:, 0]
    table = parent + 1
    first_up = parent_lookup(own, table)
    second_up = parent_lookup(first_up, table)
    is_branch = (first_up >= 0) & (second_up < 0)
    is_leaf = second_up >= 0
    branch = jnp.where(is_leaf, first_up, own)
    rank = jnp.sum((is_branch[None, :] & (own[None, :] < branch[:, None])).astype(jnp.int32), axis=1)
    twin = is_leaf[None, :] & (first_up[None, :] == first_up[:, None]) & (own[None, :] < own[:, None])
    leaf = 1 + jnp.sum(twin.astype(jnp.int32), axis=1)
    target = jnp.where(
        first_up < 0, start // PIECE, TRUNK // PIECE + 3 * rank + jnp.where(is_leaf, leaf, 0)
    )
    pieces = jnp.arange(own.shape[0], dtype=jnp.int32)
    order = jnp.sum(jnp.where(target[None, :] == pieces[:, None], pieces[None, :], 0), axis=1)
    return order, first_up, second_up


def local(
    tokens,
    cotangent,
    segment_of,
    position_of,
    parent,
    ln1_gain,
    ln1_bias,
    w_qkv,
    b_query,
    b_value,
    w_out,
    b_out,
    ln2_gain,
    ln2_bias,
    w_fc,
    b_fc,
    w_proj,
    b_proj,
):
    rows, width = tokens.shape
    half = w_qkv.shape[0]
    shard = lax.axis_index("shard")
    tensor, context, me = place()
    members = 2 * lax.axis_size("tensor")
    tree_rows = members * rows
    low = shard == 0
    shared = width - HEAD_DIM
    scale = HEAD_DIM ** (-0.5)

    def both(mine, other, axis=0):
        return jnp.concatenate([jnp.where(low, mine, other), jnp.where(low, other, mine)], axis=axis)

    vectors = jnp.stack(
        [ln1_gain, ln1_bias, b_query, b_value, b_out, ln2_gain, ln2_bias, b_proj]
    )
    vectors = both(vectors, swap(vectors, "shard", 0), 1).astype(F32)
    gain_one, shift_one, bias_query, bias_value, bias_out, gain_two, shift_two, bias_proj = vectors

    def pair_columns(array, axis):
        return lax.dynamic_slice_in_dim(array, me * PAIR, PAIR, axis)

    mixer = jnp.concatenate(
        [pair_columns(w_qkv[:, i * width : (i + 1) * width], 1) for i in range(3)]
        + [w_qkv[:, i * width + shared : (i + 1) * width] for i in (1, 2, 0)],
        axis=1,
    )
    mixer = both(mixer, swap(mixer, "shard", 0))
    everyone = group_gather(tokens, True, True, 0, "gather_tokens")
    out_other = swap(w_out, "shard", 0)
    out_weight = both(w_out, out_other)
    fc_weight = both(w_fc, swap(w_fc, "shard", 0))
    proj_other = swap(w_proj, "shard", 0)
    proj_weight = both(w_proj, proj_other, 1)
    quarter = half // 2
    near = lax.rem(tensor, 2)
    mixer_part = lax.dynamic_slice_in_dim(w_qkv, near * quarter, quarter, 0)
    mixer_part, _ = lax.optimization_barrier((mixer_part, proj_other))
    mixer_part = swap(mixer_part, "shard", 0)
    mixer_rest = swap(mixer_part, "tensor", 0)
    mixer_other = jnp.concatenate(
        [
            jnp.where(near == 0, mixer_part, mixer_rest),
            jnp.where(near == 0, mixer_rest, mixer_part),
        ],
        axis=0,
    )

    tree_start = lax.div(context, 2) * tree_rows
    segments = lax.dynamic_slice_in_dim(segment_of, tree_start, tree_rows)
    places = lax.dynamic_slice_in_dim(position_of, tree_start, tree_rows)
    order, first_up, second_up = tree_order(segments, places, parent)
    key_info = jnp.stack([segments, places])
    query_info = jnp.stack(
        [segments, jnp.repeat(first_up, PIECE), jnp.repeat(second_up, PIECE), places], axis=1
    )
    query_info = lax.dynamic_slice_in_dim(query_info, me * rows, rows, 0)

    normed_all = layer_norm(everyone.astype(F32), gain_one, shift_one).astype(BF16)
    inputs = tokens.astype(F32)
    normed_f, norm_one_pull = jax.vjp(layer_norm, inputs, gain_one, shift_one)
    normed = normed_f.astype(BF16)
    zero = jnp.zeros((PAIR,), F32)
    mixed_bias = jnp.concatenate(
        [pair_columns(bias_query, 0), zero, pair_columns(bias_value, 0), zero[:HEAD_DIM], bias_value[shared:]]
    )
    mixed_scale = jnp.concatenate([jnp.full((PAIR,), scale, F32), jnp.ones((3 * PAIR,), F32)])
    mixed = (
        (jnp.dot(normed_all, mixer[:, : 4 * PAIR], preferred_element_type=F32) + mixed_bias) * mixed_scale
    ).astype(BF16)
    query_last = (
        (jnp.dot(normed, mixer[:, 4 * PAIR :], preferred_element_type=F32) + bias_query[shared:]) * scale
    ).astype(BF16)
    query_last = jnp.pad(query_last, ((0, 0), (0, HEAD_DIM)))
    attended_pair, attended_last, sorted_qkv, exact, level, exact_last, level_last = attention_forward(
        order, mixed, query_last, query_info, key_info
    )
    attended = jnp.concatenate(
        [exchange(attended_pair, True, 1, "attended_to_rows"), attended_last[:, HEAD_DIM:]], axis=1
    )
    middle = inputs + jnp.dot(attended, out_weight, preferred_element_type=F32) + bias_out

    normed_two_f, norm_two_pull = jax.vjp(layer_norm, middle, gain_two, shift_two)
    group_rows = group_gather(normed_two_f.astype(BF16), False, False, 2, "gather_normed")
    grads = [cotangent]
    for mask in range(1, lax.axis_size("tensor")):
        grads.append(
            lax.ppermute(cotangent, "tensor", [(i, i ^ mask) for i in range(lax.axis_size("tensor"))])
        )
    group_grads = jnp.concatenate(grads, axis=0)
    before = jnp.dot(group_rows, fc_weight, preferred_element_type=F32) + b_fc.astype(F32)
    hidden_f, gelu_pull = jax.vjp(gelu_exact, before)
    hidden = hidden_f.astype(BF16)
    d_hidden = contract(group_grads, proj_weight, 1, 1)
    d_before = gelu_pull(d_hidden)[0].astype(BF16)
    d_normed_two = sum_scatter(contract(d_before, fc_weight, 1, 1).astype(BF16), 3, "sum_d_normed")
    mlp_out = sum_scatter(
        jnp.dot(hidden, proj_weight, preferred_element_type=F32).astype(BF16), 4, "sum_mlp"
    )
    output = (middle + mlp_out + bias_proj).astype(BF16)
    grad_proj = contract(group_grads, hidden, 0, 0)
    grad_fc = contract(group_rows, d_before, 0, 0)
    grad_bias_fc = jnp.sum(d_before, axis=0, dtype=F32)

    def halves(array, axis=0):
        first, second = jnp.split(array, 2, axis)
        return jnp.where(low, first, second), jnp.where(low, second, first)

    def low_half(array, is_low, axis=0):
        first, second = jnp.split(array, 2, axis)
        return jnp.where(is_low, first, second), jnp.where(is_low, second, first)

    keep_fc, give_fc = halves(grad_fc)
    keep_proj, give_proj = halves(grad_proj)
    got = swap(jnp.stack([give_fc, give_proj]).astype(BF16), "shard", 0).astype(F32)
    partial = jnp.stack([keep_fc + got[0], keep_proj + got[1]])
    contexts = lax.axis_size("context")
    chunk = half // 4
    low_bits = lax.rem(context, 4)

    def context_swap(value, mask):
        return lax.ppermute(value, "context", [(i, i ^ mask) for i in range(contexts)])

    def relative(mask):
        index = low_bits
        for bit in range(2):
            if mask >> bit & 1:
                index = flip(index, bit)
        return index * chunk

    total = lax.dynamic_slice_in_dim(partial, relative(0), chunk, 1)
    for mask in range(1, 4):
        part = lax.dynamic_slice_in_dim(partial, relative(mask), chunk, 1).astype(BF16)
        total = total + context_swap(part, mask).astype(F32)
    mask = 4
    while mask < contexts:
        total = total + context_swap(total.astype(BF16), mask).astype(F32)
        mask *= 2
    total = total.astype(BF16)
    whole = jnp.zeros((2, half, grad_fc.shape[1]), F32)
    whole = lax.dynamic_update_slice_in_dim(whole, total.astype(F32), relative(0), 1)
    for mask in range(1, 4):
        whole = lax.dynamic_update_slice_in_dim(
            whole, context_swap(total, mask).astype(F32), relative(mask), 1
        )
    own_fc, own_proj = whole[0], whole[1].T

    d_middle, grad_gain_two, grad_shift_two = norm_two_pull(d_normed_two)
    d_middle = d_middle + cotangent.astype(F32)
    d_attn = d_middle.astype(BF16)
    d_attended = contract(d_attn, out_weight, 1, 1).astype(BF16)
    d_pair = exchange(d_attended[:, :shared], False, 5, "d_attended_to_heads")
    d_last = jnp.pad(d_attended[:, shared:], ((0, 0), (HEAD_DIM, 0)))
    d_mixed, d_query_last = attention_backward(
        order, sorted_qkv, exact, level, d_pair, mixed, query_last, exact_last, level_last, d_last,
        query_info, key_info,
    )
    d_rows = exchange(d_mixed, True, 6, "d_mixed_to_rows").reshape(rows, members, 4, PAIR)
    d_key_value_last = jnp.sum(d_rows[:, :, 3].astype(F32), axis=1).astype(BF16)
    d_last_rows = jnp.concatenate([d_query_last[:, :HEAD_DIM], d_key_value_last], axis=1)
    d_own = jnp.concatenate(
        [
            part
            for i in range(3)
            for part in (
                d_rows[:, :, i].reshape(rows, shared),
                d_last_rows[:, i * HEAD_DIM : (i + 1) * HEAD_DIM],
            )
        ],
        axis=1,
    )
    d_normed = both(contract(d_own, w_qkv, 1, 1), contract(d_own, mixer_other, 1, 1), 1)
    d_inputs, grad_gain_one, grad_shift_one = norm_one_pull(d_normed)
    d_inputs = d_inputs + d_middle

    grad_pair = contract(normed_all, d_mixed[:, : 3 * PAIR], 0, 0)
    keep, give = halves(grad_pair)
    keep = keep + swap(give.astype(BF16), "shard", 0).astype(F32)
    mask = 2
    while mask < contexts:
        keep = keep + context_swap(keep.astype(BF16), mask).astype(F32)
        mask *= 2
    pairs = group_gather(keep.astype(BF16), True, True, 7, "gather_pair_gradients")
    pairs = pairs.reshape(members, half, 3, PAIR)

    grad_out = contract(attended, d_attn, 0, 0)
    grad_last = contract(normed, d_last_rows, 0, 0)
    joint = jnp.concatenate([grad_out, jnp.pad(grad_last, ((0, 0), (0, HEAD_DIM)))], axis=1)
    is_near = near == 0
    keep, give = low_half(joint, is_near, 1)
    keep = keep + swap(give.astype(BF16), "tensor", 0).astype(F32)
    keep, give = halves(keep)
    keep = keep + swap(give.astype(BF16), "shard", 0).astype(F32)
    is_second = lax.rem(lax.div(tensor, 2), 2) == 0
    keep, give = low_half(keep, is_second)
    keep = keep + swap(give.astype(BF16), "tensor", 1).astype(F32)
    is_context = lax.rem(context, 2) == 0
    keep, give = low_half(keep, is_context)
    keep = keep + context_swap(give.astype(BF16), 1).astype(F32)
    mask = 2
    while mask < contexts:
        keep = keep + context_swap(keep.astype(BF16), mask).astype(F32)
        mask *= 2
    keep = keep.astype(BF16)

    def rejoin(mine, other, is_low, axis=0):
        return jnp.concatenate(
            [jnp.where(is_low, mine, other), jnp.where(is_low, other, mine)], axis=axis
        )

    keep = rejoin(keep, context_swap(keep, 1), is_context)
    keep = rejoin(keep, swap(keep, "tensor", 1), is_second)
    keep = rejoin(keep, swap(keep, "tensor", 0), is_near, 1).astype(F32)
    own_out = keep[:, :width]
    own_mixer = jnp.concatenate(
        [
            part
            for i in range(3)
            for part in (
                pairs[:, :, i].transpose(1, 0, 2).reshape(half, shared).astype(F32),
                keep[:, width + i * HEAD_DIM : width + (i + 1) * HEAD_DIM],
            )
        ],
        axis=1,
    )

    sums = [
        grad_gain_one,
        grad_shift_one,
        jnp.sum(d_own[:, :width], axis=0, dtype=F32),
        jnp.sum(d_own[:, 2 * width :], axis=0, dtype=F32),
        jnp.sum(d_attn, axis=0, dtype=F32),
        grad_gain_two,
        grad_shift_two,
        jnp.sum(cotangent, axis=0, dtype=F32),
    ]
    sums += [jnp.where(tensor == i, grad_bias_fc, 0.0) for i in range(lax.axis_size("tensor"))]
    sums = lax.psum(jnp.stack(sums), ("shard", "context", "tensor"))
    mine = lax.dynamic_slice_in_dim(sums[:8], shard * half, half, 1)
    own_bias_fc = lax.dynamic_slice_in_dim(sums, 8 + tensor, 1, 0)[0]
    return (
        output,
        d_inputs,
        mine[0],
        mine[1],
        own_mixer,
        mine[2],
        mine[3],
        own_out,
        mine[4],
        mine[5],
        mine[6],
        own_fc,
        own_bias_fc,
        own_proj,
        mine[7],
    )


def solution(mesh):
    return jax.shard_map(
        local,
        mesh=mesh,
        in_specs=(
            P(("shard", "context", "tensor"), None),
            P(("shard", "context", "tensor"), None),
            P("shard"),
            P("shard"),
            P(),
            P("shard"),
            P("shard"),
            P("shard", None),
            P("shard"),
            P("shard"),
            P("shard", None),
            P("shard"),
            P("shard"),
            P("shard"),
            P("shard", "tensor"),
            P("tensor"),
            P("tensor", "shard"),
            P("shard"),
        ),
        out_specs=(
            P(("shard", "context", "tensor"), None),
            P(("shard", "context", "tensor"), None),
            P("shard"),
            P("shard"),
            P("shard", None),
            P("shard"),
            P("shard"),
            P("shard", None),
            P("shard"),
            P("shard"),
            P("shard"),
            P("shard", "tensor"),
            P("tensor"),
            P("tensor", "shard"),
            P("shard"),
        ),
        check_vma=False,
    )
```

time: 1800 us -> 767 us (0.43)
  waiting for transfers between devices: 1210 us -> 105 us
  Pallas kernels: 0 us -> 249 us
  matrix products: 328 us -> 88.1 us
  local copies, waits for them, and re-layouts: 74.9 us -> 134 us
  blocking collectives: 103 us -> 64.6 us
  other arithmetic: 53.3 us -> 84.6 us
  starting transfers between devices: 4.99 us -> 32.4 us
    psum x2 -> x0, waiting for transfers between devices: 403 us -> none  [the longest x1 296 us: local(): lax.psum((grad_fc, grad_proj, grad_bias_fc), ('shard', 'context'))]
    reduce_scatter x4 -> x0, waiting for transfers between devices: 284 us -> none  [the longest x1 167 us: local(): lax.psum_scatter(grad_mixer, 'shard', scatter_dimension=0, tiled=True)]
    dot_general x129 -> x10, matrix products: 313 us -> 49.5 us  [contract(): lax.dot_general(left, right, (((left_dim,), (right_dim,)), ((), ())), pre...]
    pallas_call x0 -> x10, Pallas kernels: none -> 249 us  [the longest x3 104 us: group_gather(): pl.pallas_call(functools.partial(group_gather_kernel, list(range(1, size)...]
    all_gather x7 -> x0, waiting for transfers between devices: 208 us -> none  [the longest x1 80.9 us: local(): lax.all_gather(w_qkv, 'shard', axis=0, tiled=True)]
    ppermute x2 -> x27, waiting for transfers between devices: 234 us -> 105 us  [the longest x10 55.5 us: context_swap(): lax.ppermute(value, 'context', [(i, i ^ mask) for i in range(contexts)])]
    unnamed x15 -> x0, waiting for transfers between devices: 84.3 us -> none
    ppermute x2 -> x27, starting transfers between devices: 2.98 us -> 32.4 us  [the longest x10 15.6 us: context_swap(): lax.ppermute(value, 'context', [(i, i ^ mask) for i in range(contexts)])]
  transfers between devices with their start and end apart: 16 -> 27, of which waited for: 14 -> 9; matrix products, arithmetic and copies ran while one was open for 11% -> 24% of each run, Pallas kernels for 0% -> 17%
where the time goes in v1:
time: 767 us; the launch traced here: 760 us
  Pallas kernels  249 us (32%)
  local copies, waits for them, and re-layouts  134 us (17%)
  waiting for transfers between devices  105 us (14%)
  matrix products  88.1 us (11%)
  other arithmetic  84.6 us (11%)
  blocking collectives  64.6 us (8%)
  starting transfers between devices  32.4 us (4%)
    pallas_call x3, Pallas kernels, group_gather(): pl.pallas_call(functools.partial(group_gather_kernel, list(range(1, size)...  104 us
    psum x1, blocking collectives, local(): sums = lax.psum(jnp.stack(sums), ('shard', 'context', 'tensor'))  64.6 us
    ppermute x10, waiting for transfers between devices, context_swap(): lax.ppermute(value, 'context', [(i, i ^ mask) for i in range(contexts)])  55.5 us
    pallas_call x3, Pallas kernels, exchange(): pl.pallas_call(functools.partial(exchange_kernel, list(range(1, size)), t...  54.2 us
    ppermute x14, waiting for transfers between devices, swap(): return lax.ppermute(value, axis, [(i, i ^ 1 << bit) for i in range(size)])  49.5 us
    dot_general x10, matrix products, contract(): lax.dot_general(left, right, (((left_dim,), (right_dim,)), ((), ())), pre...  49.5 us
    pallas_call x2, Pallas kernels, sum_scatter(): pl.pallas_call(sum_scatter_kernel, in_specs=[VMEM], out_specs=VMEM, out_s...  41.8 us
    unnamed x205, local copies, waits for them, and re-layouts  32.7 us
  transfers between devices with their start and end apart: 27, of which 9 were waited for; matrix products, arithmetic and copies ran while one was open for 24% of the time, Pallas kernels for 17%

profile of v1, /device:TPU:0, one launch (start us, length us, event | category | flops | bytes accessed | tf_op | source)
XLA Modules:
  0.0 759.6 jit_solution(1214666836784149546)
XLA Ops:
  1.2 2.6 collective-permute-start.6
  11.4 4.3 fusion.93
  16.9 56.1 %gather_tokens.1 = bf16[2560,1088]{1,0:T(8,128)(2,1)} custom-call(bf16[320,1088]{1,0:T(8,128)(2,1)} %x.7), custom_call_target="tpu_custom_call" | custom-call | tf_op jit(solution)/shard_map/gather_tokens/pallas_call | solution.py:128
  75.9 3.7 convert_reduce_fusion
  87.4 2.8 constant_dynamic-slice_fusion.1
  94.4 7.5 fusion.5
  102.2 7.7 %collective-permute-done.1 = bf16[544,576]{1,0:T(8,128)(2,1)} collective-permute-done((bf16[544,576]{1,0:T(8,128)(2,1)S(1)}, bf16[544,576]{1,0:T(8,128)(2,1)}, u32[]{:S(2)}, u32[]{:S(2)}) %collective-permute-start.1) | collective-permute-done | bytes 626720 | tf_op jit(solution)/shard_map/ppermute | solution.py:73
  113.4 7.6 multiply_convert_fusion.1.qkv.kv16
  121.0 17.7 %tree_attention_forward.1 = (bf16[2560,128]{1,0:T(8,128)(2,1)S(1)}, bf16[320,128]{1,0:T(8,128)(2,1)S(1)}, bf16[2560,384]{1,0:T(8,128)(2,1)}, f32[2560,128]{1,0:T...) custom-call(s32[20]{0:T(128)S(1)} %select_reduce_fusion.order, ...), custom_call_target="tpu_custom_call" | custom-call | flops 20000000000 | bytes 8000000 | tf_op jit(solution)/shard_map/tree_attention_forward/pallas_call | solution.py:317
  143.0 11.1 %attended_to_rows.1 = bf16[320,1024]{1,0:T(8,128)(2,1)} custom-call(bf16[2560,128]{1,0:T(8,128)(2,1)} %copy-done.2), custom_call_target="tpu_custom_call" | custom-call | tf_op jit(solution)/shard_map/attended_to_rows/pallas_call | solution.py:179
  156.8 2.1 constant_dynamic-update-slice_fusion.1
  165.6 25.0 %gather_normed.1 = bf16[1280,1088]{1,0:T(8,128)(2,1)} custom-call(bf16[320,1088]{1,0:T(8,128)(2,1)} %add_convert_fusion.2.x), custom_call_target="tpu_custom_call" | custom-call | tf_op jit(solution)/shard_map/gather_normed/pallas_call | solution.py:128
  192.8 23.2 %multiply_convert_fusion = (bf16[1280,1088]{0,1:T(8,128)(2,1)}, f32[1280,1088]{0,1:T(8,128)}, f32[1280,1088]{0,1:T(8,128)}) fusion(f32[1088]{0:T(1024)S(1)} %copy-done.81, bf16[1280,1088]{1,0:T(8,128)(2,1)S(1)} %copy-done.33, bf16[544,1088]{1,0:T(8,128)(2,1)S(1)} %get-tuple-element.122, bf16[544,1088]{1,0:T(8,128)(2,1)S(1)} %get-tuple-element.121), kind=kOutput, calls=%fused_computation.23 | convolution fusion | flops 3127033856 | bytes 19083520 | tf_op jit(solution)/shard_map/dot_general | solution.py:535
  216.0 2.1 broadcast_select_fusion.3
  218.6 10.3 %convert_reduce_fusion.1 = (f32[1088]{0:T(1024)}, bf16[1280,1088]{0,1:T(8,128)(2,1)S(1)}) fusion(f32[1280,1088]{0,1:T(8,128)} %get-tuple-element.100, f32[1280,1088]{0,1:T(8,128)} %get-tuple-element.168, bf16[1280,1088]{1,0:T(8,128)(2,1)S(1)} %copy-done.56, bf16[1088,544]{0,1:T(8,128)(2,1)S(1)} %get-tuple-element.120, ...), kind=kOutput, calls=%fused_computation.21 | convolution fusion | flops 3057400832 | bytes 19083520 | tf_op jit(solution)/shard_map/dot_general | solution.py:26
  230.5 6.3 convolution_convert_fusion
  236.8 5.4 copy.129.x
  244.0 20.6 %sum_d_normed.1 = f32[320,1088]{1,0:T(8,128)S(1)} custom-call(bf16[1280,1088]{1,0:T(8,128)(2,1)S(1)} %copy-done), custom_call_target="tpu_custom_call" | custom-call | tf_op jit(solution)/shard_map/sum_d_normed/pallas_call | solution.py:225
  266.2 6.0 convolution_convert_fusion.1
  272.3 5.4 copy.128.x
  279.5 21.2 %sum_mlp.1 = f32[320,1088]{1,0:T(8,128)S(1)} custom-call(bf16[1280,1088]{1,0:T(8,128)(2,1)S(1)} %copy-done.1), custom_call_target="tpu_custom_call" | custom-call | tf_op jit(solution)/shard_map/sum_mlp/pallas_call | solution.py:225
  306.6 11.0 %d_attended_to_heads.1.datt = bf16[2560,128]{1,0:T(8,128)(2,1)} custom-call(bf16[320,1024]{1,0:T(8,128)(2,1)} %slice.191.x), custom_call_target="tpu_custom_call" | custom-call | tf_op jit(solution)/shard_map/d_attended_to_heads/pallas_call | solution.py:179
  318.3 31.1 %tree_attention_backward.1 = (bf16[2560,512]{1,0:T(8,128)(2,1)}, bf16[320,128]{1,0:T(8,128)(2,1)}) custom-call(s32[20]{0:T(128)} %copy-done.6, bf16[2560,384]{1,0:T(8,128)(2,1)} %get-tuple-element.27.canon, f32[2560,128]{1,0:T(8,128)} %copy-done.7, f32[2560,128]{1,0:T(8,128)} %copy-done.8, bf16[2560,128]{1,0:T(8,128)(2,1)} %d_attended_to_heads.1.datt, ...), custom_call_target="tpu_custom_call" | custom-call | flops 49999998976 | bytes 15000000 | tf_op jit(solution)/shard_map/tree_attention_backward/pallas_call | solution.py:388
  349.4 32.1 %d_mixed_to_rows.1 = bf16[320,4096]{1,0:T(8,128)(2,1)} custom-call(bf16[2560,512]{1,0:T(8,128)(2,1)} %get-tuple-element.32.x), custom_call_target="tpu_custom_call" | custom-call | tf_op jit(solution)/shard_map/d_mixed_to_rows/pallas_call | solution.py:179
  381.5 7.0 fusion.25
  388.5 3.9 fusion.54
  392.4 6.3 fusion.98
  398.6 6.5 fusion.99
  405.1 4.3 reshape.269
  409.5 14.0 %slice_reduce_fusion = (bf16[320,8,128]{2,1,0:T(8,128)(2,1)S(1)}, bf16[320,8,128]{2,1,0:T(8,128)(2,1)S(1)}, bf16[320,8,128]{2,1,0:T(8,128)(2,1)S(1)}, bf16[320,128]{1,0:T(8,128)(2,1)S(1)}) fusion(bf16[320,8,4,128]{3,2,1,0:T(4,128)(2,1)S(1)} %reshape.269), kind=kLoop, calls=%fused_computation.111 | loop fusion | flops 286720 | bytes 4669440 | tf_op jit(solution)/shard_map/slice | solution.py:610
  440.7 4.4 concatenate.69
  445.2 30.5 %collective-permute-done.10 = bf16[544,384]{1,0:T(8,128)(2,1)S(1)} collective-permute-done((bf16[544,384]{1,0:T(8,128)(2,1)}, bf16[544,384]{1,0:T(8,128)(2,1)S(1)}, u32[]{:S(2)}, u32[]{:S(2)}) %collective-permute-start.10) | collective-permute-done | bytes 417824 | tf_op jit(solution)/shard_map/ppermute | solution.py:73
  476.5 2.6 collective-permute-start.11
  479.1 3.4 convert_add_fusion
  483.8 2.2 copy.137
  487.5 5.4 fusion.97
  493.0 4.2 collective-permute-done.11
  499.1 22.8 %gather_pair_gradients.1 = bf16[4352,384]{1,0:T(8,128)(2,1)} custom-call(bf16[544,384]{1,0:T(8,128)(2,1)} %add_convert_fusion.3.x), custom_call_target="tpu_custom_call" | custom-call | tf_op jit(solution)/shard_map/gather_pair_gradients/pallas_call | solution.py:128
  521.9 5.8 copy.133
  527.7 9.3 %reshape.274 = bf16[8,544,3,128]{1,0,3,2:T(8,128)(2,1)} reshape(bf16[4352,384]{0,1:T(8,128)(2,1)} %copy.133) | data formatting | bytes 6684672 | tf_op jit(solution)/shard_map/reshape | solution.py:628
  537.0 9.8 %collective-permute-done.13 = bf16[544,672]{1,0:T(8,128)(2,1)} collective-permute-done((bf16[544,672]{1,0:T(8,128)(2,1)}, bf16[544,672]{1,0:T(8,128)(2,1)}, u32[]{:S(2)}, u32[]{:S(2)}) %collective-permute-start.13) | collective-permute-done | bytes 731168 | tf_op jit(solution)/shard_map/ppermute | solution.py:73
  546.8 2.2 copy.138
  553.3 2.9 convert_bitcast_fusion
  556.2 3.3 copy.143
  559.4 2.3 copy.142
  561.8 2.1 convert_element_type.254
  568.6 5.1 fusion.18
  573.7 2.2 collective-permute-done.15
  576.2 2.7 collective-permute-start.16
  584.6 35.8 %collective-permute-done.16 = bf16[136,672]{0,1:T(8,128)(2,1)S(1)} collective-permute-done((bf16[136,672]{0,1:T(8,128)(2,1)S(1)}, bf16[136,672]{0,1:T(8,128)(2,1)S(1)}, u32[]{:S(2)}, u32[]{:S(2)}) %collective-permute-start.16) | collective-permute-done | bytes 182816 | tf_op jit(solution)/shard_map/ppermute | solution.py:566
  620.8 3.1 copy_bitcast_fusion
  623.9 3.3 copy.134
  627.1 3.5 copy.170
  634.4 11.9 %collective-permute-done.22 = bf16[2,136,1088]{2,1,0:T(8,128)(2,1)} collective-permute-done((bf16[2,136,1088]{2,1,0:T(8,128)(2,1)}, bf16[2,136,1088]{2,1,0:T(8,128)(2,1)}, u32[]{:S(2)}, u32[]{:S(2)}) %collective-permute-start.22) | collective-permute-done | bytes 591904 | tf_op jit(solution)/shard_map/ppermute | solution.py:566
  648.5 2.3 copy-done.14
  651.4 3.4 collective-permute-start.25
  656.7 2.4 broadcast_select_fusion.1
  665.5 64.6 %psum.7 = f32[12,1088]{1,0:T(8,128)S(1)} all-reduce(f32[12,1088]{1,0:T(8,128)S(1)} %stack.108), channel_id=1, replica_groups=mesh['shard'=2,'context'=4,'tensor'=4] {'shard','context','tensor'}, use_global_device_ids=true, to_apply=%region_25.26 | all-reduce | flops 13056 | bytes 104448 | tf_op jit(solution)/shard_map/psum | solution.py:682
  731.5 2.2 convert_dynamic-update-slice_fusion.2
  733.7 2.2 convert_dynamic-update-slice_fusion.1
  735.9 2.2 convert_dynamic-update-slice_fusion
  738.1 5.1 slice_bitcast_fusion
  748.5 2.2 copy.147
  750.7 8.4 %concatenate.79 = f32[544,3264]{1,0:T(8,128)} concatenate(f32[544,1024]{1,0:T(8,128)} %bitcast.121, f32[544,64]{1,0:T(8,128)S(1)} %copy.144, f32[544,1024]{1,0:T(8,128)} %get-tuple-element.176, f32[544,64]{1,0:T(8,128)S(1)} %copy.145, f32[544,1024]{1,0:T(8,128)} %get-tuple-element.175, f32[544,64]{1,0:T(8,128)} %copy.146), dimensions={1} | concatenate | bytes 14204928 | tf_op jit(solution)/shard_map/concatenate | solution.py:659
  (378 shorter events, 116.8 us)
Async XLA Ops:
  0.6 153.5 %collective-permute-start.5 = (bf16[320,1088]{1,0:T(8,128)(2,1)}, bf16[320,1088]{1,0:T(8,128)(2,1)}, u32[]{:S(2)}, u32[]{:S(2)}) collective-permute-start(bf16[320,1088]{1,0:T(8,128)(2,1)} %param.19), channel_id=1, source_target_pairs={{0,1},{1,0},{2,3},{3,2},{4,5},{5,4},{6,7},{7,6},{8,9},{9,8},{10,11... | collective-permute-start | bytes 2088968 | tf_op jit(solution)/shard_map/ppermute | solution.py:532
  1.2 155.7 %collective-permute-start.6 = (bf16[320,1088]{1,0:T(8,128)(2,1)}, bf16[320,1088]{1,0:T(8,128)(2,1)}, u32[]{:S(2)}, u32[]{:S(2)}) collective-permute-start(bf16[320,1088]{1,0:T(8,128)(2,1)} %param.19), channel_id=1, source_target_pairs={{0,2},{1,3},{2,0},{3,1},{4,6},{5,7},{6,4},{7,5},{8,10},{9,11},{10,... | collective-permute-start | bytes 2088968 | tf_op jit(solution)/shard_map/ppermute | solution.py:532
  3.8 155.1 %collective-permute-start.7 = (bf16[320,1088]{1,0:T(8,128)(2,1)}, bf16[320,1088]{1,0:T(8,128)(2,1)}, u32[]{:S(2)}, u32[]{:S(2)}) collective-permute-start(bf16[320,1088]{1,0:T(8,128)(2,1)} %param.19), channel_id=1, source_target_pairs={{0,3},{1,2},{2,1},{3,0},{4,7},{5,6},{6,5},{7,4},{8,11},{9,10},{10,... | collective-permute-start | bytes 2088968 | tf_op jit(solution)/shard_map/ppermute | solution.py:532
  9.4 82.4 %collective-permute-start = (bf16[8,544]{1,0:T(8,128)(2,1)S(1)}, bf16[8,544]{1,0:T(8,128)(2,1)S(1)}, u32[]{:S(2)}, u32[]{:S(2)}) collective-permute-start(bf16[8,544]{1,0:T(8,128)(2,1)S(1)} %stack.97), channel_id=1, source_target_pairs={{0,16},{16,0},{1,17},{17,1},{2,18},{18,2},{3,19},{19,3},{4,20},{20... | collective-permute-start | bytes 26120 | tf_op jit(solution)/shard_map/ppermute | solution.py:73
  11.1 149.8 %collective-permute-start.2 = (bf16[544,1088]{1,0:T(8,128)(2,1)}, bf16[544,1088]{1,0:T(8,128)(2,1)}, u32[]{:S(2)}, u32[]{:S(2)}) collective-permute-start(bf16[544,1088]{1,0:T(8,128)(2,1)} %param.28), channel_id=1, source_target_pairs={{0,16},{16,0},{1,17},{17,1},{2,18},{18,2},{3,19},{19,3},{4,20},{20... | collective-permute-start | bytes 3551240 | tf_op jit(solution)/shard_map/ppermute | solution.py:73
  16.9 56.1 %copy-start.15 = (bf16[320,1088]{1,0:T(8,128)(2,1)S(1)}, bf16[320,1088]{1,0:T(8,128)(2,1)}, u32[]{:S(2)}) copy-start(bf16[320,1088]{1,0:T(8,128)(2,1)} %x.7) | copy-start | bytes 2088964
  16.9 56.3 %copy-start.66 = (s32[5120]{0:T(1024)S(1)}, s32[5120]{0:T(1024)}, u32[]{:S(2)}) copy-start(s32[5120]{0:T(1024)} %param.20) | copy-start | bytes 61444
  16.9 56.5 %copy-start.84 = (s32[52]{0:T(128)S(1)}, s32[52]{0:T(128)}, u32[]{:S(2)}) copy-start(s32[52]{0:T(128)} %param.22) | copy-start | bytes 628
  16.9 57.0 %copy-start.67 = (s32[5120]{0:T(1024)S(1)}, s32[5120]{0:T(1024)}, u32[]{:S(2)}) copy-start(s32[5120]{0:T(1024)} %param.21) | copy-start | bytes 61444
  16.9 57.3 %copy-start.28 = (bf16[320,1088]{1,0:T(8,128)(2,1)S(1)}, bf16[320,1088]{1,0:T(8,128)(2,1)}, u32[]{:S(2)}) copy-start(bf16[320,1088]{1,0:T(8,128)(2,1)} %param.19) | copy-start | bytes 2088964
  75.9 45.1 %copy-start.6 = (s32[20]{0:T(128)}, s32[20]{0:T(128)S(1)}, u32[]{:S(2)}) copy-start(s32[20]{0:T(128)S(1)} %select_reduce_fusion.order) | copy-start | bytes 244
  86.3 26.5 %copy-start.64 = (f32[320]{0:T(512)}, f32[320]{0:T(512)S(1)}, u32[]{:S(2)}) copy-start(f32[320]{0:T(512)S(1)} %broadcast_multiply_fusion.2) | copy-start | bytes 3844
  87.3 25.6 %copy-start.77 = (f32[320]{0:T(512)}, f32[320]{0:T(512)S(1)}, u32[]{:S(2)}) copy-start(f32[320]{0:T(512)S(1)} %fusion.68) | copy-start | bytes 3844
  90.2 30.8 %copy-start.5 = (s32[2,2560]{1,0:T(2,128)}, s32[2,2560]{1,0:T(2,128)S(1)}, u32[]{:S(2)}) copy-start(s32[2,2560]{1,0:T(2,128)S(1)} %pad_add_fusion.kinfo) | copy-start | bytes 61444
  91.1 29.9 %copy-start.3 = (s32[320,4]{1,0:T(8,128)}, s32[320,4]{1,0:T(8,128)S(1)}, u32[]{:S(2)}) copy-start(s32[320,4]{1,0:T(8,128)S(1)} %copy.150.qinfo) | copy-start | bytes 15364
  91.8 18.1 %collective-permute-start.1 = (bf16[544,576]{1,0:T(8,128)(2,1)S(1)}, bf16[544,576]{1,0:T(8,128)(2,1)}, u32[]{:S(2)}, u32[]{:S(2)}) collective-permute-start(bf16[544,576]{1,0:T(8,128)(2,1)S(1)} %concatenate.61), channel_id=1, source_target_pairs={{0,16},{16,0},{1,17},{17,1},{2,18},{18,2},{3,19},{19,3},{4,20},{20... | collective-permute-start | bytes 1880072 | tf_op jit(solution)/shard_map/ppermute | solution.py:73
  94.4 18.5 %copy-start.58 = (f32[1088]{0:T(1024)}, f32[1088]{0:T(1024)S(1)}, u32[]{:S(2)}) copy-start(f32[1088]{0:T(1024)S(1)} %get-tuple-element.145) | copy-start | bytes 13060
  94.4 18.5 %copy-start.60 = (f32[1088]{0:T(1024)}, f32[1088]{0:T(1024)S(1)}, u32[]{:S(2)}) copy-start(f32[1088]{0:T(1024)S(1)} %get-tuple-element.146) | copy-start | bytes 13060
  94.4 15.5 %copy-start.40 = (bf16[544,1088]{1,0:T(8,128)(2,1)S(1)}, bf16[544,1088]{1,0:T(8,128)(2,1)}, u32[]{:S(2)}) copy-start(bf16[544,1088]{1,0:T(8,128)(2,1)} %param.32) | copy-start | bytes 3551236
  102.2 11.2 %copy-start.85 = (f32[512]{0:T(512)S(1)}, f32[512]{0:T(512)}, u32[]{:S(2)}) copy-start(f32[512]{0:T(512)} %constant.141.clone.1) | copy-start | bytes 6148
  109.8 80.8 %collective-permute-start.3 = (bf16[544,1088]{1,0:T(8,128)(2,1)S(1)}, bf16[544,1088]{1,0:T(8,128)(2,1)}, u32[]{:S(2)}, u32[]{:S(2)}) collective-permute-start(bf16[544,1088]{1,0:T(8,128)(2,1)S(1)} %copy-done.40), channel_id=1, source_target_pairs={{0,16},{16,0},{1,17},{17,1},{2,18},{18,2},{3,19},{19,3},{4,20},{20... | collective-permute-start | bytes 3551240 | tf_op jit(solution)/shard_map/ppermute | solution.py:73
  113.4 7.6 %copy-start.4 = (bf16[320,128]{1,0:T(8,128)(2,1)}, bf16[320,128]{1,0:T(8,128)(2,1)S(1)}, u32[]{:S(2)}) copy-start(bf16[320,128]{1,0:T(8,128)(2,1)S(1)} %pad.12.q16) | copy-start | bytes 245764
  143.0 19.5 %copy-start.53 = (bf16[320,64]{1,0:T(8,128)(2,1)}, bf16[320,64]{1,0:T(8,128)(2,1)S(1)}, u32[]{:S(2)}) copy-start(bf16[320,64]{1,0:T(8,128)(2,1)S(1)} %slice.156) | copy-start | bytes 122884
  154.2 61.8 %collective-permute-start.4 = (bf16[1088,544]{0,1:T(8,128)(2,1)}, bf16[1088,544]{0,1:T(8,128)(2,1)}, u32[]{:S(2)}, u32[]{:S(2)}) collective-permute-start(bf16[1088,544]{0,1:T(8,128)(2,1)} %param.34), channel_id=1, source_target_pairs={{0,16},{16,0},{1,17},{17,1},{2,18},{18,2},{3,19},{19,3},{4,20},{20... | collective-permute-start | bytes 3551240 | tf_op jit(solution)/shard_map/ppermute | solution.py:73
  218.1 10.9 %copy-start.45 = (bf16[1088,544]{0,1:T(8,128)(2,1)}, bf16[1088,544]{0,1:T(8,128)(2,1)S(1)}, u32[]{:S(2)}) copy-start(bf16[1088,544]{0,1:T(8,128)(2,1)S(1)} %get-tuple-element.119) | copy-start | bytes 3551236
  218.1 10.8 %copy-start.47 = (bf16[1088,544]{0,1:T(8,128)(2,1)}, bf16[1088,544]{0,1:T(8,128)(2,1)S(1)}, u32[]{:S(2)}) copy-start(bf16[1088,544]{0,1:T(8,128)(2,1)S(1)} %get-tuple-element.120) | copy-start | bytes 3551236
  244.0 21.2 %copy-start.87 = (bf16[1280,1088]{0,1:T(8,128)(2,1)S(1)}, bf16[1280,1088]{0,1:T(8,128)(2,1)}, u32[]{:S(2)}) copy-start(bf16[1280,1088]{0,1:T(8,128)(2,1)} %get-tuple-element.99) | copy-start | bytes 8355844
  279.5 21.2 %copy-start.62 = (f32[1088]{0:T(1024)S(1)}, f32[1088]{0:T(1024)}, u32[]{:S(2)}) copy-start(f32[1088]{0:T(1024)} %get-tuple-element.150) | copy-start | bytes 13060
  349.4 32.1 %copy-start.35 = (bf16[2560,512]{1,0:T(8,128)(2,1)S(1)}, bf16[2560,512]{1,0:T(8,128)(2,1)}, u32[]{:S(2)}) copy-start(bf16[2560,512]{1,0:T(8,128)(2,1)} %get-tuple-element.32.x) | copy-start | bytes 7864324
  405.1 22.7 %slice-start = ((s8[5013504]{0:T(1024)(128)(4,1)}), s8[819200]{0:T(1024)(128)(4,1)S(1)}, s32[]{:S(2)}) async-start(s8[5013504]{0:T(1024)(128)(4,1)} %bitcast.115), calls=%async_computation | async-start | bytes 1638400
  409.4 16.3 %copy-start.23 = (f32[1088,384]{1,0:T(8,128)S(1)}, f32[1088,384]{1,0:T(8,128)}, u32[]{:S(2)}) copy-start(f32[1088,384]{1,0:T(8,128)} %fusion.25) | copy-start | bytes 5013508
  409.4 17.7 %copy-start.16 = (bf16[320,1088]{1,0:T(8,128)(2,1)S(1)}, bf16[320,1088]{1,0:T(8,128)(2,1)}, u32[]{:S(2)}) copy-start(bf16[320,1088]{1,0:T(8,128)(2,1)} %x.7) | copy-start | bytes 2088964
  409.4 17.6 %copy-start.55 = (bf16[320,128]{1,0:T(8,128)(2,1)S(1)}, bf16[320,128]{1,0:T(8,128)(2,1)}, u32[]{:S(2)}) copy-start(bf16[320,128]{1,0:T(8,128)(2,1)} %get-tuple-element.33) | copy-start | bytes 245764
  409.5 17.6 %copy-start.59 = (f32[1088]{0:T(1024)S(1)}, f32[1088]{0:T(1024)}, u32[]{:S(2)}) copy-start(f32[1088]{0:T(1024)} %copy-done.58) | copy-start | bytes 13060
  409.5 17.6 %copy-start.61 = (f32[1088]{0:T(1024)S(1)}, f32[1088]{0:T(1024)}, u32[]{:S(2)}) copy-start(f32[1088]{0:T(1024)} %copy-done.60) | copy-start | bytes 13060
  409.5 17.6 %copy-start.65 = (f32[320]{0:T(512)S(1)}, f32[320]{0:T(512)}, u32[]{:S(2)}) copy-start(f32[320]{0:T(512)} %copy-done.64) | copy-start | bytes 3844
  409.5 17.6 %copy-start.78 = (f32[320]{0:T(512)S(1)}, f32[320]{0:T(512)}, u32[]{:S(2)}) copy-start(f32[320]{0:T(512)} %copy-done.77) | copy-start | bytes 3844
  409.5 18.3 %slice-start.1 = ((s8[5013504]{0:T(1024)(128)(4,1)}), s8[4194304]{0:T(1024)(128)(4,1)S(1)}, s32[]{:S(2)}) async-start(s8[5013504]{0:T(1024)(128)(4,1)} %bitcast.115), calls=%async_computation.1 | async-start | bytes 8388608
  424.2 137.5 %collective-permute-start.8 = (bf16[272,3264]{1,0:T(8,128)(2,1)}, bf16[272,3264]{1,0:T(8,128)(2,1)}, u32[]{:S(2)}, u32[]{:S(2)}) collective-permute-start(bf16[272,3264]{1,0:T(8,128)(2,1)} %constant_dynamic-slice_fusion.1), channel_id=1, source_target_pairs={{0,16},{16,0},{1,17},{17,1},{2,18},{18,2},{3,19},{19,3},{4,20},{20... | collective-permute-start | bytes 5326856 | tf_op jit(solution)/shard_map/ppermute | solution.py:73
  426.6 49.1 %collective-permute-start.10 = (bf16[544,384]{1,0:T(8,128)(2,1)}, bf16[544,384]{1,0:T(8,128)(2,1)S(1)}, u32[]{:S(2)}, u32[]{:S(2)}) collective-permute-start(bf16[544,384]{1,0:T(8,128)(2,1)} %select_convert_fusion.5), channel_id=1, source_target_pairs={{0,16},{16,0},{1,17},{17,1},{2,18},{18,2},{3,19},{19,3},{4,20},{20... | collective-permute-start | bytes 1253384 | tf_op jit(solution)/shard_map/ppermute | solution.py:73
  429.3 49.8 %collective-permute-start.12 = (bf16[1088,672]{0,1:T(8,128)(2,1)}, bf16[1088,672]{0,1:T(8,128)(2,1)}, u32[]{:S(2)}, u32[]{:S(2)}) collective-permute-start(bf16[1088,672]{0,1:T(8,128)(2,1)} %select_convert_fusion), channel_id=1, source_target_pairs={{0,1},{1,0},{2,3},{3,2},{4,5},{5,4},{6,7},{7,6},{8,9},{9,8},{10,11... | collective-permute-start | bytes 4386824 | tf_op jit(solution)/shard_map/ppermute | solution.py:73
  439.2 36.5 %copy-start.24 = (f32[1088,384]{1,0:T(8,128)S(1)}, f32[1088,384]{1,0:T(8,128)}, u32[]{:S(2)}) copy-start(f32[1088,384]{1,0:T(8,128)} %fusion.25) | copy-start | bytes 5013508
  439.2 122.6 %collective-permute-start.20 = (bf16[2,544,1088]{2,1,0:T(8,128)(2,1)}, bf16[2,544,1088]{2,1,0:T(8,128)(2,1)}, u32[]{:S(2)}, u32[]{:S(2)}) collective-permute-start(bf16[2,544,1088]{2,1,0:T(8,128)(2,1)} %pad_maximum_fusion.4), channel_id=1, source_target_pairs={{0,16},{16,0},{1,17},{17,1},{2,18},{18,2},{3,19},{19,3},{4,20},{20... | collective-permute-start | bytes 7102472 | tf_op jit(solution)/shard_map/ppermute | solution.py:73
  445.2 34.0 %copy-start.32 = (f32[1088,192]{0,1:T(8,128)S(1)}, f32[1088,192]{0,1:T(8,128)}, u32[]{:S(2)}) copy-start(f32[1088,192]{0,1:T(8,128)} %copy-done.31) | copy-start | bytes 2506756
  476.5 20.6 %collective-permute-start.11 = (bf16[544,384]{1,0:T(8,128)(2,1)}, bf16[544,384]{1,0:T(8,128)(2,1)}, u32[]{:S(2)}, u32[]{:S(2)}) collective-permute-start(bf16[544,384]{1,0:T(8,128)(2,1)} %fusion.61), channel_id=1, source_target_pairs={{0,8},{4,12},{8,0},{12,4},{1,9},{5,13},{9,1},{13,5},{2,10},{6,14},... | collective-permute-start | bytes 1253384 | tf_op jit(solution)/shard_map/ppermute | solution.py:566
  486.0 11.1 %copy-start.25 = (f32[1088,384]{1,0:T(8,128)S(1)}, f32[1088,384]{1,0:T(8,128)}, u32[]{:S(2)}) copy-start(f32[1088,384]{1,0:T(8,128)} %fusion.25) | copy-start | bytes 5013508
  486.0 60.8 %collective-permute-start.13 = (bf16[544,672]{1,0:T(8,128)(2,1)}, bf16[544,672]{1,0:T(8,128)(2,1)}, u32[]{:S(2)}, u32[]{:S(2)}) collective-permute-start(bf16[544,672]{1,0:T(8,128)(2,1)} %copy.137), channel_id=1, source_target_pairs={{0,16},{16,0},{1,17},{17,1},{2,18},{18,2},{3,19},{19,3},{4,20},{20... | collective-permute-start | bytes 2193416 | tf_op jit(solution)/shard_map/ppermute | solution.py:73
  552.2 13.3 %collective-permute-start.14 = (bf16[272,672]{0,1:T(8,128)(2,1)S(1)}, bf16[272,672]{0,1:T(8,128)(2,1)}, u32[]{:S(2)}, u32[]{:S(2)}) collective-permute-start(bf16[272,672]{0,1:T(8,128)(2,1)S(1)} %select_convert_fusion.4), channel_id=1, source_target_pairs={{0,2},{1,3},{2,0},{3,1},{4,6},{5,7},{6,4},{7,5},{8,10},{9,11},{10,... | collective-permute-start | bytes 1096712 | tf_op jit(solution)/shard_map/ppermute | solution.py:73
  561.8 95.0 %collective-permute-start.9 = (bf16[272,3264]{1,0:T(8,128)(2,1)}, bf16[272,3264]{1,0:T(8,128)(2,1)}, u32[]{:S(2)}, u32[]{:S(2)}) collective-permute-start(bf16[272,3264]{1,0:T(8,128)(2,1)} %collective-permute-done.8), channel_id=1, source_target_pairs={{0,1},{1,0},{2,3},{3,2},{4,5},{5,4},{6,7},{7,6},{8,9},{9,8},{10,11... | collective-permute-start | bytes 5326856 | tf_op jit(solution)/shard_map/ppermute | solution.py:73
  567.1 8.9 %collective-permute-start.15 = (bf16[136,672]{0,1:T(8,128)(2,1)S(1)}, bf16[136,672]{0,1:T(8,128)(2,1)S(1)}, u32[]{:S(2)}, u32[]{:S(2)}) collective-permute-start(bf16[136,672]{0,1:T(8,128)(2,1)S(1)} %select_convert_fusion.6), channel_id=1, source_target_pairs={{0,4},{4,0},{8,12},{12,8},{1,5},{5,1},{9,13},{13,9},{2,6},{6,2},{1... | collective-permute-start | bytes 548360 | tf_op jit(solution)/shard_map/ppermute | solution.py:566
  576.2 44.2 %collective-permute-start.16 = (bf16[136,672]{0,1:T(8,128)(2,1)S(1)}, bf16[136,672]{0,1:T(8,128)(2,1)S(1)}, u32[]{:S(2)}, u32[]{:S(2)}) collective-permute-start(bf16[136,672]{0,1:T(8,128)(2,1)S(1)} %fusion.62), channel_id=1, source_target_pairs={{0,8},{4,12},{8,0},{12,4},{1,9},{5,13},{9,1},{13,5},{2,10},{6,14},... | collective-permute-start | bytes 548360 | tf_op jit(solution)/shard_map/ppermute | solution.py:566
  578.9 41.9 %copy-start.27 = (f32[544,8,128]{2,1,0:T(8,128)S(1)}, f32[544,8,128]{2,1,0:T(8,128)}, u32[]{:S(2)}) copy-start(f32[544,8,128]{2,1,0:T(8,128)} %copy.142) | copy-start | bytes 6684676
  580.2 40.5 %copy-start.26 = (f32[544,8,128]{2,1,0:T(8,128)S(1)}, f32[544,8,128]{2,1,0:T(8,128)}, u32[]{:S(2)}) copy-start(f32[544,8,128]{2,1,0:T(8,128)} %copy.143) | copy-start | bytes 6684676
  580.2 54.2 %collective-permute-start.23 = (bf16[2,136,1088]{2,1,0:T(8,128)(2,1)}, bf16[2,136,1088]{2,1,0:T(8,128)(2,1)S(1)}, u32[]{:S(2)}, u32[]{:S(2)}) collective-permute-start(bf16[2,136,1088]{2,1,0:T(8,128)(2,1)} %get-tuple-element.105), channel_id=1, source_target_pairs={{0,12},{4,8},{8,4},{12,0},{1,13},{5,9},{9,5},{13,1},{2,14},{6,10},... | collective-permute-start | bytes 1775624 | tf_op jit(solution)/shard_map/ppermute | solution.py:566
  581.4 64.9 %collective-permute-start.22 = (bf16[2,136,1088]{2,1,0:T(8,128)(2,1)}, bf16[2,136,1088]{2,1,0:T(8,128)(2,1)}, u32[]{:S(2)}, u32[]{:S(2)}) collective-permute-start(bf16[2,136,1088]{2,1,0:T(8,128)(2,1)} %get-tuple-element.104), channel_id=1, source_target_pairs={{0,8},{4,12},{8,0},{12,4},{1,9},{5,13},{9,1},{13,5},{2,10},{6,14},... | collective-permute-start | bytes 1775624 | tf_op jit(solution)/shard_map/ppermute | solution.py:566
  583.1 63.2 %collective-permute-start.21 = (bf16[2,136,1088]{2,1,0:T(8,128)(2,1)}, bf16[2,136,1088]{2,1,0:T(8,128)(2,1)}, u32[]{:S(2)}, u32[]{:S(2)}) collective-permute-start(bf16[2,136,1088]{2,1,0:T(8,128)(2,1)} %get-tuple-element.103), channel_id=1, source_target_pairs={{0,4},{4,0},{8,12},{12,8},{1,5},{5,1},{9,13},{13,9},{2,6},{6,2},{1... | collective-permute-start | bytes 1775624 | tf_op jit(solution)/shard_map/ppermute | solution.py:566
  620.7 11.4 %collective-permute-start.17 = (bf16[136,672]{0,1:T(8,128)(2,1)S(1)}, bf16[136,672]{0,1:T(8,128)(2,1)}, u32[]{:S(2)}, u32[]{:S(2)}) collective-permute-start(bf16[136,672]{0,1:T(8,128)(2,1)S(1)} %add_convert_fusion.4), channel_id=1, source_target_pairs={{0,4},{4,0},{8,12},{12,8},{1,5},{5,1},{9,13},{13,9},{2,6},{6,2},{1... | collective-permute-start | bytes 548360 | tf_op jit(solution)/shard_map/ppermute | solution.py:566
  633.3 13.4 %copy-start.13 = (f32[1,544,1088]{2,1,0:T(8,128)S(1)}, f32[1,544,1088]{2,1,0:T(8,128)}, u32[]{:S(2)}) copy-start(f32[1,544,1088]{2,1,0:T(8,128)} %copy-done.12) | copy-start | bytes 7102468
  633.3 21.9 %collective-permute-start.18 = (bf16[272,672]{0,1:T(8,128)(2,1)S(1)}, bf16[272,672]{0,1:T(8,128)(2,1)S(1)}, u32[]{:S(2)}, u32[]{:S(2)}) collective-permute-start(bf16[272,672]{0,1:T(8,128)(2,1)S(1)} %pad_maximum_fusion.17), channel_id=1, source_target_pairs={{0,2},{1,3},{2,0},{3,1},{4,6},{5,7},{6,4},{7,5},{8,10},{9,11},{10,... | collective-permute-start | bytes 1096712 | tf_op jit(solution)/shard_map/ppermute | solution.py:73
  634.4 11.9 %copy-start.49 = (bf16[2,136,1088]{2,1,0:T(8,128)(2,1)}, bf16[2,136,1088]{2,1,0:T(8,128)(2,1)S(1)}, u32[]{:S(2)}) copy-start(bf16[2,136,1088]{2,1,0:T(8,128)(2,1)S(1)} %collective-permute-done.23) | copy-start | bytes 1775620
  650.7 80.8 %collective-permute-start.24 = (bf16[2,136,1088]{2,1,0:T(8,128)(2,1)S(1)}, bf16[2,136,1088]{2,1,0:T(8,128)(2,1)}, u32[]{:S(2)}, u32[]{:S(2)}) collective-permute-start(bf16[2,136,1088]{2,1,0:T(8,128)(2,1)S(1)} %get-tuple-element.92), channel_id=1, source_target_pairs={{0,4},{4,0},{8,12},{12,8},{1,5},{5,1},{9,13},{13,9},{2,6},{6,2},{1... | collective-permute-start | bytes 1775624 | tf_op jit(solution)/shard_map/ppermute | solution.py:566
  651.4 82.3 %collective-permute-start.25 = (bf16[2,136,1088]{2,1,0:T(8,128)(2,1)S(1)}, bf16[2,136,1088]{2,1,0:T(8,128)(2,1)}, u32[]{:S(2)}, u32[]{:S(2)}) collective-permute-start(bf16[2,136,1088]{2,1,0:T(8,128)(2,1)S(1)} %get-tuple-element.92), channel_id=1, source_target_pairs={{0,8},{4,12},{8,0},{12,4},{1,9},{5,13},{9,1},{13,5},{2,10},{6,14},... | collective-permute-start | bytes 1775624 | tf_op jit(solution)/shard_map/ppermute | solution.py:566
  654.8 81.1 %collective-permute-start.26 = (bf16[2,136,1088]{2,1,0:T(8,128)(2,1)S(1)}, bf16[2,136,1088]{2,1,0:T(8,128)(2,1)}, u32[]{:S(2)}, u32[]{:S(2)}) collective-permute-start(bf16[2,136,1088]{2,1,0:T(8,128)(2,1)S(1)} %get-tuple-element.92), channel_id=1, source_target_pairs={{0,12},{4,8},{8,4},{12,0},{1,13},{5,9},{9,5},{13,1},{2,14},{6,10},... | collective-permute-start | bytes 1775624 | tf_op jit(solution)/shard_map/ppermute | solution.py:566
  656.7 86.5 %collective-permute-start.19 = (bf16[544,672]{1,0:T(8,128)(2,1)S(1)}, bf16[544,672]{1,0:T(8,128)(2,1)}, u32[]{:S(2)}, u32[]{:S(2)}) collective-permute-start(bf16[544,672]{1,0:T(8,128)(2,1)S(1)} %copy.139), channel_id=1, source_target_pairs={{0,1},{1,0},{2,3},{3,2},{4,5},{5,4},{6,7},{7,6},{8,9},{9,8},{10,11... | collective-permute-start | bytes 2193416 | tf_op jit(solution)/shard_map/ppermute | solution.py:73
  (60 other events, 165.1 us)

commit v2 on v1

v2 whole, which is shorter than its diff:
```python
import functools

import jax
import jax.numpy as jnp
from jax import lax
from jax.experimental import pallas as pl
from jax.experimental.pallas import tpu as pltpu
from jax.sharding import PartitionSpec as P

HEAD_DIM = 64
PAIR = 2 * HEAD_DIM
PIECE = 128
TRUNK = 8 * PIECE
BRANCH = 3 * PIECE
EPSILON = 1e-05
NEGATIVE = -1e30
F32 = jnp.float32
BF16 = jnp.bfloat16
VMEM = pl.BlockSpec(memory_space=pltpu.VMEM)
SMEM = pl.BlockSpec(memory_space=pltpu.SMEM)
ANY = pl.BlockSpec(memory_space=pl.ANY)
MESH = pl.DeviceIdType.MESH


def contract(left, right, left_dim, right_dim):
    return lax.dot_general(
        left, right, (((left_dim,), (right_dim,)), ((), ())), preferred_element_type=F32
    )


def flip(value, bit):
    low = 1 << bit
    return value + low - 2 * low * lax.rem(lax.div(value, low), 2)


def place():
    tensor, context = lax.axis_index("tensor"), lax.axis_index("context")
    return tensor, context, lax.rem(context, 2) * lax.axis_size("tensor") + tensor


def member(mask):
    tensor, context, _ = place()
    size = lax.axis_size("tensor")
    bits = size.bit_length() - 1
    for bit in range(bits):
        if mask >> bit & 1:
            tensor = flip(tensor, bit)
    if mask >> bits & 1:
        context = flip(context, 0)
    return {"context": context, "tensor": tensor}, lax.rem(context, 2) * size + tensor


def swap(value, axis, bit):
    size = lax.axis_size(axis)
    return lax.ppermute(value, axis, [(i, i ^ 1 << bit) for i in range(size)])


class Wires:
    def __init__(self, send, recv):
        self.send, self.recv, self.used = send, recv, 0

    def start(self, source, target, device):
        copy = pltpu.make_async_remote_copy(
            src_ref=source,
            dst_ref=target,
            send_sem=self.send.at[self.used],
            recv_sem=self.recv.at[self.used],
            device_id=device,
            device_id_type=MESH,
        )
        self.used += 1
        copy.start()
        return copy


def by_rows(rows, step, body, first=0):
    def run(i, carry):
        body(pl.ds(pl.multiple_of(first + i * step, step), step))
        return carry

    lax.fori_loop(0, rows // step, run, 0)


def norm_backward(values, grad, gain):
    average = jnp.mean(values, axis=1, keepdims=True)
    centered = values - average
    inverse = lax.rsqrt(jnp.mean(centered * centered, axis=1, keepdims=True) + EPSILON)
    normal = centered * inverse
    scaled = grad * gain
    result = inverse * (
        scaled
        - jnp.mean(scaled, axis=1, keepdims=True)
        - normal * jnp.mean(scaled * normal, axis=1, keepdims=True)
    )
    return result, jnp.sum(grad * normal, axis=0, keepdims=True), jnp.sum(grad, axis=0, keepdims=True)


def norm_forward(values, gain, shift):
    average = jnp.mean(values, axis=1, keepdims=True)
    centered = values - average
    spread = jnp.mean(centered * centered, axis=1, keepdims=True)
    return centered * lax.rsqrt(spread + EPSILON) * gain + shift


def project_kernel(
    tokens, w_qkv, half_vectors, w_fc, normed, mixed, query_last, vectors, weight, fc_other, everyone, seen, local_sem, send, recv
):
    tensor, context, me = place()
    shard = lax.axis_index("shard")
    members = 2 * lax.axis_size("tensor")
    rows, width = tokens.shape
    half = width // 2
    cut = rows // 2
    shared = width - HEAD_DIM
    across = {"shard": 1 - shard}
    wires = Wires(send, recv)
    turn = members // 2

    barrier = pltpu.get_barrier_semaphore()
    peers = [member(mask)[0] for mask in (1, 2, turn)] + [across]
    rest = [m for m in range(4, members) if m & 1 == 0 and m not in (turn, turn + 2)]
    for peer in peers:
        pl.semaphore_signal(barrier, inc=1, device_id=peer, device_id_type=MESH)
    pl.semaphore_wait(barrier, len(peers))
    assert not rest

    def slot(owner, first=0, size=rows):
        index = member(owner)[1] * rows + first
        return everyone.at[pl.ds(pl.multiple_of(index, 16), size)]

    def hand(source, target):
        return wires.start(source, source, member(target)[0])

    own = pltpu.make_async_copy(tokens, slot(0), local_sem.at[0])
    own.start()
    far = {m: wires.start(tokens, slot(0), member(m)[0]) for m in (2, turn)}
    vector_wire = wires.start(half_vectors, seen, across)
    close = {0: wires.start(tokens, slot(0), member(1)[0])}
    lane = lax.broadcasted_iota(jnp.int32, (1, PAIR), 1) < HEAD_DIM

    def choose(i, carry):
        r = pl.ds(pl.multiple_of(i * 32, 32), 32)
        to = pl.ds(pl.multiple_of(shard * half + i * 32, 32), 32)

        def window(start, size=PAIR):
            return w_qkv[r, pl.ds(pl.multiple_of(start, PAIR), size)]

        def turned(value):
            return pltpu.roll(value.astype(F32), HEAD_DIM, 1)

        weight[to, 0:PAIR] = window(me * PAIR)
        left, right = window(shared + me * PAIR), window(shared + (me + 1) * PAIR)
        weight[to, PAIR : 2 * PAIR] = jnp.where(lane, turned(left), turned(right)).astype(BF16)
        weight[to, 2 * PAIR : 3 * PAIR] = window(2 * width + me * PAIR)
        value = w_qkv[r, 2 * width + shared :]
        value = jnp.concatenate([value, value], axis=1)
        key = turned(w_qkv[r, 2 * width - PAIR : 2 * width])
        weight[to, 3 * PAIR : 4 * PAIR] = jnp.where(lane, key, value.astype(F32)).astype(BF16)
        query = w_qkv[r, shared : shared + PAIR]
        weight[to, 4 * PAIR :] = jnp.where(lane, query, jnp.zeros_like(query))
        return carry

    lax.fori_loop(0, half // 32, choose, 0)
    chosen = weight.at[pl.ds(pl.multiple_of(shard * half, half), half)]
    weight_wire = wires.start(chosen, chosen, across)

    vector_wire.wait_recv()
    vectors[...] = half_vectors[...] + seen[...]
    gain, shift = vectors[0:1, :], vectors[1:2, :]
    scale = HEAD_DIM ** (-0.5)
    pair_lanes = pl.ds(pl.multiple_of(me * PAIR, PAIR), PAIR)
    bias_query, bias_value = vectors[2:3, pair_lanes], vectors[3:4, pair_lanes]
    value_tail = vectors[3:4, shared:]
    bias_last = jnp.where(lane, 0.0, jnp.concatenate([value_tail, value_tail], axis=1))
    query_tail = vectors[2:3, shared:]
    query_tail = jnp.where(lane, jnp.concatenate([query_tail, query_tail], axis=1), 0.0)

    def normalise(owner, first=0, size=rows):
        index = member(owner)[1] * rows + first

        def run(i, carry):
            r = pl.ds(pl.multiple_of(index + i * 32, 32), 32)
            normed[r, :] = norm_forward(everyone[r, :].astype(F32), gain, shift).astype(BF16)
            return carry

        lax.fori_loop(0, size // 32, run, 0)

    def multiply(owner, first=0, size=rows):
        r = pl.ds(pl.multiple_of(member(owner)[1] * rows + first, 32), size)
        result = jnp.dot(normed[r, :], weight[:, 0 : 4 * PAIR], preferred_element_type=F32)
        mixed[r, 0:PAIR] = ((result[:, 0:PAIR] + bias_query) * scale).astype(BF16)
        mixed[r, PAIR : 2 * PAIR] = result[:, PAIR : 2 * PAIR].astype(BF16)
        mixed[r, 2 * PAIR : 3 * PAIR] = (result[:, 2 * PAIR : 3 * PAIR] + bias_value).astype(BF16)
        mixed[r, 3 * PAIR :] = (result[:, 3 * PAIR :] + bias_last).astype(BF16)

    own.wait()
    normalise(0)
    close[0].wait_recv()
    normalise(1)
    pieces = {}
    for m, other, first in ((2, turn, 0), (turn, 2, cut)):
        far[m].wait_recv()
        close[m] = hand(slot(m), 1)
        pieces[other] = hand(slot(m, first, cut), other)
    weight_wire.wait_recv()
    fc_wire = wires.start(w_fc, fc_other, across)
    multiply(0)
    last = jnp.dot(
        normed[pl.ds(pl.multiple_of(me * rows, 32), rows), :], weight[:, 4 * PAIR :], preferred_element_type=F32
    )
    query_last[...] = ((last + query_tail) * scale).astype(BF16)
    multiply(1)
    for m in (2, turn):
        normalise(m)
        multiply(m)
    for m in (2, turn):
        close[m].wait_recv()
        normalise(m ^ 1)
        multiply(m ^ 1)
    opposite = 2 ^ turn
    passed = []
    for m, first in ((turn, 0), (2, cut)):
        pieces[m].wait_recv()
        passed.append(hand(slot(opposite, first, cut), 1))
    normalise(opposite)
    multiply(opposite)
    for wire in passed:
        wire.wait_recv()
    normalise(opposite ^ 1)
    multiply(opposite ^ 1)
    fc_wire.wait_recv()
    for wire in list(far.values()) + list(close.values()) + list(pieces.values()) + passed + [vector_wire, weight_wire, fc_wire]:
        wire.wait_send()


def project(tokens, w_qkv, half_vectors, w_fc):
    rows, width = tokens.shape
    tree = 2 * lax.axis_size("tensor") * rows
    shape = jax.ShapeDtypeStruct
    return pl.pallas_call(
        project_kernel,
        in_specs=[VMEM] * 3 + [ANY],
        out_specs=[VMEM] * 5 + [ANY],
        out_shape=[
            shape((tree, width), BF16),
            shape((tree, 4 * PAIR), BF16),
            shape((rows, PAIR), BF16),
            shape(half_vectors.shape, F32),
            shape((width, 5 * PAIR), BF16),
            shape(w_fc.shape, BF16),
        ],
        scratch_shapes=[
            pltpu.VMEM((tree, width), BF16),
            pltpu.VMEM(half_vectors.shape, F32),
            pltpu.SemaphoreType.DMA((1,)),
            pltpu.SemaphoreType.DMA((16,)),
            pltpu.SemaphoreType.DMA((16,)),
        ],
        compiler_params=pltpu.CompilerParams(
            collective_id=0, has_side_effects=True, vmem_limit_bytes=32 << 20
        ),
        name="project",
    )(tokens, w_qkv, half_vectors, w_fc)


def feed_forward_kernel(
    pair,
    last,
    tokens,
    cotangent,
    cotangent_far,
    out_mine,
    fc_mine,
    fc_other,
    proj_mine,
    proj_other,
    vectors,
    bias_fc,
    residual,
    fed_give,
    d_middle,
    d_pair,
    d_last,
    joint_keep,
    joint_give,
    fc_keep,
    fc_give,
    proj_sum,
    sums,
    w_out,
    w_fc,
    w_proj,
    attended,
    middle,
    normed,
    hidden,
    d_before,
    d_hidden,
    part,
    near,
    passing,
    far,
    d_attn,
    d_attended,
    grads,
    proj_keep,
    proj_give,
    proj_got,
    joint,
    joint_near,
    local_sem,
    send,
    recv,
):
    tensor, context, me = place()
    shard = lax.axis_index("shard")
    near_bit = lax.rem(tensor, 2)
    members = 2 * lax.axis_size("tensor")
    rows, width = tokens.shape
    half = width // 2
    shared = width - HEAD_DIM
    group = range(1, members)
    wires = Wires(send, recv)
    bias_out, gain, shift, bias_proj = (vectors[i : i + 1, :] for i in (4, 5, 6, 7))
    across = {"shard": 1 - shard}

    barrier = pltpu.get_barrier_semaphore()
    peers = [member(mask)[0] for mask in group] + [across]
    for peer in peers:
        pl.semaphore_signal(barrier, inc=1, device_id=peer, device_id_type=MESH)
    pl.semaphore_wait(barrier, len(peers))

    def slab(ref, index, size):
        return ref.at[pl.ds(pl.multiple_of(index * size, size), size)]

    def beside(ref, index):
        return ref.at[:, pl.ds(pl.multiple_of(index * PAIR, PAIR), PAIR)]

    moved = []
    for mask in group:
        device, index = member(mask)
        moved.append(wires.start(slab(pair, index, rows), beside(attended, me), device))
    quarter = half // 2
    out_wire = wires.start(
        slab(out_mine, near_bit, quarter), slab(w_out, 2 * shard + near_bit, quarter), across
    )
    local = [
        pltpu.make_async_copy(source, target, local_sem.at[i])
        for i, (source, target) in enumerate(
            (
                (slab(pair, me, rows), beside(attended, me)),
                (out_mine, slab(w_out, shard, half)),
                (fc_mine, slab(w_fc, shard, half)),
                (fc_other, slab(w_fc, 1 - shard, half)),
                (proj_mine, slab(w_proj, shard, half)),
                (proj_other, slab(w_proj, 1 - shard, half)),
                (cotangent, slab(grads, 0, rows)),
                (cotangent_far, slab(grads, 2, rows)),
            )
        )
    ]
    pulled_wires = [
        wires.start(source, slab(grads, index, rows), member(1)[0])
        for index, source in ((1, cotangent), (3, cotangent_far))
    ]
    for copy in local:
        copy.start()
    attended[:, shared:] = last[:, 0:HEAD_DIM]
    out_wire.wait_recv()
    out_part = slab(w_out, 2 * (1 - shard) + near_bit, quarter)
    out_near = wires.start(out_part, out_part, member(1)[0])
    for copy in local:
        copy.wait()
    for wire in moved + [out_near]:
        wire.wait_recv()

    start = 0
    while start < width:
        stop = min(start + 2 * PAIR, width)
        middle[:, start:stop] = (
            tokens[:, start:stop].astype(F32)
            + jnp.dot(attended[...], w_out[:, start:stop], preferred_element_type=F32)
            + bias_out[:, start:stop]
        )
        start = stop

    def second_norm(r):
        normed[r, :] = norm_forward(middle[r, :], gain, shift).astype(BF16)

    cut = rows // 2

    def piece(mask, i):
        return slice(mask * rows + i * cut, mask * rows + (i + 1) * cut)

    cross = []
    for i in range(2):
        by_rows(cut, 32, second_norm, i * cut)
        cross.append(wires.start(normed.at[piece(0, i)], normed.at[piece(2, i)], member(2)[0]))

    def block(ref, mask):
        return ref.at[mask * rows : (mask + 1) * rows, :]

    close = wires.start(block(normed, 0), block(normed, 1), member(1)[0])
    for wire in pulled_wires:
        wire.wait_recv()
    for mask in range(4):
        block(d_hidden, mask)[...] = jnp.dot(
            block(grads, mask)[...], w_proj[...], preferred_element_type=F32
        )

    def feed(r):
        start = 0
        while start < width:
            stop = min(start + 2 * PAIR, width)
            c = slice(start, stop)
            before = jnp.dot(normed[r, :], w_fc[:, c], preferred_element_type=F32) + bias_fc[0:1, c]
            cumulative = 0.5 + 0.5 * lax.erf(before * (0.5**0.5))
            hidden[r, c] = (before * cumulative).astype(BF16)
            slope = cumulative + before * jnp.exp(-0.5 * before * before) * ((2 * jnp.pi) ** -0.5)
            d_before[r, c] = (d_hidden[r, c] * slope).astype(BF16)
            start = stop

    def back(r):
        return contract(d_before[r, :], w_fc[...], 1, 1)

    def ahead(mask):
        return contract(hidden[mask * rows : (mask + 1) * rows, :], w_proj[...], 1, 1)

    feed(slice(0, rows))
    close.wait_recv()
    feed(slice(rows, 2 * rows))
    part[0] = back(slice(rows, 2 * rows)).astype(BF16)
    to_near = wires.start(part.at[0], near.at[0], member(1)[0])
    relay, to_pass, to_far = [], [], []
    for i in range(2):
        h = slice(i * cut, (i + 1) * cut)
        cross[i].wait_recv()
        relay.append(wires.start(normed.at[piece(2, i)], normed.at[piece(3, i)], member(1)[0]))
        feed(piece(2, i))
        relay[i].wait_recv()
        feed(piece(3, i))
        part[1, h] = back(piece(3, i)).astype(BF16)
        to_pass.append(wires.start(part.at[1, h], near.at[1, h], member(1)[0]))
        mine = back(piece(2, i))
        to_pass[i].wait_recv()
        passing[h] = (mine + near[1, h].astype(F32)).astype(BF16)
        to_far.append(wires.start(passing.at[h], far.at[h], member(2)[0]))

    other_part = pl.ds(pl.multiple_of(2 * rows + (1 - shard) * half, 8), half)
    own_part = pl.ds(pl.multiple_of(2 * rows + shard * half, 8), half)
    proj_wires = []
    start = 0
    while start < width:
        stop = min(start + 2 * PAIR, width)
        c = slice(start, stop)
        d_hidden_part = d_hidden.at[2 * rows : 2 * rows + width, 0 : stop - start]
        d_hidden_part[...] = contract(grads[...], hidden[:, c], 0, 0)
        proj_give[:, c] = d_hidden[other_part, 0 : stop - start].astype(BF16)
        proj_wires.append(wires.start(proj_give.at[:, c], proj_got.at[:, c], across))
        proj_keep[:, c] = d_hidden[own_part, 0 : stop - start]
        start = stop
    start = 0
    while start < width:
        stop = min(start + 2 * PAIR, width)
        c = slice(start, stop)
        d_hidden_part = d_hidden.at[2 * rows : 2 * rows + width, 0 : stop - start]
        d_hidden_part[...] = contract(normed[...], d_before[:, c], 0, 0)
        fc_give[:, c] = d_hidden[other_part, 0 : stop - start].astype(BF16)
        fc_keep[:, c] = d_hidden[own_part, 0 : stop - start].astype(BF16)
        start = stop
    d_hidden[0:rows, :] = back(slice(0, rows))
    to_near.wait_recv()
    for wire in to_far:
        wire.wait_recv()

    sums[...] = jnp.zeros_like(sums)

    def second_back(r):
        grad = d_hidden[r, :] + near[0, r, :].astype(F32) + far[r, :].astype(F32)
        result, by_gain, by_shift = norm_backward(middle[r, :], grad, gain)
        pulled = cotangent[r, :].astype(F32)
        result = result + pulled
        d_middle[r, :] = result
        low = result.astype(BF16)
        d_attn[r, 0:width] = low
        d_attn[r, width:] = jnp.zeros((r.size, d_attn.shape[1] - width), BF16)
        sums[4:5, :] += jnp.sum(low.astype(F32), axis=0, keepdims=True)
        sums[5:6, :] += by_gain
        sums[6:7, :] += by_shift
        sums[7:8, :] += jnp.sum(pulled, axis=0, keepdims=True)

    by_rows(rows, 64, second_back)
    start = 0
    while start < width:
        stop = min(start + 2 * PAIR, width)
        d_attended[:, start:stop] = contract(d_attn[:, 0:width], w_out[start:stop, :], 1, 1).astype(BF16)
        start = stop
    returned = []
    for mask in group:
        device, index = member(mask)
        returned.append(wires.start(beside(d_attended, index), slab(d_pair, me, rows), device))
    own_copy = pltpu.make_async_copy(beside(d_attended, me), slab(d_pair, me, rows), local_sem.at[0])
    own_copy.start()
    lane = lax.broadcasted_iota(jnp.int32, (1, PAIR), 1) >= HEAD_DIM
    tail = jnp.concatenate([d_attended[:, shared:]] * 2, axis=1)
    d_last[...] = jnp.where(lane, tail, jnp.zeros_like(tail))
    joint[:, shared : shared + PAIR] = jnp.zeros((width, PAIR), BF16)
    start = 0
    while start < d_attn.shape[1]:
        stop = min(start + 2 * PAIR, d_attn.shape[1])
        to = start if start < shared else start + PAIR
        joint[:, to : to + stop - start] = contract(attended[...], d_attn[:, start:stop], 0, 0).astype(BF16)
        start = stop
    side = joint.shape[1] // 2
    kept = pl.ds(pl.multiple_of(near_bit * side, side), side)
    given = pl.ds(pl.multiple_of((1 - near_bit) * side, side), side)
    joint_wire = wires.start(joint.at[:, given], joint_near, member(1)[0])
    part[2] = ahead(3).astype(BF16)
    to_pass_out = wires.start(part.at[2], near.at[3], member(1)[0])
    part[3] = ahead(1).astype(BF16)
    to_near_out = wires.start(part.at[3], near.at[2], member(1)[0])
    d_hidden[2 * rows : 3 * rows, :] = ahead(2)
    d_hidden[rows : 2 * rows, :] = ahead(0)
    bias = jnp.zeros((1, width), F32)

    def add_bias(i, total):
        r = pl.ds(pl.multiple_of(i * 64, 64), 64)
        return total + jnp.sum(d_before[r, :].astype(F32), axis=0, keepdims=True)

    bias = lax.fori_loop(0, 4 * rows // 64, add_bias, bias)
    for i in range(lax.axis_size("tensor")):
        sums[8 + i : 9 + i, :] = jnp.where(tensor == i, bias, 0.0)
    to_near_out.wait_recv()
    to_pass_out.wait_recv()

    def finish_output(r):
        third = pl.ds(pl.multiple_of(2 * rows + r.start, 64), r.size)
        again = pl.ds(pl.multiple_of(rows + r.start, 64), r.size)
        fed_give[r, :] = (d_hidden[third, :] + near[3, r, :].astype(F32)).astype(BF16)
        residual[r, :] = middle[r, :] + d_hidden[again, :] + near[2, r, :].astype(F32) + bias_proj

    by_rows(rows, 64, finish_output)
    joint_wire.wait_recv()
    second = lax.rem(lax.div(tensor, 2), 2)

    def add_joint(target, which):
        for i in range(2):

            def run(r):
                source = pl.ds(pl.multiple_of((2 * i + which) * quarter - i * quarter + r.start, 16), r.size)
                total = joint[source, kept].astype(F32) + joint_near[source, :].astype(F32)
                target[r, :] = total.astype(BF16)

            by_rows(quarter, 16, run, i * quarter)

    add_joint(joint_keep, second)
    add_joint(joint_give, 1 - second)
    for wire in proj_wires:
        wire.wait_recv()

    def add_proj(r):
        proj_sum[r, :] = (proj_keep[r, :] + proj_got[r, :].astype(F32)).astype(BF16)

    by_rows(half, 32, add_proj)
    own_copy.wait()
    for wire in returned:
        wire.wait_recv()
    for wire in (
        moved + returned + [out_wire, out_near] + pulled_wires + proj_wires
        + cross + relay + to_pass + to_far + [joint_wire, close, to_near, to_near_out, to_pass_out]
    ):
        wire.wait_send()


def feed_forward(pair, last, tokens, cotangent, cotangent_far, out_mine, fc_mine, fc_other, proj_mine, proj_other, vectors, bias_fc):
    rows, width = tokens.shape
    members = 2 * lax.axis_size("tensor")
    hidden = fc_mine.shape[1]
    tall = 4 * rows
    shape = jax.ShapeDtypeStruct
    return pl.pallas_call(
        feed_forward_kernel,
        in_specs=[ANY] + [VMEM] * 4 + [ANY] * 5 + [VMEM] * 2,
        out_specs=[VMEM] * 3 + [ANY] + [VMEM] * 7,
        out_shape=[
            shape((rows, width), F32),
            shape((rows, width), BF16),
            shape((rows, width), F32),
            shape((members * rows, PAIR), BF16),
            shape((rows, PAIR), BF16),
            shape((width // 2, 5 * PAIR), BF16),
            shape((width // 2, 5 * PAIR), BF16),
            shape((width // 2, hidden), BF16),
            shape((width // 2, hidden), BF16),
            shape((width // 2, hidden), BF16),
            shape((16, width), F32),
        ],
        scratch_shapes=[
            pltpu.VMEM((width, width), BF16),
            pltpu.VMEM((width, hidden), BF16),
            pltpu.VMEM((width, hidden), BF16),
            pltpu.VMEM((rows, width), BF16),
            pltpu.VMEM((rows, width), F32),
            pltpu.VMEM((tall, width), BF16),
            pltpu.VMEM((tall, hidden), BF16),
            pltpu.VMEM((tall, hidden), BF16),
            pltpu.VMEM((2 * rows + max(2 * rows, width), hidden), F32),
            pltpu.VMEM((4, rows, width), BF16),
            pltpu.VMEM((4, rows, width), BF16),
            pltpu.VMEM((rows, width), BF16),
            pltpu.VMEM((rows, width), BF16),
            pltpu.VMEM((rows, 9 * PAIR), BF16),
            pltpu.VMEM((rows, width), BF16),
            pltpu.VMEM((tall, width), BF16),
            pltpu.VMEM((width // 2, hidden), F32),
            pltpu.VMEM((width // 2, hidden), BF16),
            pltpu.VMEM((width // 2, hidden), BF16),
            pltpu.VMEM((width, 10 * PAIR), BF16),
            pltpu.VMEM((width, 5 * PAIR), BF16),
            pltpu.SemaphoreType.DMA((8,)),
            pltpu.SemaphoreType.DMA((2 * members + 20,)),
            pltpu.SemaphoreType.DMA((2 * members + 20,)),
        ],
        compiler_params=pltpu.CompilerParams(
            collective_id=3, has_side_effects=True, vmem_limit_bytes=62 << 20
        ),
        name="feed_forward",
    )(pair, last, tokens, cotangent, cotangent_far, out_mine, fc_mine, fc_other, proj_mine, proj_other, vectors, bias_fc)


def finish_kernel(
    d_mixed,
    d_query_last,
    normed,
    weight,
    tokens,
    d_middle,
    gain,
    joint_keep,
    joint_other,
    vectors,
    residual,
    fed_give,
    output,
    d_tokens,
    own_mixer,
    own_out,
    sums,
    near_give,
    near_got,
    row_sum,
    second_got,
    turn_got,
    second_last,
    turn_last,
    last_low,
    fed_got,
    pair_t,
    pair,
    pair_give,
    pair_got,
    pair_low,
    pair_seen,
    pairs,
    tail,
    tail_near,
    tail_sum,
    tail_give,
    tail_got,
    joint_give,
    joint_got,
    half_low,
    half_seen,
    joint_all,
    pair_sum,
    half_sum,
    vec,
    vec_give,
    vec_got,
    mixer_rows,
    mixer_sem,
    send,
    recv,
):
    tensor, context, me = place()
    shard = lax.axis_index("shard")
    near = lax.rem(tensor, 2)
    second = lax.rem(lax.div(tensor, 2), 2)
    contexts = lax.axis_size("context")
    members = 2 * lax.axis_size("tensor")
    turn = members // 2
    rows, width = tokens.shape
    half = width // 2
    quarter = half // 2
    cut = rows // 2
    side = joint_keep.shape[1]
    shared = width - HEAD_DIM
    block = 4 * PAIR
    across = {"shard": 1 - shard}
    higher = [
        {"context": flip(context, bit)} for bit in range(1, contexts.bit_length() - 1)
    ]
    group = range(1, members)
    wires = Wires(send, recv)
    lane = lax.broadcasted_iota(jnp.int32, (1, PAIR), 1) < HEAD_DIM

    barrier = pltpu.get_barrier_semaphore()
    peers = [member(mask)[0] for mask in group] + [across] + higher
    for peer in peers:
        pl.semaphore_signal(barrier, inc=1, device_id=peer, device_id_type=MESH)
    pl.semaphore_wait(barrier, len(peers))

    def part(ref, index, size):
        return ref.at[pl.ds(pl.multiple_of(index * size, size), size)]

    def term(mask):
        r = pl.ds(pl.multiple_of(member(mask)[1] * rows, rows), rows)
        return contract(d_mixed[r, :], weight[:, 0:block], 1, 1)

    steps = d_mixed.shape[0] // (2 * rows)
    pair_t[...] = jnp.zeros_like(pair_t)

    def accumulate(i, carry):
        r = pl.ds(pl.multiple_of(i * 2 * rows, 2 * rows), 2 * rows)
        pair_t[...] += contract(d_mixed[r, :], normed[r, :], 0, 0)
        return carry

    lax.fori_loop(0, steps, accumulate, 0)
    pair[...] = pair_t[...].T
    other = pl.ds(pl.multiple_of((1 - shard) * half, half), half)
    own = pl.ds(pl.multiple_of(shard * half, half), half)
    pair_give[...] = pair[other, 0 : 3 * PAIR].astype(BF16)
    pair_wire = wires.start(pair_give, pair_got, across)
    mine = pl.ds(pl.multiple_of(me * rows, rows), rows)
    tail[:, 0:PAIR] = pair[:, 3 * PAIR :].astype(BF16)
    tail[:, PAIR:] = contract(d_query_last[...], normed[mine, :], 0, 0).T.astype(BF16)
    tail_near_wire = wires.start(tail, tail_near, member(1)[0])

    order = [6, 2, 4, 0]
    near_wires = {}
    for i, mask in enumerate(order):
        near_give[i] = term(mask ^ 1).astype(BF16)
        near_wires[mask] = wires.start(near_give.at[i], near_got.at[i], member(1)[0])

    tail_near_wire.wait_recv()

    def add_tail_near(r):
        tail_sum[r, :] = tail[r, :].astype(F32) + tail_near[r, :].astype(F32)

    by_rows(width, 64, add_tail_near)
    to_second, to_turn = member(2)[0], member(turn)[0]
    for i in range(2):
        source = pl.ds(pl.multiple_of(i * half + (1 - second) * quarter, 16), quarter)
        tail_give[i * quarter : (i + 1) * quarter, :] = tail_sum[source, :].astype(BF16)
    tail_wire = wires.start(tail_give, tail_got, to_second)

    first = slice(0, cut)
    rest = slice(cut, rows)
    second_wires, turn_wires = [], []
    for i, mask in enumerate(order):
        total = term(mask)
        if mask == 0:
            query = pltpu.roll(d_query_last[...].astype(F32), HEAD_DIM, 1).astype(BF16)
            total = total + contract(query, weight[:, block:], 1, 1)
        near_wires[mask].wait_recv()
        total = total + near_got[i].astype(F32)
        if i:
            row_sum[i - 1] = total
        if mask:
            near_got[i] = total.astype(BF16)
        if mask & 2:
            second_wires.append(
                wires.start(near_got.at[i, first], second_got.at[len(second_wires)], to_second)
            )
        if mask & turn:
            turn_wires.append(wires.start(near_got.at[i, rest], turn_got.at[len(turn_wires)], to_turn))

    pair_wire.wait_recv()
    pair_own = pair[own, 0 : 3 * PAIR] + pair_got[...].astype(F32)
    pair_wires = []
    for i, device in enumerate(higher):
        pair_low[i] = pair_own.astype(BF16)
        wire = wires.start(pair_low.at[i], pair_seen.at[i], device)
        pair_wires.append(wire)
        if i < len(higher) - 1:
            wire.wait_recv()
            pair_own = pair_own + pair_seen[i].astype(F32)
    pair_sum[...] = pair_own

    tail_wire.wait_recv()
    wide = joint_keep.shape[1] - 2 * PAIR

    def joint_term(which):
        r = pl.ds(pl.multiple_of(which * quarter, quarter), quarter)
        s = pl.ds(pl.multiple_of(which * half + second * quarter, quarter), quarter)
        total = joint_keep[r, :].astype(F32) + joint_other[r, :].astype(F32)
        last = jnp.where(near == 1, tail_sum[s, :] + tail_got[r, :].astype(F32), 0.0)
        return jnp.concatenate([total[:, :wide], total[:, wide:] + last], axis=1)

    joint_give[...] = joint_term(1 - shard).astype(BF16)
    joint_wire = wires.start(joint_give, joint_got, across)

    vec[...] = vectors[...]

    def add_columns(i, total):
        r = pl.ds(pl.multiple_of(i * 64, 64), 64)
        return total + jnp.sum(d_mixed[r, :].astype(F32), axis=0, keepdims=True)

    columns = lax.fori_loop(0, d_mixed.shape[0] // 64, add_columns, jnp.zeros((1, block), F32))
    pair_lanes = pl.ds(pl.multiple_of(me * PAIR, PAIR), PAIR)
    vec[2:3, pair_lanes] = columns[:, 0:PAIR]
    vec[3:4, pair_lanes] = columns[:, 2 * PAIR : 3 * PAIR]
    query = jnp.sum(d_query_last[...].astype(F32), axis=0, keepdims=True)
    vec[2:3, shared:] = pltpu.roll(query, HEAD_DIM, 1)[:, :HEAD_DIM]
    vec[3:4, shared:] = pltpu.roll(columns[:, 3 * PAIR :], HEAD_DIM, 1)[:, :HEAD_DIM]

    joint_wire.wait_recv()
    half_sum[...] = joint_term(shard) + joint_got[...].astype(F32)
    hops = [to_turn] + higher
    joint_wires = []

    def joint_hop(i):
        if i:
            joint_wires[-1].wait_recv()
            half_sum[...] += half_seen[i - 1].astype(F32)
        if i < len(hops):
            half_low[i] = half_sum[...].astype(BF16)
            joint_wires.append(wires.start(half_low.at[i], half_seen.at[i], hops[i]))

    joint_hop(0)

    second_wires[0].wait_recv()
    last_low[0] = (row_sum[1, first] + second_got[0].astype(F32)).astype(BF16)
    turn_wires.append(wires.start(last_low.at[0], turn_last, to_turn))
    turn_wires[0].wait_recv()
    last_low[1] = (row_sum[0, rest] + turn_got[0].astype(F32)).astype(BF16)
    second_wires.append(wires.start(last_low.at[1], second_last, to_second))

    for i in range(1, len(hops)):
        joint_hop(i)

    if pair_wires:
        pair_wires[-1].wait_recv()
        pair_sum[...] += pair_seen[len(higher) - 1].astype(F32)

    def slot(owner, start=0, size=half):
        return pairs.at[pl.ds(pl.multiple_of(member(owner)[1] * half + start, 16), size)]

    def hand(source, target):
        return wires.start(source, source, member(target)[0])

    pairs[pl.ds(pl.multiple_of(me * half, half), half), :] = pair_sum[...].astype(BF16)
    far = {mask: hand(slot(0), mask) for mask in (2, turn)}
    close = {0: hand(slot(0), 1)}

    second_wires[1].wait_recv()
    second_wires[2].wait_recv()
    turn_wires[1].wait_recv()
    turn_wires[2].wait_recv()
    row_sum[2, first] = row_sum[2, first] + second_got[1].astype(F32) + turn_last[...].astype(F32)
    row_sum[2, rest] = row_sum[2, rest] + turn_got[1].astype(F32) + second_last[...].astype(F32)

    def first_norm(r):
        result, by_gain, by_shift = norm_backward(tokens[r, :].astype(F32), row_sum[2, r, :], gain[0:1, :])
        d_tokens[r, :] = result + d_middle[r, :]
        vec[0:1, :] += by_gain
        vec[1:2, :] += by_shift

    by_rows(rows, 64, first_norm)
    vec_wires = []

    def vec_send(i, device):
        vec_give[i] = vec[...]
        vec_wires.append(wires.start(vec_give.at[i], vec_got.at[i], device))

    def vec_add():
        i = len(vec_wires) - 1
        vec_wires[i].wait_recv()
        vec[...] += vec_got[i]

    vec_stops = [member(1)[0], to_second, to_turn, across] + higher
    vec_send(0, vec_stops[0])

    pieces = {}
    for mask, onward, start in ((2, turn, 0), (turn, 2, quarter)):
        far[mask].wait_recv()
        close[mask] = hand(slot(mask), 1)
        pieces[onward] = hand(slot(mask, start, quarter), onward)
    vec_add()
    vec_send(1, vec_stops[1])

    joint_hop(len(hops))
    keep = pl.ds(pl.multiple_of(second * quarter, quarter), quarter)
    kept = pl.ds(pl.multiple_of(near * side, side), side)
    joint_all[keep, kept] = half_sum[...].astype(BF16)
    joint_mine = joint_all.at[keep, kept]
    back = wires.start(joint_mine, joint_mine, to_second)
    vec_add()
    vec_send(2, vec_stops[2])
    fed_wire = wires.start(fed_give, fed_got, to_second)
    opposite = 2 ^ turn
    passed = []
    for mask, start in ((turn, 0), (2, quarter)):
        pieces[mask].wait_recv()
        passed.append(hand(slot(opposite, start, quarter), 1))
    vec_add()
    vec_send(3, vec_stops[3])
    back.wait_recv()
    joint_side = joint_all.at[:, kept]
    back_near = wires.start(joint_side, joint_side, member(1)[0])
    vec_add()
    for i in range(4, len(vec_stops)):
        vec_send(i, vec_stops[i])
        vec_add()
    sums[...] = vec[...]
    fed_wire.wait_recv()

    def add_fed(r):
        output[r, :] = (residual[r, :] + fed_got[r, :].astype(F32)).astype(BF16)

    by_rows(rows, 64, add_fed)
    for wire in list(close.values()) + passed:
        wire.wait_recv()
    back_near.wait_recv()

    tall = mixer_rows.shape[1]

    def mixer_copy(i, j):
        r = pl.ds(pl.multiple_of((2 * i + j) * tall, tall), tall)
        return pltpu.make_async_copy(mixer_rows.at[j], own_mixer.at[r], mixer_sem.at[j])

    def write(i, carry):
        for j in range(2):

            @pl.when(i > 0)
            def _():
                mixer_copy(i - 1, j).wait()

            start = (2 * i + j) * tall
            r = pl.ds(pl.multiple_of(start, tall), tall)
            own_out[r, 0:shared] = joint_all[r, 0:shared].astype(F32)
            eighth = joint_all[r, shared : shared + PAIR].astype(F32)
            ninth = joint_all[r, shared + PAIR :].astype(F32)
            own_out[r, shared:] = ninth[:, :HEAD_DIM]
            keys = []
            for k in range(members):
                value = pairs[pl.ds(pl.multiple_of(k * half + start, tall), tall), :].astype(F32)
                mixer_rows[j, :, k * PAIR : (k + 1) * PAIR] = value[:, 0:PAIR]
                mixer_rows[j, :, 2 * width + k * PAIR : 2 * width + (k + 1) * PAIR] = value[:, 2 * PAIR :]
                keys.append(value[:, PAIR : 2 * PAIR])
            keys = jnp.concatenate(keys + [jnp.where(lane, eighth, ninth)], axis=1)
            mixer_rows[j, :, shared : 2 * width] = pltpu.roll(keys, HEAD_DIM, 1)
            mixer_rows[j, :, 2 * width + shared :] = pltpu.roll(eighth, HEAD_DIM, 1)[:, :HEAD_DIM]
            mixer_copy(i, j).start()
        return carry

    trips = half // (2 * tall)
    lax.fori_loop(0, trips, write, 0)
    for j in range(2):
        mixer_copy(trips - 1, j).wait()
    for wire in (
        [pair_wire, tail_near_wire, tail_wire, joint_wire, back, back_near, fed_wire]
        + list(near_wires.values()) + second_wires + turn_wires + pair_wires + list(far.values())
        + list(close.values()) + list(pieces.values()) + passed + joint_wires + vec_wires
    ):
        wire.wait_send()


def finish(d_mixed, d_query_last, normed, weight, tokens, d_middle, gain, joint_keep, joint_other, vectors, residual, fed_give):
    rows, width = tokens.shape
    half = width // 2
    members = 2 * lax.axis_size("tensor")
    higher = lax.axis_size("context").bit_length() - 2
    side = joint_keep.shape[1]
    tall = vectors.shape[0]
    scratch = [
        pltpu.VMEM((4, rows, width), BF16),
        pltpu.VMEM((4, rows, width), BF16),
        pltpu.VMEM((3, rows, width), F32),
        pltpu.VMEM((2, rows // 2, width), BF16),
        pltpu.VMEM((2, rows // 2, width), BF16),
        pltpu.VMEM((rows // 2, width), BF16),
        pltpu.VMEM((rows // 2, width), BF16),
        pltpu.VMEM((2, rows // 2, width), BF16),
        pltpu.VMEM((rows, width), BF16),
        pltpu.VMEM((4 * PAIR, width), F32),
        pltpu.VMEM((width, 4 * PAIR), F32),
        pltpu.VMEM((half, 3 * PAIR), BF16),
        pltpu.VMEM((half, 3 * PAIR), BF16),
        pltpu.VMEM((max(higher, 1), half, 3 * PAIR), BF16),
        pltpu.VMEM((max(higher, 1), half, 3 * PAIR), BF16),
        pltpu.VMEM((members * half, 3 * PAIR), BF16),
        pltpu.VMEM((width, 2 * PAIR), BF16),
        pltpu.VMEM((width, 2 * PAIR), BF16),
        pltpu.VMEM((width, 2 * PAIR), F32),
        pltpu.VMEM((half, 2 * PAIR), BF16),
        pltpu.VMEM((half, 2 * PAIR), BF16),
        pltpu.VMEM((half // 2, side), BF16),
        pltpu.VMEM((half // 2, side), BF16),
        pltpu.VMEM((higher + 1, half // 2, side), BF16),
        pltpu.VMEM((higher + 1, half // 2, side), BF16),
        pltpu.VMEM((half, 2 * side), BF16),
        pltpu.VMEM((half, 3 * PAIR), F32),
        pltpu.VMEM((half // 2, side), F32),
        pltpu.VMEM((tall, width), F32),
        pltpu.VMEM((higher + 4, tall, width), F32),
        pltpu.VMEM((higher + 4, tall, width), F32),
        pltpu.VMEM((2, 16, 3 * width), F32),
        pltpu.SemaphoreType.DMA((2,)),
        pltpu.SemaphoreType.DMA((3 * members + 3 * higher + 20,)),
        pltpu.SemaphoreType.DMA((3 * members + 3 * higher + 20,)),
    ]
    return pl.pallas_call(
        finish_kernel,
        in_specs=[VMEM] * 12,
        out_specs=[VMEM] * 2 + [ANY] + [VMEM] * 2,
        out_shape=[
            jax.ShapeDtypeStruct((rows, width), BF16),
            jax.ShapeDtypeStruct((rows, width), F32),
            jax.ShapeDtypeStruct((half, 3 * width), F32),
            jax.ShapeDtypeStruct((half, width), F32),
            jax.ShapeDtypeStruct((tall, width), F32),
        ],
        scratch_shapes=scratch,
        compiler_params=pltpu.CompilerParams(
            collective_id=6, has_side_effects=True, vmem_limit_bytes=63 << 20
        ),
        name="finish",
    )(d_mixed, d_query_last, normed, weight, tokens, d_middle, gain, joint_keep, joint_other, vectors, residual, fed_give)


def tri(n):
    r=lax.broadcasted_iota(jnp.int32,(n,n),0); c=lax.broadcasted_iota(jnp.int32,(n,n),1)
    return c<=r

def branch_mask():
    r=lax.broadcasted_iota(jnp.int32,(BRANCH,BRANCH),0); c=lax.broadcasted_iota(jnp.int32,(BRANCH,BRANCH),1)
    return (c<=r)&((c<PIECE)|(c//PIECE==r//PIECE))

def split_heads(x):
    lane=lax.broadcasted_iota(jnp.int32,(1,2*64),1)<64
    z=jnp.zeros_like(x)
    return jnp.concatenate([jnp.where(lane,x,z),jnp.where(lane,z,x)],axis=0)

def join_heads(x):
    n=x.shape[0]//2
    lane=lax.broadcasted_iota(jnp.int32,(1,2*64),1)<64
    return jnp.where(lane,x[:n],x[n:])

def fwd_kernel(order, qkv, q16, qinfo, kinfo, att, att16, canon, of, lse, of16, lse16):
    n_p=qkv.shape[0]//PIECE
    for i in range(n_p):
        src=pl.ds(pl.multiple_of(order[i]*PIECE,PIECE),PIECE)
        canon[i*PIECE:(i+1)*PIECE,:]=qkv[src,0:384]
    def rows(start,size,parts):
        qh=split_heads(canon[pl.ds(start,size),0:128])
        ss=[]
        for ks,kn,mask in parts:
            s=contract(qh,canon[pl.ds(ks,kn),128:256],1,1)
            if mask is not None:
                m2=jnp.concatenate([mask,mask],axis=0)
                s=jnp.where(m2,s,NEGATIVE)
            ss.append(s)
        top=functools.reduce(jnp.maximum,[jnp.max(s,axis=1,keepdims=True) for s in ss])
        tot=0.; o=0.
        for (ks,kn,_),s in zip(parts,ss):
            e=jnp.exp(s-top)
            tot=tot+jnp.sum(e,axis=1,keepdims=True)
            o=o+contract(e.astype(BF16),canon[pl.ds(ks,kn),256:384],1,0)
        o=join_heads(o*(1.0/tot))
        of[pl.ds(start,size),:]=o
        l=top+jnp.log(tot)
        lse[pl.ds(start,size),:]=join_heads(jnp.broadcast_to(l,(2*size,128)))
    t=tri(256)
    for b in range(4):
        parts=[(b*256,256,t)]
        if b: parts.insert(0,(0,b*256,None))
        rows(b*256,256,parts)
    bm=branch_mask()
    def branch(b,_):
        st=pl.multiple_of(TRUNK+b*BRANCH,PIECE)
        rows(st,BRANCH,[(0,TRUNK,None),(st,BRANCH,bm)])
        return 0
    lax.fori_loop(0,4,branch,0)
    for i in range(n_p):
        dst=pl.ds(pl.multiple_of(order[i]*PIECE,PIECE),PIECE)
        att[dst,:]=of[i*PIECE:(i+1)*PIECE,:].astype(BF16)
    s=contract(q16[...],qkv[:,384:512],1,1)
    s=jnp.where(allowed_mask(qinfo,kinfo),s,NEGATIVE)
    top=jnp.max(s,axis=1,keepdims=True)
    e=jnp.exp(s-top)
    tot=jnp.sum(e,axis=1,keepdims=True)
    o=contract(e.astype(BF16),qkv[:,384:512],1,0)*(1.0/tot)
    of16[...]=o
    att16[...]=pltpu.roll(o,64,1).astype(BF16)
    lse16[...]=jnp.broadcast_to(top+jnp.log(tot),o.shape)

def allowed_mask(qinfo,kinfo):
    ks=kinfo[0:1,:]; kp=kinfo[1:2,:]
    return ((ks==qinfo[:,0:1])|(ks==qinfo[:,1:2])|(ks==qinfo[:,2:3]))&(kp<=qinfo[:,3:4])

def attention_forward(order,qkv,q16,qinfo,kinfo):
    n=qkv.shape[0]; r=q16.shape[0]
    sd=jax.ShapeDtypeStruct
    V=pl.BlockSpec(memory_space=pltpu.VMEM)
    return pl.pallas_call(fwd_kernel,
        in_specs=[pl.BlockSpec(memory_space=pltpu.SMEM)]+[V]*4,
        out_specs=[V]*7,
        out_shape=[sd((n,128),BF16),sd((r,128),BF16),sd((n,384),BF16),sd((n,128),F32),sd((n,128),F32),sd((r,128),F32),sd((r,128),F32)],
        compiler_params=pltpu.CompilerParams(vmem_limit_bytes=32<<20),
        cost_estimate=pl.CostEstimate(flops=20_000_000_000,bytes_accessed=8_000_000,transcendentals=7_000_000),
        name="tree_attention_forward",
    )(order,qkv,q16,qinfo,kinfo)

def bwd_kernel(order, canon, of, lse, datt, kv16, q16, of16, lse16, datt16, qinfo, kinfo, dqkv, dq16, dc, dacc):
    n_p=canon.shape[0]//PIECE
    for i in range(n_p):
        src=pl.ds(pl.multiple_of(order[i]*PIECE,PIECE),PIECE)
        dc[i*PIECE:(i+1)*PIECE,:]=datt[src,:]
    def rows(start,size,parts):
        r=pl.ds(start,size)
        qh=split_heads(canon[r,0:128])
        d=dc[r,:]
        dh=split_heads(d)
        prod=d.astype(F32)*of[r,:]
        delta=jnp.concatenate([jnp.sum(prod[:,0:64],axis=1,keepdims=True),jnp.sum(prod[:,64:128],axis=1,keepdims=True)],axis=0)
        l=jnp.concatenate([lse[r,0:1],lse[r,64:65]],axis=0)
        dq=0.
        for ks,kn,mask,first in parts:
            kk=canon[pl.ds(ks,kn),128:256]
            s=contract(qh,kk,1,1)
            if mask is not None:
                s=jnp.where(jnp.concatenate([mask,mask],axis=0),s,NEGATIVE)
            p=jnp.exp(s-l)
            dp=contract(dh,canon[pl.ds(ks,kn),256:384],1,1)
            ds=(p*(dp-delta)).astype(BF16)
            dv=contract(p.astype(BF16),dh,0,0)
            dk=contract(ds,qh,0,0)
            dq=dq+contract(ds,kk,1,0)
            if first:
                dacc[pl.ds(ks,kn),128:256]=dk
                dacc[pl.ds(ks,kn),256:384]=dv
            else:
                dacc[pl.ds(ks,kn),128:256]+=dk
                dacc[pl.ds(ks,kn),256:384]+=dv
        dacc[r,0:128]=join_heads(dq)
    t=tri(256)
    for b in range(4):
        parts=[(b*256,256,t,True)]
        if b: parts.insert(0,(0,b*256,None,False))
        rows(b*256,256,parts)
    bm=branch_mask()
    def branch(b,_):
        st=pl.multiple_of(TRUNK+b*BRANCH,PIECE)
        rows(st,BRANCH,[(0,TRUNK,None,False),(st,BRANCH,bm,True)])
        return 0
    lax.fori_loop(0,4,branch,0)
    for i in range(n_p):
        dst=pl.ds(pl.multiple_of(order[i]*PIECE,PIECE),PIECE)
        x=dacc[i*PIECE:(i+1)*PIECE,:]
        dqkv[dst,0:128]=(x[:,0:128]*0.125).astype(BF16)
        dqkv[dst,128:384]=x[:,128:384].astype(BF16)
    k16=kv16[:,384:512]
    s=contract(q16[...],k16,1,1)
    s=jnp.where(allowed_mask(qinfo,kinfo),s,NEGATIVE)
    p=jnp.exp(s-lse16[:,0:1])
    dp=contract(datt16[...],k16,1,1)
    delta=jnp.sum(datt16[...].astype(F32)*of16[...],axis=1,keepdims=True)
    ds=(p*(dp-delta)).astype(BF16)
    dqkv[:,384:512]=(contract(ds,q16[...],0,0)+contract(p.astype(BF16),datt16[...],0,0)).astype(BF16)
    lane=lax.broadcasted_iota(jnp.int32,(1,128),1)>=64
    dq=pltpu.roll(contract(ds,k16,1,0)*0.125,64,1)
    dq16[...]=jnp.where(lane,dq,0.0).astype(BF16)

def attention_backward(order,canon,of,lse,datt,qkv,q16,of16,lse16,datt16,qinfo,kinfo):
    n=canon.shape[0]; r=q16.shape[0]
    sd=jax.ShapeDtypeStruct
    V=pl.BlockSpec(memory_space=pltpu.VMEM)
    return pl.pallas_call(bwd_kernel,
        in_specs=[pl.BlockSpec(memory_space=pltpu.SMEM)]+[V]*11,
        out_specs=[V]*2,
        out_shape=[sd((n,512),BF16),sd((r,128),BF16)],
        scratch_shapes=[pltpu.VMEM((n,128),BF16),pltpu.VMEM((n,384),F32)],
        compiler_params=pltpu.CompilerParams(vmem_limit_bytes=40<<20),
        cost_estimate=pl.CostEstimate(flops=50_000_000_000,bytes_accessed=15_000_000,transcendentals=7_000_000),
        name="tree_attention_backward",
    )(order,canon,of,lse,datt,qkv,q16,of16,lse16,datt16,qinfo,kinfo)


def parent_lookup(identities, shifted_table):
    labels = jnp.arange(shifted_table.shape[0], dtype=jnp.int32)
    matches = identities[:, None] == labels[None, :]
    return jnp.sum(jnp.where(matches, shifted_table[None, :], 0), axis=1) - 1


def tree_order(segments, places, parent):
    own = segments.reshape(-1, PIECE)[:, 0]
    start = places.reshape(-1, PIECE)[:, 0]
    table = parent + 1
    first_up = parent_lookup(own, table)
    second_up = parent_lookup(first_up, table)
    is_branch = (first_up >= 0) & (second_up < 0)
    is_leaf = second_up >= 0
    branch = jnp.where(is_leaf, first_up, own)
    rank = jnp.sum((is_branch[None, :] & (own[None, :] < branch[:, None])).astype(jnp.int32), axis=1)
    twin = is_leaf[None, :] & (first_up[None, :] == first_up[:, None]) & (own[None, :] < own[:, None])
    leaf = 1 + jnp.sum(twin.astype(jnp.int32), axis=1)
    target = jnp.where(
        first_up < 0, start // PIECE, TRUNK // PIECE + 3 * rank + jnp.where(is_leaf, leaf, 0)
    )
    pieces = jnp.arange(own.shape[0], dtype=jnp.int32)
    order = jnp.sum(jnp.where(target[None, :] == pieces[:, None], pieces[None, :], 0), axis=1)
    return order, first_up, second_up


def local(
    tokens,
    cotangent,
    segment_of,
    position_of,
    parent,
    ln1_gain,
    ln1_bias,
    w_qkv,
    b_query,
    b_value,
    w_out,
    b_out,
    ln2_gain,
    ln2_bias,
    w_fc,
    b_fc,
    w_proj,
    b_proj,
):
    rows = tokens.shape[0]
    half = w_qkv.shape[0]
    shard = lax.axis_index("shard")
    tensor, context, me = place()
    members = 2 * lax.axis_size("tensor")
    tree_rows = members * rows
    low = shard == 0

    vectors = jnp.stack(
        [ln1_gain, ln1_bias, b_query, b_value, b_out, ln2_gain, ln2_bias, b_proj]
    ).astype(F32)
    zeros = jnp.zeros_like(vectors)
    half_vectors = jnp.concatenate(
        [jnp.where(low, vectors, zeros), jnp.where(low, zeros, vectors)], axis=1
    )
    proj_mine = w_proj.T
    normed_all, mixed, query_last, vectors, weight, fc_other = project(tokens, w_qkv, half_vectors, w_fc)
    proj_give, cotangent_give, mixed = lax.optimization_barrier((proj_mine, cotangent, mixed))
    proj_other = swap(proj_give, "shard", 0)
    cotangent_far = swap(cotangent_give, "tensor", 1)

    tree_start = lax.div(context, 2) * tree_rows
    segments = lax.dynamic_slice_in_dim(segment_of, tree_start, tree_rows)
    places = lax.dynamic_slice_in_dim(position_of, tree_start, tree_rows)
    order, first_up, second_up = tree_order(segments, places, parent)
    key_info = jnp.stack([segments, places])
    query_info = jnp.stack(
        [segments, jnp.repeat(first_up, PIECE), jnp.repeat(second_up, PIECE), places], axis=1
    )
    query_info = lax.dynamic_slice_in_dim(query_info, me * rows, rows, 0)

    gain_one = vectors[0]
    attended_pair, attended_last, sorted_qkv, exact, level, exact_last, level_last = attention_forward(
        order, mixed, query_last, query_info, key_info
    )
    residual, fed_give, d_middle, d_pair, d_last, joint_keep, joint_give, fc_keep, fc_give, proj_sum, sums = feed_forward(
        attended_pair,
        attended_last,
        tokens,
        cotangent,
        cotangent_far,
        w_out,
        w_fc,
        fc_other,
        proj_mine,
        proj_other,
        vectors,
        b_fc.astype(F32)[None, :],
    )

    fc_got = swap(fc_give, "shard", 0)
    joint_other = swap(joint_give, "tensor", 1)
    proj_sum = lax.psum(proj_sum, "context")

    d_mixed, d_query_last = attention_backward(
        order, sorted_qkv, exact, level, d_pair, mixed, query_last, exact_last, level_last, d_last,
        query_info, key_info,
    )
    fc_got, joint_other, d_mixed = lax.optimization_barrier((fc_got, joint_other, d_mixed))
    fc_sum = (fc_keep.astype(F32) + fc_got.astype(F32)).astype(BF16)
    fc_sum = lax.psum(
        fc_sum, "context", axis_index_groups=[list(range(lax.axis_size("context")))[::-1]]
    )
    output, d_inputs, own_mixer, own_out, sums = finish(
        d_mixed,
        d_query_last,
        normed_all,
        weight,
        tokens,
        d_middle,
        gain_one[None, :],
        joint_keep,
        joint_other,
        sums,
        residual,
        fed_give,
    )
    proj_sum, fc_sum, sums = lax.optimization_barrier((proj_sum, fc_sum, sums))
    own_fc, own_proj = fc_sum.astype(F32), proj_sum.T.astype(F32)
    mine = lax.dynamic_slice_in_dim(sums[:8], shard * half, half, 1)
    own_bias_fc = lax.dynamic_slice_in_dim(sums, 8 + tensor, 1, 0)[0]
    return (
        output,
        d_inputs,
        mine[0],
        mine[1],
        own_mixer,
        mine[2],
        mine[3],
        own_out,
        mine[4],
        mine[5],
        mine[6],
        own_fc,
        own_bias_fc,
        own_proj,
        mine[7],
    )


def solution(mesh):
    return jax.shard_map(
        local,
        mesh=mesh,
        in_specs=(
            P(("shard", "context", "tensor"), None),
            P(("shard", "context", "tensor"), None),
            P("shard"),
            P("shard"),
            P(),
            P("shard"),
            P("shard"),
            P("shard", None),
            P("shard"),
            P("shard"),
            P("shard", None),
            P("shard"),
            P("shard"),
            P("shard"),
            P("shard", "tensor"),
            P("tensor"),
            P("tensor", "shard"),
            P("shard"),
        ),
        out_specs=(
            P(("shard", "context", "tensor"), None),
            P(("shard", "context", "tensor"), None),
            P("shard"),
            P("shard"),
            P("shard", None),
            P("shard"),
            P("shard"),
            P("shard", None),
            P("shard"),
            P("shard"),
            P("shard"),
            P("shard", "tensor"),
            P("tensor"),
            P("tensor", "shard"),
            P("shard"),
        ),
        check_vma=False,
    )
```

time: 767 us -> 420 us (0.55)
  waiting for transfers between devices: 105 us -> 1.58 us
  Pallas kernels: 249 us -> 338 us
  local copies, waits for them, and re-layouts: 134 us -> 45 us
  matrix products: 88.1 us -> 0 us
  other arithmetic: 84.6 us -> 7.09 us
  blocking collectives: 64.6 us -> 0 us
  starting transfers between devices: 32.4 us -> 5.18 us
  between operations: 2.61 us -> 14.5 us
    pallas_call x8 -> x3, Pallas kernels: 200 us -> 295 us  [the longest x1 164 us: finish(): pl.pallas_call(finish_kernel, in_specs=[VMEM] * 12, out_specs=[VMEM] * 2...]
    dot_general x15 -> x0, matrix products: 88.1 us -> none  [the longest x10 49.5 us: contract(): lax.dot_general(left, right, (((left_dim,), (right_dim,)), ((), ())), pre...]
    psum x1 -> x0, blocking collectives: 64.6 us -> none  [local(): sums = lax.psum(jnp.stack(sums), ('shard', 'context', 'tensor'))]
    ppermute x13 -> x0, waiting for transfers between devices: 55.5 us -> none  [the longest x10 55.5 us: context_swap(): lax.ppermute(value, 'context', [(i, i ^ mask) for i in range(contexts)])]
    ppermute x14 -> x4, waiting for transfers between devices: 49.5 us -> 1.51 us  [swap(): return lax.ppermute(value, axis, [(i, i ^ 1 << bit) for i in range(size)])]
    convert_element_type x7 -> x0, local copies, waits for them, and re-layouts: 24.8 us -> none  [the longest x4 11.9 us: local(): pairs[:, :, i].transpose(1, 0, 2).reshape(half, shared).astype(F32)]
    ppermute x13 -> x0, starting transfers between devices: 18.8 us -> none  [the longest x10 15.6 us: context_swap(): lax.ppermute(value, 'context', [(i, i ^ mask) for i in range(contexts)])]
    convert_element_type x17 -> x3, other arithmetic: 23.3 us -> 6.09 us  [the longest x2 4.7 us: local(): own_fc, own_proj = (fc_sum.astype(F32), proj_sum.T.astype(F32))]
  transfers between devices with their start and end apart: 27 -> 6, of which waited for: 9 -> 1; matrix products, arithmetic and copies ran while one was open for 24% -> 1% of each run, Pallas kernels for 17% -> 50%
where the time goes in v2:
time: 420 us; the launch traced here: 411 us
  Pallas kernels  338 us (80%)
  local copies, waits for them, and re-layouts  45 us (11%)
  between operations  14.5 us (3%)
  other arithmetic  7.09 us (2%)
  starting transfers between devices  5.18 us (1%)
    pallas_call x1, Pallas kernels, finish(): pl.pallas_call(finish_kernel, in_specs=[VMEM] * 12, out_specs=[VMEM] * 2...  164 us
    pallas_call x1, Pallas kernels, feed_forward(): pl.pallas_call(feed_forward_kernel, in_specs=[ANY] + [VMEM] * 4 + [ANY] *...  81.5 us
    pallas_call x1, Pallas kernels, project(): pl.pallas_call(project_kernel, in_specs=[VMEM] * 3 + [ANY], out_specs=[VM...  49.6 us
    unnamed x71, local copies, waits for them, and re-layouts  33.8 us
    pallas_call x1, Pallas kernels, attention_backward(): pl.pallas_call(bwd_kernel, in_specs=[pl.BlockSpec(memory_space=pltpu.SMEM...  26.7 us
    pallas_call x1, Pallas kernels, attention_forward(): pl.pallas_call(fwd_kernel, in_specs=[pl.BlockSpec(memory_space=pltpu.SMEM...  16.7 us
  transfers between devices with their start and end apart: 6, of which 1 were waited for; matrix products, arithmetic and copies ran while one was open for 1% of the time, Pallas kernels for 50%

profile of v2, /device:TPU:0, one launch (start us, length us, event | category | flops | bytes accessed | tf_op | source)
XLA Modules:
  0.0 411.5 jit_solution(5760944231530135757)
XLA Ops:
  7.2 0.7 stack.45
  7.9 0.7 stack.46
  8.6 0.7 stack.47
  9.3 0.7 stack.48
  10.0 0.7 stack.49
  10.7 0.7 stack.50
  11.3 0.7 stack.51
  12.0 0.7 stack.52
  12.9 1.1 copy-done
  14.0 1.3 copy-done.2
  15.3 2.0 copy-done.3
  17.3 49.6 %project.1 = (bf16[2560,1088]{1,0:T(8,128)(2,1)S(1)}, bf16[2560,512]{1,0:T(8,128)(2,1)S(1)}, bf16[320,128]{1,0:T(8,128)(2,1)S(1)}, f32[8,1088]{1,0:T(8,128)S(1)}...) custom-call(bf16[320,1088]{1,0:T(8,128)(2,1)S(1)} %copy-done, bf16[544,3264]{1,0:T(8,128)(2,1)S(1)} %copy-done.3, ...), custom_call_target="tpu_custom_call" | custom-call | tf_op jit(solution)/shard_map/project/pallas_call | solution.py:240
  66.9 2.6 copy-done.1
  69.5 1.1 copy-done.5
  70.6 1.0 copy-done.6
  71.6 0.6 copy-done.10
  72.2 1.5 copy-done.11
  73.7 1.4 collective-permute-start
  75.1 1.4 collective-permute-start.1
  76.6 0.1 slice_reduce_fusion.1
  76.7 0.2 select_reduce_fusion.3
  76.9 0.2 select_reduce_fusion.2
  77.2 0.1 dynamic_slice.16
  77.5 0.1 copy.48
  77.6 0.1 copy.49
  77.7 0.1 slice_reduce_fusion
  77.8 0.1 select_reduce_fusion.1
  77.9 0.2 convert_reduce_fusion.1
  78.1 0.1 select_reduce_fusion.order
  78.3 0.1 fusion.2
  78.4 0.1 copy.51.qinfo
  78.6 1.7 copy-done.12
  80.3 16.7 %tree_attention_forward.1 = (bf16[2560,128]{1,0:T(8,128)(2,1)S(1)}, bf16[320,128]{1,0:T(8,128)(2,1)S(1)}, bf16[2560,384]{1,0:T(8,128)(2,1)S(1)}, f32[2560,128]{1...) custom-call(s32[20]{0:T(128)S(1)} %select_reduce_fusion.order, ...), custom_call_target="tpu_custom_call" | custom-call | flops 20000000000 | bytes 8000000 | tf_op jit(solution)/shard_map/tree_attention_forward/pallas_call | solution.py:1106
  97.0 0.8 copy-done.7
  97.9 0.6 copy-done.8
  98.5 1.3 copy-done.16
  99.8 1.1 copy-done.18
  100.8 0.6 reshape.121.bias_fc
  101.4 1.5 collective-permute-done.1.proj_other
  102.9 81.5 %feed_forward.1 = (f32[320,1088]{1,0:T(8,128)}, bf16[320,1088]{1,0:T(8,128)(2,1)}, f32[320,1088]{1,0:T(8,128)}, bf16[2560,128]{1,0:T(8,128)(2,1)}, bf16[320,128]...) custom-call(bf16[2560,128]{1,0:T(8,128)(2,1)} %copy-done.7, ...), custom_call_target="tpu_custom_call" | custom-call | tf_op jit(solution)/shard_map/feed_forward/pallas_call | solution.py:581
  184.5 0.9 collective-permute-start.3
  185.4 1.5 collective-permute-start.2
  186.9 1.7 copy-done.13
  188.6 1.2 copy-done.14
  189.8 0.9 copy-done.15
  190.7 1.5 copy-done.17
  192.2 1.3 copy-done.19
  193.5 26.7 %tree_attention_backward.1 = (bf16[2560,512]{1,0:T(8,128)(2,1)S(1)}, bf16[320,128]{1,0:T(8,128)(2,1)S(1)}) custom-call(s32[20]{0:T(128)S(1)} %select_reduce_fusion.order, bf16[2560,384]{1,0:T(8,128)(2,1)S(1)} %copy-done.17, f32[2560,128]{1,0:T(8,128)S(1)} %get-tuple-element.67.of, f32[2560,128]{1,0:T(8,128)S(1)} %copy-done.19, ...), custom_call_target="tpu_custom_call" | custom-call | flops 49999998976 | bytes 15000000 | tf_op jit(solution)/shard_map/tree_attention_backward/pallas_call | solution.py:1179
  220.3 1.6 copy-done.4
  221.8 0.6 copy-done.9
  222.5 0.8 copy-done.27
  223.3 1.4 add_convert_fusion
  224.7 1.4 slice.38.gain
  226.1 163.7 %finish.1 = (bf16[320,1088]{1,0:T(8,128)(2,1)}, f32[320,1088]{1,0:T(8,128)}, f32[544,3264]{1,0:T(8,128)}, f32[544,1088]{1,0:T(8,128)}, f32[16,1088]{1,0:T(8,128)}) custom-call(bf16[2560,512]{1,0:T(8,128)(2,1)} %copy-done.4, bf16[320,128]{1,0:T(8,128)(2,1)} %copy-done.9, bf16[2560,1088]{1,0:T(8,128)(2,1)} %copy-done.1, bf16[1088,640]{1,0:T(8,128)(2,1)} %copy-done.5, ...), custom_call_target="tpu_custom_call" | custom-call | tf_op jit(solution)/shard_map/finish/pallas_call | solution.py:1013
  389.9 0.8 slice.39
  390.7 1.4 dynamic-slice_reduce_fusion
  392.0 3.1 convert_element_type.34
  395.1 1.6 convert_bitcast_fusion
  396.8 0.7 dynamic-slice_reduce_fusion.1
  397.5 0.9 copy.62
  398.3 1.1 copy.63
  399.5 3.3 copy.64
  402.8 0.3 copy-done.21
  403.0 1.5 copy.65
  (69 shorter events, 0.9 us)
Async XLA Ops:
  7.2 382.7 %all-reduce.3.cloned.1.call-start = ((), (), s32[]{:S(2)}) async-start(), calls=%async_computation | async-start | bytes 2506752 | tf_op jit(solution)/shard_map/psum | solution.py:1288
  12.9 1.1 copy-start
  14.0 1.3 copy-start.2
  15.3 2.0 copy-start.3
  17.3 57.8 %copy-start.23 = (bf16[1088,544]{0,1:T(8,128)(2,1)S(1)}, bf16[1088,544]{0,1:T(8,128)(2,1)}, u32[]{:S(2)}) copy-start(bf16[1088,544]{0,1:T(8,128)(2,1)} %param.34) | copy-start | bytes 3551236
  17.3 59.2 %copy-start.31 = (s32[52]{0:T(128)S(1)}, s32[52]{0:T(128)}, u32[]{:S(2)}) copy-start(s32[52]{0:T(128)} %param.22) | copy-start | bytes 628
  17.3 59.2 %copy-start.28 = (s32[5120]{0:T(1024)S(1)}, s32[5120]{0:T(1024)}, u32[]{:S(2)}) copy-start(s32[5120]{0:T(1024)} %param.20) | copy-start | bytes 61444
  17.3 59.9 %copy-start.29 = (s32[5120]{0:T(1024)S(1)}, s32[5120]{0:T(1024)}, u32[]{:S(2)}) copy-start(s32[5120]{0:T(1024)} %param.21) | copy-start | bytes 61444
  66.9 2.6 copy-start.1
  69.5 1.1 copy-start.5
  70.6 1.0 copy-start.6
  71.6 0.6 copy-start.10
  72.2 1.5 copy-start.11
  73.7 27.7 %collective-permute-start = (bf16[320,1088]{1,0:T(8,128)(2,1)}, bf16[320,1088]{1,0:T(8,128)(2,1)}, u32[]{:S(2)}, u32[]{:S(2)}) collective-permute-start(bf16[320,1088]{1,0:T(8,128)(2,1)} %cotangent.1), channel_id=1, source_target_pairs={{0,2},{1,3},{2,0},{3,1},{4,6},{5,7},{6,4},{7,5},{8,10},{9,11},{10,... | collective-permute-start | bytes 2088968 | tf_op jit(solution)/shard_map/ppermute | solution.py:55
  75.1 27.8 %collective-permute-start.1 = (bf16[544,1088]{1,0:T(8,128)(2,1)S(1)}, bf16[544,1088]{1,0:T(8,128)(2,1)}, u32[]{:S(2)}, u32[]{:S(2)}) collective-permute-start(bf16[544,1088]{1,0:T(8,128)(2,1)S(1)} %bitcast.24), channel_id=1, source_target_pairs={{0,16},{16,0},{1,17},{17,1},{2,18},{18,2},{3,19},{19,3},{4,20},{20... | collective-permute-start | bytes 3551240 | tf_op jit(solution)/shard_map/ppermute | solution.py:55
  78.6 1.7 copy-start.12
  80.3 20.5 %copy-start.30 = (bf16[1088]{0:T(1024)(128)(2,1)S(1)}, bf16[1088]{0:T(1024)(128)(2,1)}, u32[]{:S(2)}) copy-start(bf16[1088]{0:T(1024)(128)(2,1)} %param.33) | copy-start | bytes 6532
  97.0 0.8 copy-start.7
  97.8 0.6 copy-start.8
  98.5 1.3 copy-start.16
  99.8 1.1 copy-start.18
  184.5 205.4 %all-reduce.5.cloned.1.call-start = ((), (), s32[]{:S(2)}) async-start(), calls=%async_computation.1 | async-start | bytes 2506752 | tf_op jit(solution)/shard_map/psum | solution.py:1296
  184.5 38.0 %collective-permute-start.3 = (bf16[544,640]{1,0:T(8,128)(2,1)}, bf16[544,640]{1,0:T(8,128)(2,1)S(1)}, u32[]{:S(2)}, u32[]{:S(2)}) collective-permute-start(bf16[544,640]{1,0:T(8,128)(2,1)} %get-tuple-element.65), channel_id=1, source_target_pairs={{0,2},{1,3},{2,0},{3,1},{4,6},{5,7},{6,4},{7,5},{8,10},{9,11},{10,... | collective-permute-start | bytes 2088968 | tf_op jit(solution)/shard_map/ppermute | solution.py:55
  185.4 37.1 %collective-permute-start.2 = (bf16[544,1088]{1,0:T(8,128)(2,1)}, bf16[544,1088]{1,0:T(8,128)(2,1)S(1)}, u32[]{:S(2)}, u32[]{:S(2)}) collective-permute-start(bf16[544,1088]{1,0:T(8,128)(2,1)} %get-tuple-element.64), channel_id=1, source_target_pairs={{0,16},{16,0},{1,17},{17,1},{2,18},{18,2},{3,19},{19,3},{4,20},{20... | collective-permute-start | bytes 3551240 | tf_op jit(solution)/shard_map/ppermute | solution.py:55
  186.9 1.7 copy-start.13
  188.6 1.2 copy-start.14
  189.8 0.9 copy-start.15
  190.7 1.5 copy-start.17
  192.2 1.3 copy-start.19
  193.5 29.8 %copy-start.25 = (bf16[544,1088]{1,0:T(8,128)(2,1)S(1)}, bf16[544,1088]{1,0:T(8,128)(2,1)}, u32[]{:S(2)}) copy-start(bf16[544,1088]{1,0:T(8,128)(2,1)} %get-tuple-element.87) | copy-start | bytes 3551236
  220.2 1.6 copy-start.4
  221.8 0.6 copy-start.9
  222.5 0.9 copy-start.27
  392.0 3.1 copy-start.24
  392.0 5.4 %copy-start.26 = (bf16[320,1088]{1,0:T(8,128)(2,1)S(1)}, bf16[320,1088]{1,0:T(8,128)(2,1)}, u32[]{:S(2)}) copy-start(bf16[320,1088]{1,0:T(8,128)(2,1)} %get-tuple-element.131) | copy-start | bytes 2088964
  392.0 6.3 %copy-start.22 = (f32[320,1088]{1,0:T(8,128)S(1)}, f32[320,1088]{1,0:T(8,128)}, u32[]{:S(2)}) copy-start(f32[320,1088]{1,0:T(8,128)} %get-tuple-element.132) | copy-start | bytes 4177924
  395.1 4.3 %copy-start.20 = (f32[544,3264]{1,0:T(8,128)S(1)}, f32[544,3264]{1,0:T(8,128)}, u32[]{:S(2)}) copy-start(f32[544,3264]{1,0:T(8,128)} %get-tuple-element.135) | copy-start | bytes 21307396
  399.4 3.6 copy-start.21
Sparse Core Ops, SparseCore 0:
  184.6 58.1 all-reduce.2
  245.9 96.0 all-reduce.4

commit v3 on v2

--- a/solution.py
+++ b/solution.py
@@ -60,6 +60,7 @@
         self.send, self.recv, self.used = send, recv, 0
 
     def start(self, source, target, device):
+        assert self.used < self.send.shape[0]
         copy = pltpu.make_async_remote_copy(
             src_ref=source,
             dst_ref=target,
@@ -103,7 +104,7 @@
 
 
 def project_kernel(
-    tokens, w_qkv, half_vectors, w_fc, normed, mixed, query_last, vectors, weight, fc_other, everyone, seen, local_sem, send, recv
+    tokens, w_all, half_vectors, w_fc, normed, mixed, query_last, vectors, weight, fc_other, everyone, w_qkv, seen, local_sem, send, recv
 ):
     tensor, context, me = place()
     shard = lax.axis_index("shard")
@@ -116,6 +117,8 @@
     wires = Wires(send, recv)
     turn = members // 2
 
+    load = pltpu.make_async_copy(w_all, w_qkv, local_sem.at[1])
+    load.start()
     barrier = pltpu.get_barrier_semaphore()
     peers = [member(mask)[0] for mask in (1, 2, turn)] + [across]
     rest = [m for m in range(4, members) if m & 1 == 0 and m not in (turn, turn + 2)]
@@ -160,9 +163,11 @@
         weight[to, 4 * PAIR :] = jnp.where(lane, query, jnp.zeros_like(query))
         return carry
 
+    load.wait()
     lax.fori_loop(0, half // 32, choose, 0)
     chosen = weight.at[pl.ds(pl.multiple_of(shard * half, half), half)]
     weight_wire = wires.start(chosen, chosen, across)
+    fc_wire = wires.start(w_fc.at[0 : half // 2], fc_other, across)
 
     vector_wire.wait_recv()
     vectors[...] = half_vectors[...] + seen[...]
@@ -203,7 +208,6 @@
         close[m] = hand(slot(m), 1)
         pieces[other] = hand(slot(m, first, cut), other)
     weight_wire.wait_recv()
-    fc_wire = wires.start(w_fc, fc_other, across)
     multiply(0)
     last = jnp.dot(
         normed[pl.ds(pl.multiple_of(me * rows, 32), rows), :], weight[:, 4 * PAIR :], preferred_element_type=F32
@@ -239,7 +243,7 @@
     shape = jax.ShapeDtypeStruct
     return pl.pallas_call(
         project_kernel,
-        in_specs=[VMEM] * 3 + [ANY],
+        in_specs=[VMEM, ANY, VMEM, ANY],
         out_specs=[VMEM] * 5 + [ANY],
         out_shape=[
             shape((tree, width), BF16),
@@ -247,12 +251,13 @@
             shape((rows, PAIR), BF16),
             shape(half_vectors.shape, F32),
             shape((width, 5 * PAIR), BF16),
-            shape(w_fc.shape, BF16),
+            shape((w_fc.shape[0] // 2, w_fc.shape[1]), BF16),
         ],
         scratch_shapes=[
             pltpu.VMEM((tree, width), BF16),
+            pltpu.VMEM(w_qkv.shape, BF16),
             pltpu.VMEM(half_vectors.shape, F32),
-            pltpu.SemaphoreType.DMA((1,)),
+            pltpu.SemaphoreType.DMA((2,)),
             pltpu.SemaphoreType.DMA((16,)),
             pltpu.SemaphoreType.DMA((16,)),
         ],
@@ -351,7 +356,7 @@
                 (slab(pair, me, rows), beside(attended, me)),
                 (out_mine, slab(w_out, shard, half)),
                 (fc_mine, slab(w_fc, shard, half)),
-                (fc_other, slab(w_fc, 1 - shard, half)),
+                (fc_other, slab(w_fc, 2 * (1 - shard), quarter)),
                 (proj_mine, slab(w_proj, shard, half)),
                 (proj_other, slab(w_proj, 1 - shard, half)),
                 (cotangent, slab(grads, 0, rows)),
@@ -369,6 +374,9 @@
     out_wire.wait_recv()
     out_part = slab(w_out, 2 * (1 - shard) + near_bit, quarter)
     out_near = wires.start(out_part, out_part, member(1)[0])
+    fc_wire = wires.start(
+        fc_mine.at[quarter:half], slab(w_fc, 2 * shard + 1, quarter), across
+    )
     for copy in local:
         copy.wait()
     for wire in moved + [out_near]:
@@ -426,6 +434,7 @@
     def ahead(mask):
         return contract(hidden[mask * rows : (mask + 1) * rows, :], w_proj[...], 1, 1)
 
+    fc_wire.wait_recv()
     feed(slice(0, rows))
     close.wait_recv()
     feed(slice(rows, 2 * rows))
@@ -566,7 +575,7 @@
     for wire in returned:
         wire.wait_recv()
     for wire in (
-        moved + returned + [out_wire, out_near] + pulled_wires + proj_wires
+        moved + returned + [out_wire, out_near, fc_wire] + pulled_wires + proj_wires
         + cross + relay + to_pass + to_far + [joint_wire, close, to_near, to_near_out, to_pass_out]
     ):
         wire.wait_send()
@@ -618,8 +627,8 @@
             pltpu.VMEM((width, 10 * PAIR), BF16),
             pltpu.VMEM((width, 5 * PAIR), BF16),
             pltpu.SemaphoreType.DMA((8,)),
-            pltpu.SemaphoreType.DMA((2 * members + 20,)),
-            pltpu.SemaphoreType.DMA((2 * members + 20,)),
+            pltpu.SemaphoreType.DMA((2 * members + 24,)),
+            pltpu.SemaphoreType.DMA((2 * members + 24,)),
         ],
         compiler_params=pltpu.CompilerParams(
             collective_id=3, has_side_effects=True, vmem_limit_bytes=62 << 20
@@ -640,28 +649,24 @@
     joint_other,
     vectors,
     residual,
-    fed_give,
+    fed_other,
     output,
     d_tokens,
-    own_mixer,
-    own_out,
+    pairs,
+    joint_all,
     sums,
     near_give,
     near_got,
     row_sum,
     second_got,
-    turn_got,
-    second_last,
     turn_last,
     last_low,
-    fed_got,
     pair_t,
     pair,
     pair_give,
     pair_got,
     pair_low,
     pair_seen,
-    pairs,
     tail,
     tail_near,
     tail_sum,
@@ -671,14 +676,11 @@
     joint_got,
     half_low,
     half_seen,
-    joint_all,
     pair_sum,
     half_sum,
     vec,
     vec_give,
     vec_got,
-    mixer_rows,
-    mixer_sem,
     send,
     recv,
 ):
@@ -692,7 +694,6 @@
     rows, width = tokens.shape
     half = width // 2
     quarter = half // 2
-    cut = rows // 2
     side = joint_keep.shape[1]
     shared = width - HEAD_DIM
     block = 4 * PAIR
@@ -702,7 +703,6 @@
     ]
     group = range(1, members)
     wires = Wires(send, recv)
-    lane = lax.broadcasted_iota(jnp.int32, (1, PAIR), 1) < HEAD_DIM
 
     barrier = pltpu.get_barrier_semaphore()
     peers = [member(mask)[0] for mask in group] + [across] + higher
@@ -754,9 +754,7 @@
         tail_give[i * quarter : (i + 1) * quarter, :] = tail_sum[source, :].astype(BF16)
     tail_wire = wires.start(tail_give, tail_got, to_second)
 
-    first = slice(0, cut)
-    rest = slice(cut, rows)
-    second_wires, turn_wires = [], []
+    second_wires = []
     for i, mask in enumerate(order):
         total = term(mask)
         if mask == 0:
@@ -764,16 +762,11 @@
             total = total + contract(query, weight[:, block:], 1, 1)
         near_wires[mask].wait_recv()
         total = total + near_got[i].astype(F32)
-        if i:
-            row_sum[i - 1] = total
-        if mask:
+        if i >= 2:
+            row_sum[i - 2] = total
+        if mask & 2:
             near_got[i] = total.astype(BF16)
-        if mask & 2:
-            second_wires.append(
-                wires.start(near_got.at[i, first], second_got.at[len(second_wires)], to_second)
-            )
-        if mask & turn:
-            turn_wires.append(wires.start(near_got.at[i, rest], turn_got.at[len(turn_wires)], to_turn))
+            second_wires.append(wires.start(near_got.at[i], second_got.at[i], to_second))
 
     pair_wire.wait_recv()
     pair_own = pair[own, 0 : 3 * PAIR] + pair_got[...].astype(F32)
@@ -814,6 +807,12 @@
     vec[2:3, shared:] = pltpu.roll(query, HEAD_DIM, 1)[:, :HEAD_DIM]
     vec[3:4, shared:] = pltpu.roll(columns[:, 3 * PAIR :], HEAD_DIM, 1)[:, :HEAD_DIM]
 
+
+    def add_fed(r):
+        output[r, :] = (residual[r, :] + fed_other[r, :].astype(F32)).astype(BF16)
+
+    by_rows(rows, 64, add_fed)
+
     joint_wire.wait_recv()
     half_sum[...] = joint_term(shard) + joint_got[...].astype(F32)
     hops = [to_turn] + higher
@@ -830,11 +829,8 @@
     joint_hop(0)
 
     second_wires[0].wait_recv()
-    last_low[0] = (row_sum[1, first] + second_got[0].astype(F32)).astype(BF16)
-    turn_wires.append(wires.start(last_low.at[0], turn_last, to_turn))
-    turn_wires[0].wait_recv()
-    last_low[1] = (row_sum[0, rest] + turn_got[0].astype(F32)).astype(BF16)
-    second_wires.append(wires.start(last_low.at[1], second_last, to_second))
+    last_low[...] = (row_sum[0] + second_got[0].astype(F32)).astype(BF16)
+    turn_wire = wires.start(last_low, turn_last, to_turn)
 
     for i in range(1, len(hops)):
         joint_hop(i)
@@ -850,18 +846,15 @@
         return wires.start(source, source, member(target)[0])
 
     pairs[pl.ds(pl.multiple_of(me * half, half), half), :] = pair_sum[...].astype(BF16)
-    far = {mask: hand(slot(0), mask) for mask in (2, turn)}
+    far = {mask: hand(slot(0), mask) for mask in (turn, 2)}
     close = {0: hand(slot(0), 1)}
 
     second_wires[1].wait_recv()
-    second_wires[2].wait_recv()
-    turn_wires[1].wait_recv()
-    turn_wires[2].wait_recv()
-    row_sum[2, first] = row_sum[2, first] + second_got[1].astype(F32) + turn_last[...].astype(F32)
-    row_sum[2, rest] = row_sum[2, rest] + turn_got[1].astype(F32) + second_last[...].astype(F32)
+    turn_wire.wait_recv()
 
     def first_norm(r):
-        result, by_gain, by_shift = norm_backward(tokens[r, :].astype(F32), row_sum[2, r, :], gain[0:1, :])
+        grad = row_sum[1, r, :] + second_got[1, r, :].astype(F32) + turn_last[r, :].astype(F32)
+        result, by_gain, by_shift = norm_backward(tokens[r, :].astype(F32), grad, gain[0:1, :])
         d_tokens[r, :] = result + d_middle[r, :]
         vec[0:1, :] += by_gain
         vec[1:2, :] += by_shift
@@ -881,11 +874,12 @@
     vec_stops = [member(1)[0], to_second, to_turn, across] + higher
     vec_send(0, vec_stops[0])
 
-    pieces = {}
-    for mask, onward, start in ((2, turn, 0), (turn, 2, quarter)):
-        far[mask].wait_recv()
-        close[mask] = hand(slot(mask), 1)
-        pieces[onward] = hand(slot(mask, start, quarter), onward)
+    opposite = 2 ^ turn
+    far[turn].wait_recv()
+    far[opposite] = hand(slot(turn), 2)
+    close[turn] = hand(slot(turn), 1)
+    far[2].wait_recv()
+    close[2] = hand(slot(2), 1)
     vec_add()
     vec_send(1, vec_stops[1])
 
@@ -897,12 +891,8 @@
     back = wires.start(joint_mine, joint_mine, to_second)
     vec_add()
     vec_send(2, vec_stops[2])
-    fed_wire = wires.start(fed_give, fed_got, to_second)
-    opposite = 2 ^ turn
-    passed = []
-    for mask, start in ((turn, 0), (2, quarter)):
-        pieces[mask].wait_recv()
-        passed.append(hand(slot(opposite, start, quarter), 1))
+    far[opposite].wait_recv()
+    close[opposite] = hand(slot(opposite), 1)
     vec_add()
     vec_send(3, vec_stops[3])
     back.wait_recv()
@@ -913,60 +903,19 @@
         vec_send(i, vec_stops[i])
         vec_add()
     sums[...] = vec[...]
-    fed_wire.wait_recv()
-
-    def add_fed(r):
-        output[r, :] = (residual[r, :] + fed_got[r, :].astype(F32)).astype(BF16)
-
-    by_rows(rows, 64, add_fed)
-    for wire in list(close.values()) + passed:
+    for wire in close.values():
         wire.wait_recv()
     back_near.wait_recv()
 
-    tall = mixer_rows.shape[1]
-
-    def mixer_copy(i, j):
-        r = pl.ds(pl.multiple_of((2 * i + j) * tall, tall), tall)
-        return pltpu.make_async_copy(mixer_rows.at[j], own_mixer.at[r], mixer_sem.at[j])
-
-    def write(i, carry):
-        for j in range(2):
-
-            @pl.when(i > 0)
-            def _():
-                mixer_copy(i - 1, j).wait()
-
-            start = (2 * i + j) * tall
-            r = pl.ds(pl.multiple_of(start, tall), tall)
-            own_out[r, 0:shared] = joint_all[r, 0:shared].astype(F32)
-            eighth = joint_all[r, shared : shared + PAIR].astype(F32)
-            ninth = joint_all[r, shared + PAIR :].astype(F32)
-            own_out[r, shared:] = ninth[:, :HEAD_DIM]
-            keys = []
-            for k in range(members):
-                value = pairs[pl.ds(pl.multiple_of(k * half + start, tall), tall), :].astype(F32)
-                mixer_rows[j, :, k * PAIR : (k + 1) * PAIR] = value[:, 0:PAIR]
-                mixer_rows[j, :, 2 * width + k * PAIR : 2 * width + (k + 1) * PAIR] = value[:, 2 * PAIR :]
-                keys.append(value[:, PAIR : 2 * PAIR])
-            keys = jnp.concatenate(keys + [jnp.where(lane, eighth, ninth)], axis=1)
-            mixer_rows[j, :, shared : 2 * width] = pltpu.roll(keys, HEAD_DIM, 1)
-            mixer_rows[j, :, 2 * width + shared :] = pltpu.roll(eighth, HEAD_DIM, 1)[:, :HEAD_DIM]
-            mixer_copy(i, j).start()
-        return carry
-
-    trips = half // (2 * tall)
-    lax.fori_loop(0, trips, write, 0)
-    for j in range(2):
-        mixer_copy(trips - 1, j).wait()
     for wire in (
-        [pair_wire, tail_near_wire, tail_wire, joint_wire, back, back_near, fed_wire]
-        + list(near_wires.values()) + second_wires + turn_wires + pair_wires + list(far.values())
-        + list(close.values()) + list(pieces.values()) + passed + joint_wires + vec_wires
+        [pair_wire, tail_near_wire, tail_wire, joint_wire, back, back_near]
+        + list(near_wires.values()) + second_wires + [turn_wire] + pair_wires + list(far.values())
+        + list(close.values()) + joint_wires + vec_wires
     ):
         wire.wait_send()
 
 
-def finish(d_mixed, d_query_last, normed, weight, tokens, d_middle, gain, joint_keep, joint_other, vectors, residual, fed_give):
+def finish(d_mixed, d_query_last, normed, weight, tokens, d_middle, gain, joint_keep, joint_other, vectors, residual, fed_other):
     rows, width = tokens.shape
     half = width // 2
     members = 2 * lax.axis_size("tensor")
@@ -976,12 +925,9 @@
     scratch = [
         pltpu.VMEM((4, rows, width), BF16),
         pltpu.VMEM((4, rows, width), BF16),
-        pltpu.VMEM((3, rows, width), F32),
-        pltpu.VMEM((2, rows // 2, width), BF16),
-        pltpu.VMEM((2, rows // 2, width), BF16),
-        pltpu.VMEM((rows // 2, width), BF16),
-        pltpu.VMEM((rows // 2, width), BF16),
-        pltpu.VMEM((2, rows // 2, width), BF16),
+        pltpu.VMEM((2, rows, width), F32),
+        pltpu.VMEM((2, rows, width), BF16),
+        pltpu.VMEM((rows, width), BF16),
         pltpu.VMEM((rows, width), BF16),
         pltpu.VMEM((4 * PAIR, width), F32),
         pltpu.VMEM((width, 4 * PAIR), F32),
@@ -989,7 +935,6 @@
         pltpu.VMEM((half, 3 * PAIR), BF16),
         pltpu.VMEM((max(higher, 1), half, 3 * PAIR), BF16),
         pltpu.VMEM((max(higher, 1), half, 3 * PAIR), BF16),
-        pltpu.VMEM((members * half, 3 * PAIR), BF16),
         pltpu.VMEM((width, 2 * PAIR), BF16),
         pltpu.VMEM((width, 2 * PAIR), BF16),
         pltpu.VMEM((width, 2 * PAIR), F32),
@@ -999,26 +944,23 @@
         pltpu.VMEM((half // 2, side), BF16),
         pltpu.VMEM((higher + 1, half // 2, side), BF16),
         pltpu.VMEM((higher + 1, half // 2, side), BF16),
-        pltpu.VMEM((half, 2 * side), BF16),
         pltpu.VMEM((half, 3 * PAIR), F32),
         pltpu.VMEM((half // 2, side), F32),
         pltpu.VMEM((tall, width), F32),
         pltpu.VMEM((higher + 4, tall, width), F32),
         pltpu.VMEM((higher + 4, tall, width), F32),
-        pltpu.VMEM((2, 16, 3 * width), F32),
-        pltpu.SemaphoreType.DMA((2,)),
         pltpu.SemaphoreType.DMA((3 * members + 3 * higher + 20,)),
         pltpu.SemaphoreType.DMA((3 * members + 3 * higher + 20,)),
     ]
     return pl.pallas_call(
         finish_kernel,
         in_specs=[VMEM] * 12,
-        out_specs=[VMEM] * 2 + [ANY] + [VMEM] * 2,
+        out_specs=[VMEM] * 5,
         out_shape=[
             jax.ShapeDtypeStruct((rows, width), BF16),
             jax.ShapeDtypeStruct((rows, width), F32),
-            jax.ShapeDtypeStruct((half, 3 * width), F32),
-            jax.ShapeDtypeStruct((half, width), F32),
+            jax.ShapeDtypeStruct((members * half, 3 * PAIR), BF16),
+            jax.ShapeDtypeStruct((half, 2 * side), BF16),
             jax.ShapeDtypeStruct((tall, width), F32),
         ],
         scratch_shapes=scratch,
@@ -1026,7 +968,55 @@
             collective_id=6, has_side_effects=True, vmem_limit_bytes=63 << 20
         ),
         name="finish",
-    )(d_mixed, d_query_last, normed, weight, tokens, d_middle, gain, joint_keep, joint_other, vectors, residual, fed_give)
+    )(d_mixed, d_query_last, normed, weight, tokens, d_middle, gain, joint_keep, joint_other, vectors, residual, fed_other)
+
+
+def write_kernel(pairs, joint, fc, own_mixer, own_out, own_fc):
+    members = pairs.shape[0]
+    width = own_out.shape[1]
+    shared = width - HEAD_DIM
+    lane = lax.broadcasted_iota(jnp.int32, (1, PAIR), 1) < HEAD_DIM
+
+    def write(r):
+        own_out[r, 0:shared] = joint[r, 0:shared].astype(F32)
+        eighth = joint[r, shared : shared + PAIR].astype(F32)
+        ninth = joint[r, shared + PAIR :].astype(F32)
+        own_out[r, shared:] = ninth[:, :HEAD_DIM]
+        own_fc[r, :] = fc[r, :].astype(F32)
+        keys = []
+        for k in range(members):
+            value = pairs[k, r, :].astype(F32)
+            own_mixer[r, k * PAIR : (k + 1) * PAIR] = value[:, 0:PAIR]
+            own_mixer[r, 2 * width + k * PAIR : 2 * width + (k + 1) * PAIR] = value[:, 2 * PAIR :]
+            keys.append(value[:, PAIR : 2 * PAIR])
+        keys = jnp.concatenate(keys + [jnp.where(lane, eighth, ninth)], axis=1)
+        own_mixer[r, shared : 2 * width] = pltpu.roll(keys, HEAD_DIM, 1)
+        own_mixer[r, 2 * width + shared :] = pltpu.roll(eighth, HEAD_DIM, 1)[:, :HEAD_DIM]
+
+    by_rows(fc.shape[0], 16, write)
+
+
+def write_gradients(pairs, joint, fc):
+    half, width = fc.shape
+    members = pairs.shape[0] // half
+    step = half // 2
+
+    def block(*shape):
+        return pl.BlockSpec(shape, lambda i: (0,) * (len(shape) - 2) + (i, 0))
+
+    return pl.pallas_call(
+        write_kernel,
+        grid=(half // step,),
+        in_specs=[block(members, step, 3 * PAIR), block(step, joint.shape[1]), block(step, width)],
+        out_specs=[block(step, 3 * width), block(step, width), block(step, width)],
+        out_shape=[
+            jax.ShapeDtypeStruct((half, 3 * width), F32),
+            jax.ShapeDtypeStruct((half, width), F32),
+            jax.ShapeDtypeStruct((half, width), F32),
+        ],
+        compiler_params=pltpu.CompilerParams(vmem_limit_bytes=40 << 20),
+        name="write_gradients",
+    )(pairs.reshape(members, half, 3 * PAIR), joint, fc)
 
 
 def tri(n):
@@ -1241,9 +1231,12 @@
     tree_rows = members * rows
     low = shard == 0
 
-    vectors = jnp.stack(
-        [ln1_gain, ln1_bias, b_query, b_value, b_out, ln2_gain, ln2_bias, b_proj]
-    ).astype(F32)
+    held = (ln1_gain, ln1_bias, b_query, b_value, b_out, ln2_gain, ln2_bias, b_proj)
+    shape = (len(held), half)
+    line = lax.broadcasted_iota(jnp.int32, shape, 0)
+    vectors = jnp.zeros(shape, F32)
+    for i, value in enumerate(held):
+        vectors = jnp.where(line == i, lax.broadcast_in_dim(value.astype(F32), shape, (1,)), vectors)
     zeros = jnp.zeros_like(vectors)
     half_vectors = jnp.concatenate(
         [jnp.where(low, vectors, zeros), jnp.where(low, zeros, vectors)], axis=1
@@ -1264,7 +1257,6 @@
     )
     query_info = lax.dynamic_slice_in_dim(query_info, me * rows, rows, 0)
 
-    gain_one = vectors[0]
     attended_pair, attended_last, sorted_qkv, exact, level, exact_last, level_last = attention_forward(
         order, mixed, query_last, query_info, key_info
     )
@@ -1285,33 +1277,37 @@
 
     fc_got = swap(fc_give, "shard", 0)
     joint_other = swap(joint_give, "tensor", 1)
+    fed_other = swap(fed_give, "tensor", 1)
     proj_sum = lax.psum(proj_sum, "context")
 
     d_mixed, d_query_last = attention_backward(
         order, sorted_qkv, exact, level, d_pair, mixed, query_last, exact_last, level_last, d_last,
         query_info, key_info,
     )
-    fc_got, joint_other, d_mixed = lax.optimization_barrier((fc_got, joint_other, d_mixed))
+    fc_got, joint_other, fed_other, d_mixed = lax.optimization_barrier(
+        (fc_got, joint_other, fed_other, d_mixed)
+    )
     fc_sum = (fc_keep.astype(F32) + fc_got.astype(F32)).astype(BF16)
     fc_sum = lax.psum(
         fc_sum, "context", axis_index_groups=[list(range(lax.axis_size("context")))[::-1]]
     )
-    output, d_inputs, own_mixer, own_out, sums = finish(
+    output, d_inputs, pairs, joint_all, sums = finish(
         d_mixed,
         d_query_last,
         normed_all,
         weight,
         tokens,
         d_middle,
-        gain_one[None, :],
+        vectors,
         joint_keep,
         joint_other,
         sums,
         residual,
-        fed_give,
+        fed_other,
     )
     proj_sum, fc_sum, sums = lax.optimization_barrier((proj_sum, fc_sum, sums))
-    own_fc, own_proj = fc_sum.astype(F32), proj_sum.T.astype(F32)
+    own_mixer, own_out, own_fc = write_gradients(pairs, joint_all, fc_sum)
+    own_proj = proj_sum.T.astype(F32)
     mine = lax.dynamic_slice_in_dim(sums[:8], shard * half, half, 1)
     own_bias_fc = lax.dynamic_slice_in_dim(sums, 8 + tensor, 1, 0)[0]
     return (

time: 420 us -> 399 us (0.950)
  Pallas kernels: 338 us -> 326 us
  local copies, waits for them, and re-layouts: 45 us -> 33.1 us
    pallas_call x2 -> x3, Pallas kernels: 213 us -> 197 us  [the longest x1 150 us: finish(): pl.pallas_call(finish_kernel, in_specs=[VMEM] * 12, out_specs=[VMEM] * 5,...]
    another operation x9 -> x0, local copies, waits for them, and re-layouts: 5.53 us -> none  [local(): jnp.stack([ln1_gain, ln1_bias, b_query, b_value, b_out, ln2_gain, ln2_bia...]
    pallas_call x1, Pallas kernels: 81.5 us -> 86 us  [feed_forward(): pl.pallas_call(feed_forward_kernel, in_specs=[ANY] + [VMEM] * 4 + [ANY] *...]
    convert_element_type x2 -> x9, other arithmetic: 4.7 us -> 8.54 us  [the longest x8 5.47 us: local(): value.astype(F32)]
    unnamed x71 -> x69, local copies, waits for them, and re-layouts: 33.8 us -> 30.4 us
  transfers between devices with their start and end apart: 6 -> 7, of which waited for: 1 -> 1; matrix products, arithmetic and copies ran while one was open for 1% -> 1% of each run, Pallas kernels for 50% -> 49%
where the time goes in v3:
time: 399 us; the launch traced here: 392 us
  Pallas kernels  326 us (82%)
  local copies, waits for them, and re-layouts  33.1 us (8%)
  between operations  14.5 us (4%)
  other arithmetic  11 us (3%)
  starting transfers between devices  4.84 us (1%)
    pallas_call x1, Pallas kernels, finish(): pl.pallas_call(finish_kernel, in_specs=[VMEM] * 12, out_specs=[VMEM] * 5,...  150 us
    pallas_call x1, Pallas kernels, feed_forward(): pl.pallas_call(feed_forward_kernel, in_specs=[ANY] + [VMEM] * 4 + [ANY] *...  86 us
    pallas_call x1, Pallas kernels, project(): pl.pallas_call(project_kernel, in_specs=[VMEM, ANY, VMEM, ANY], out_specs...  40.7 us
    unnamed x69, local copies, waits for them, and re-layouts  30.4 us
    pallas_call x1, Pallas kernels, attention_backward(): pl.pallas_call(bwd_kernel, in_specs=[pl.BlockSpec(memory_space=pltpu.SMEM...  26.7 us
    pallas_call x1, Pallas kernels, attention_forward(): pl.pallas_call(fwd_kernel, in_specs=[pl.BlockSpec(memory_space=pltpu.SMEM...  16.6 us
  transfers between devices with their start and end apart: 7, of which 1 were waited for; matrix products, arithmetic and copies ran while one was open for 1% of the time, Pallas kernels for 49%

profile of v3, /device:TPU:0, one launch (start us, length us, event | category | flops | bytes accessed | tf_op | source)
XLA Modules:
  0.0 391.6 jit_solution(17918635248639599666)
XLA Ops:
  7.3 0.7 convert_element_type.48
  8.0 0.7 convert_element_type.49
  8.7 0.7 convert_element_type.50
  9.3 0.7 convert_element_type.51
  10.0 0.7 convert_element_type.52
  10.7 0.7 convert_element_type.53
  11.4 0.7 convert_element_type.54
  12.1 0.7 convert_element_type.55
  12.8 0.1 fusion.1
  12.9 1.1 copy-done
  14.0 1.3 copy-done.2
  15.3 2.0 copy-done.3
  17.4 40.7 %project.1 = (bf16[2560,1088]{1,0:T(8,128)(2,1)S(1)}, bf16[2560,512]{1,0:T(8,128)(2,1)S(1)}, bf16[320,128]{1,0:T(8,128)(2,1)S(1)}, f32[8,1088]{1,0:T(8,128)S(1)}...) custom-call(bf16[320,1088]{1,0:T(8,128)(2,1)S(1)} %copy-done, bf16[544,3264]{1,0:T(8,128)(2,1)S(1)} %copy-done.3, ...), custom_call_target="tpu_custom_call" | custom-call | tf_op jit(solution)/shard_map/project/pallas_call | solution.py:244
  58.1 2.6 copy-done.1
  60.7 1.1 copy-done.6
  61.8 0.8 copy-done.10
  62.6 0.6 copy-done.11
  63.2 1.5 copy-done.14
  64.7 0.5 collective-permute-start.1
  65.2 1.5 collective-permute-start
  66.8 0.1 dynamic-slice_bitcast_fusion.1
  66.8 0.1 slice_reduce_fusion.1
  67.0 0.2 select_reduce_fusion.3
  67.2 0.2 select_reduce_fusion.2
  67.4 0.1 dynamic_slice.15
  67.5 0.1 dynamic-slice_bitcast_fusion
  67.7 0.1 copy.48
  67.8 0.1 copy.49
  67.9 0.1 slice_reduce_fusion
  68.1 0.1 select_reduce_fusion.1
  68.2 0.2 convert_reduce_fusion.1
  68.5 0.1 fusion.4
  68.6 0.1 copy.51.qinfo
  68.7 0.1 select_reduce_fusion.order
  68.9 1.7 copy-done.15
  70.6 16.6 %tree_attention_forward.1 = (bf16[2560,128]{1,0:T(8,128)(2,1)S(1)}, bf16[320,128]{1,0:T(8,128)(2,1)S(1)}, bf16[2560,384]{1,0:T(8,128)(2,1)S(1)}, f32[2560,128]{1...) custom-call(s32[20]{0:T(128)S(1)} %select_reduce_fusion.order, ...), custom_call_target="tpu_custom_call" | custom-call | flops 20000000000 | bytes 8000000 | tf_op jit(solution)/shard_map/tree_attention_forward/pallas_call | solution.py:1096
  87.2 0.8 copy-done.9
  88.0 0.6 copy-done.13
  88.7 1.3 copy-done.19
  89.9 1.1 copy-done.21
  91.0 0.6 reshape.125.bias_fc
  91.6 2.2 collective-permute-done.1.proj_other
  93.8 86.0 %feed_forward.1 = (f32[320,1088]{1,0:T(8,128)}, bf16[320,1088]{1,0:T(8,128)(2,1)}, f32[320,1088]{1,0:T(8,128)}, bf16[2560,128]{1,0:T(8,128)(2,1)}, bf16[320,128]...) custom-call(bf16[2560,128]{1,0:T(8,128)(2,1)} %copy-done.9, ...), custom_call_target="tpu_custom_call" | custom-call | tf_op jit(solution)/shard_map/feed_forward/pallas_call | solution.py:590
  179.8 0.7 collective-permute-start.2
  180.5 1.5 collective-permute-start.4
  182.0 0.5 collective-permute-start.3
  182.6 1.7 copy-done.16
  184.3 1.1 copy-done.17
  185.4 0.9 copy-done.18
  186.3 1.7 copy-done.20
  188.0 1.3 copy-done.22
  189.4 26.7 %tree_attention_backward.1 = (bf16[2560,512]{1,0:T(8,128)(2,1)S(1)}, bf16[320,128]{1,0:T(8,128)(2,1)S(1)}) custom-call(s32[20]{0:T(128)S(1)} %select_reduce_fusion.order, bf16[2560,384]{1,0:T(8,128)(2,1)S(1)} %copy-done.20, f32[2560,128]{1,0:T(8,128)S(1)} %get-tuple-element.72.of, f32[2560,128]{1,0:T(8,128)S(1)} %copy-done.22, ...), custom_call_target="tpu_custom_call" | custom-call | flops 49999998976 | bytes 15000000 | tf_op jit(solution)/shard_map/tree_attention_backward/pallas_call | solution.py:1169
  216.1 1.5 copy-done.5
  217.6 0.6 copy-done.12
  218.2 1.3 add_convert_fusion
  219.6 149.5 %finish.1 = (bf16[320,1088]{1,0:T(8,128)(2,1)}, f32[320,1088]{1,0:T(8,128)}, bf16[4352,384]{1,0:T(8,128)(2,1)}, bf16[544,1280]{1,0:T(8,128)(2,1)}, f32[16,1088]{1,0:T(8,128)}) custom-call(bf16[2560,512]{1,0:T(8,128)(2,1)} %copy-done.5, bf16[320,128]{1,0:T(8,128)(2,1)} %copy-done.12, bf16[2560,1088]{1,0:T(8,128)(2,1)} %copy-done.1, ...), custom_call_target="tpu_custom_call" | custom-call | tf_op jit(solution)/shard_map/finish/pallas_call | solution.py:955
  369.2 3.1 convert_bitcast_fusion
  372.3 0.6 dynamic-slice_reduce_fusion
  372.9 1.3 copy-done.7
  374.2 1.3 copy-done.8
  375.5 6.3 %write_gradients.1 = (f32[544,3264]{1,0:T(8,128)}, f32[544,1088]{1,0:T(8,128)}, f32[544,1088]{1,0:T(8,128)}) custom-call(bf16[8,544,384]{2,1,0:T(8,128)(2,1)S(1)} %bitcast.24, bf16[544,1280]{1,0:T(8,128)(2,1)S(1)} %copy-done.7, bf16[544,1088]{1,0:T(8,128)(2,1)S(1)} %copy-done.8), custom_call_target="tpu_custom_call" | custom-call | tf_op jit(solution)/shard_map/write_gradients/pallas_call | solution.py:1007
  381.8 0.7 dynamic-slice_reduce_fusion.1
  382.6 0.9 copy.60
  383.4 1.1 copy.61
  (71 shorter events, 0.7 us)
Async XLA Ops:
  7.2 362.0 %all-reduce.3.cloned.1.call-start = ((), (), s32[]{:S(2)}) async-start(), calls=%async_computation | async-start | bytes 2506752 | tf_op jit(solution)/shard_map/psum | solution.py:1281
  12.9 1.1 copy-start
  14.0 1.3 copy-start.2
  15.3 2.0 copy-start.3
  17.4 47.3 %copy-start.24 = (bf16[1088,544]{0,1:T(8,128)(2,1)S(1)}, bf16[1088,544]{0,1:T(8,128)(2,1)}, u32[]{:S(2)}) copy-start(bf16[1088,544]{0,1:T(8,128)(2,1)} %param.34) | copy-start | bytes 3551236
  17.4 49.4 %copy-start.27 = (s32[5120]{0:T(1024)S(1)}, s32[5120]{0:T(1024)}, u32[]{:S(2)}) copy-start(s32[5120]{0:T(1024)} %param.20) | copy-start | bytes 61444
  17.4 49.6 %copy-start.31 = (s32[52]{0:T(128)S(1)}, s32[52]{0:T(128)}, u32[]{:S(2)}) copy-start(s32[52]{0:T(128)} %param.22) | copy-start | bytes 628
  17.4 50.1 %copy-start.28 = (s32[5120]{0:T(1024)S(1)}, s32[5120]{0:T(1024)}, u32[]{:S(2)}) copy-start(s32[5120]{0:T(1024)} %param.21) | copy-start | bytes 61444
  58.1 2.6 copy-start.1
  60.7 1.1 copy-start.6
  61.8 0.8 copy-start.10
  62.6 0.6 copy-start.11
  63.2 1.5 copy-start.14
  64.7 29.1 %collective-permute-start.1 = (bf16[544,1088]{1,0:T(8,128)(2,1)S(1)}, bf16[544,1088]{1,0:T(8,128)(2,1)}, u32[]{:S(2)}, u32[]{:S(2)}) collective-permute-start(bf16[544,1088]{1,0:T(8,128)(2,1)S(1)} %bitcast.26), channel_id=1, source_target_pairs={{0,16},{16,0},{1,17},{17,1},{2,18},{18,2},{3,19},{19,3},{4,20},{20... | collective-permute-start | bytes 3551240 | tf_op jit(solution)/shard_map/ppermute | solution.py:55
  65.2 26.4 %collective-permute-start = (bf16[320,1088]{1,0:T(8,128)(2,1)}, bf16[320,1088]{1,0:T(8,128)(2,1)}, u32[]{:S(2)}, u32[]{:S(2)}) collective-permute-start(bf16[320,1088]{1,0:T(8,128)(2,1)} %cotangent.1), channel_id=1, source_target_pairs={{0,2},{1,3},{2,0},{3,1},{4,6},{5,7},{6,4},{7,5},{8,10},{9,11},{10,... | collective-permute-start | bytes 2088968 | tf_op jit(solution)/shard_map/ppermute | solution.py:55
  68.9 1.7 copy-start.15
  70.6 20.4 %copy-start.30 = (bf16[1088]{0:T(1024)(128)(2,1)S(1)}, bf16[1088]{0:T(1024)(128)(2,1)}, u32[]{:S(2)}) copy-start(bf16[1088]{0:T(1024)(128)(2,1)} %param.33) | copy-start | bytes 6532
  87.2 0.8 copy-start.9
  88.0 0.6 copy-start.13
  88.7 1.3 copy-start.19
  89.9 1.1 copy-start.21
  179.8 38.4 %collective-permute-start.2 = (bf16[544,1088]{1,0:T(8,128)(2,1)}, bf16[544,1088]{1,0:T(8,128)(2,1)S(1)}, u32[]{:S(2)}, u32[]{:S(2)}) collective-permute-start(bf16[544,1088]{1,0:T(8,128)(2,1)} %get-tuple-element.68), channel_id=1, source_target_pairs={{0,16},{16,0},{1,17},{17,1},{2,18},{18,2},{3,19},{19,3},{4,20},{20... | collective-permute-start | bytes 3551240 | tf_op jit(solution)/shard_map/ppermute | solution.py:55
  180.5 37.8 %collective-permute-start.4 = (bf16[320,1088]{1,0:T(8,128)(2,1)}, bf16[320,1088]{1,0:T(8,128)(2,1)}, u32[]{:S(2)}, u32[]{:S(2)}) collective-permute-start(bf16[320,1088]{1,0:T(8,128)(2,1)} %get-tuple-element.70), channel_id=1, source_target_pairs={{0,2},{1,3},{2,0},{3,1},{4,6},{5,7},{6,4},{7,5},{8,10},{9,11},{10,... | collective-permute-start | bytes 2088968 | tf_op jit(solution)/shard_map/ppermute | solution.py:55
  182.0 36.3 %collective-permute-start.3 = (bf16[544,640]{1,0:T(8,128)(2,1)}, bf16[544,640]{1,0:T(8,128)(2,1)}, u32[]{:S(2)}, u32[]{:S(2)}) collective-permute-start(bf16[544,640]{1,0:T(8,128)(2,1)} %get-tuple-element.69), channel_id=1, source_target_pairs={{0,2},{1,3},{2,0},{3,1},{4,6},{5,7},{6,4},{7,5},{8,10},{9,11},{10,... | collective-permute-start | bytes 2088968 | tf_op jit(solution)/shard_map/ppermute | solution.py:55
  182.5 186.6 %all-reduce.5.cloned.1.call-start = ((), (), s32[]{:S(2)}) async-start(), calls=%async_computation.1 | async-start | bytes 2506752 | tf_op jit(solution)/shard_map/psum | solution.py:1291
  182.6 1.7 copy-start.16
  184.3 1.1 copy-start.17
  185.4 0.9 copy-start.18
  186.3 1.7 copy-start.20
  188.0 1.3 copy-start.22
  189.3 28.9 %copy-start.25 = (bf16[544,1088]{1,0:T(8,128)(2,1)S(1)}, bf16[544,1088]{1,0:T(8,128)(2,1)}, u32[]{:S(2)}) copy-start(bf16[544,1088]{1,0:T(8,128)(2,1)} %get-tuple-element.92) | copy-start | bytes 3551236
  216.1 1.5 copy-start.5
  217.6 0.6 copy-start.12
  369.2 3.1 copy-start.29
  369.2 3.7 copy-start.4
  372.9 1.3 copy-start.7
  374.2 1.3 copy-start.8
  375.5 7.0 %copy-start.26 = (bf16[320,1088]{1,0:T(8,128)(2,1)S(1)}, bf16[320,1088]{1,0:T(8,128)(2,1)}, u32[]{:S(2)}) copy-start(bf16[320,1088]{1,0:T(8,128)(2,1)} %get-tuple-element.147) | copy-start | bytes 2088964
  381.8 1.6 copy-start.23
Sparse Core Ops, SparseCore 0:
  182.6 57.9 all-reduce.2
  243.7 91.7 all-reduce.4
